TPU v7x, 256 devices: a whole 4x4x8 slice. The times are simulated.
256 devices in a mesh: dp: 4 (over z_lo), ctx: 64 (over z_hi, y, x, core).
Axes of the slice: x: 4, y: 4, z: 8 (z_hi: 2, z_lo: 4; z = z_hi * 4 + z_lo), core: 2. Of those that a mesh axis runs over, the one named last changes fastest.
Arguments:
- qkv: bfloat16 [4, 8192, 6144], P('dp', 'ctx'), may hold values from -6 to 6
- short_filter: float32 [7, 768], replicated, may hold values from -2 to 2
- long_filter: float32 [2048, 8192], P('ctx'), may hold values from -1.1 to 1.1
- cotangent: bfloat16 [4, 8192, 2048], P('dp', 'ctx'), may hold values from -6 to 6
Outputs:
- mixer_out: bfloat16 [4, 8192, 2048], P('dp', 'ctx')
- grad_qkv: bfloat16 [4, 8192, 6144], P('dp', 'ctx')
- grad_long: float32 [2048, 8192], P('ctx')
- grad_short: float32 [7, 768], replicated
All inputs are finite; a program needn't handle non-finite values.
Results may differ from a plain program's by a relative error of at most 0.014.
Values may be sent and summed in bfloat16 or wider, within the bound.
No kernel may reach another device: no remote copies, remote signals or barrier semaphores. Data moves between devices by JAX's collectives and lax.ppermute only.
A program may use at most 128 MiB of HBM per device.

v0:
```python
import math

import jax
import jax.numpy as jnp
from jax import lax
from jax.sharding import PartitionSpec as P

precise = lax.Precision.HIGHEST


def from_behind(array, axis, by):
    devices = lax.axis_size(axis)
    pairs = [(i, i + by) for i in range(devices) if 0 <= i + by < devices]
    return lax.ppermute(array, axis, pairs)


def angles(row_count, col_count, period):
    row_iota = lax.broadcasted_iota(jnp.int32, (row_count, col_count), 0)
    col_iota = lax.broadcasted_iota(jnp.int32, (row_count, col_count), 1)
    return (row_iota * col_iota % period).astype(jnp.float32) * (2.0 * math.pi / period)


def matmul(left_side, right_side):
    return jnp.dot(left_side, right_side, precision=precise, preferred_element_type=jnp.float32)


def column_table(col_count, sign_flip):
    angle_cols = angles(col_count, col_count, col_count)
    cos_part = jnp.cos(angle_cols)
    sin_part = sign_flip * jnp.sin(angle_cols)
    upper = jnp.concatenate([cos_part, sin_part], axis=1)
    lower = jnp.concatenate([-sin_part, cos_part], axis=1)
    return jnp.concatenate([upper, lower], axis=0)


def forward_transform(signal):
    half_rows, own_chans, col_count = signal.shape
    row_count = 2 * half_rows
    total_len = row_count * col_count
    angle_rows = angles(row_count, half_rows, row_count)
    row_table = jnp.concatenate([jnp.cos(angle_rows), -jnp.sin(angle_rows)], axis=0)
    rows_out = matmul(
        row_table, signal.reshape(half_rows, own_chans * col_count).astype(jnp.float32)
    )
    rows_out = rows_out.reshape(2, row_count, own_chans, col_count)
    part_real = rows_out[0]
    part_imag = rows_out[1]
    twist = angles(row_count, col_count, total_len)[:, None, :]
    twist_real = jnp.cos(twist)
    twist_imag = -jnp.sin(twist)
    turned = jnp.concatenate(
        [
            part_real * twist_real - part_imag * twist_imag,
            part_real * twist_imag + part_imag * twist_real,
        ],
        axis=2,
    )
    spec = matmul(
        turned.reshape(row_count * own_chans, 2 * col_count), column_table(col_count, -1.0)
    )
    return spec.reshape(row_count, own_chans, 2 * col_count)


def inverse_transform(spec):
    row_count, own_chans, double_cols = spec.shape
    col_count = double_cols // 2
    half_rows = row_count // 2
    total_len = row_count * col_count
    back = matmul(spec.reshape(row_count * own_chans, double_cols), column_table(col_count, 1.0))
    back = back.reshape(row_count, own_chans, double_cols)
    back_real = back[:, :, :col_count]
    back_imag = back[:, :, col_count:]
    twist = angles(row_count, col_count, total_len)[:, None, :]
    twist_real = jnp.cos(twist)
    twist_imag = jnp.sin(twist)
    turned = jnp.concatenate(
        [
            back_real * twist_real - back_imag * twist_imag,
            back_real * twist_imag + back_imag * twist_real,
        ],
        axis=0,
    )
    angle_rows = angles(half_rows, row_count, row_count)
    row_table = jnp.concatenate([jnp.cos(angle_rows), -jnp.sin(angle_rows)], axis=1) * (
        1.0 / total_len
    )
    result = matmul(row_table, turned.reshape(2 * row_count, own_chans * col_count))
    return result.reshape(half_rows, own_chans, col_count)


def spec_times(first_spec, second_spec, conjugate):
    col_count = first_spec.shape[2] // 2
    first_real = first_spec[:, :, :col_count]
    first_imag = first_spec[:, :, col_count:]
    second_real = second_spec[:, :, :col_count]
    second_imag = conjugate * second_spec[:, :, col_count:]
    return jnp.concatenate(
        [
            first_real * second_real - first_imag * second_imag,
            first_real * second_imag + first_imag * second_real,
        ],
        axis=2,
    )


def shards(qkv, short_filter, long_filter, cotangent):
    seq_rows = qkv[0]
    row_count, width_all = seq_rows.shape
    width = width_all // 3
    tap_count = short_filter.shape[0]
    group_size = width_all // short_filter.shape[1]
    ctx_count = lax.axis_size("ctx")
    own_chans = width // ctx_count
    grad_scale = 1.0 / math.sqrt(lax.axis_size("dp") * ctx_count * row_count)
    tap_weights = jnp.repeat(short_filter, group_size, axis=1)
    left_rim = from_behind(seq_rows[row_count - tap_count + 1 :], "ctx", 1)
    padded = jnp.concatenate([left_rim, seq_rows], axis=0).astype(jnp.float32)
    short_out = jnp.zeros((row_count, width_all), jnp.float32)
    for lag_index in range(tap_count):
        start = tap_count - 1 - lag_index
        short_out = short_out + tap_weights[lag_index] * padded[start : start + row_count]
    query_rows = short_out[:, :width]
    key_rows = short_out[:, width : 2 * width]
    value_rows = short_out[:, 2 * width :]
    cot_rows = cotangent[0].astype(jnp.float32)
    product = (key_rows * value_rows).T.astype(jnp.bfloat16)[None]
    grad_out = (cot_rows * query_rows).T.astype(jnp.bfloat16)[None]
    filter_taps = long_filter.reshape(own_chans, ctx_count, row_count).transpose(1, 0, 2)
    filter_spec = forward_transform(filter_taps)
    own_prod = lax.all_to_all(product, "ctx", split_axis=1, concat_axis=0, tiled=True)
    prod_spec = forward_transform(own_prod)
    y_own = inverse_transform(spec_times(prod_spec, filter_spec, 1.0))
    y_own, prod_spec = (y_own.astype(jnp.bfloat16), prod_spec)
    long_back = lax.all_to_all(y_own, "ctx", split_axis=0, concat_axis=1, tiled=True)
    own_grad = lax.all_to_all(grad_out, "ctx", split_axis=1, concat_axis=0, tiled=True)
    grad_spec = forward_transform(own_grad)
    du_own = inverse_transform(spec_times(grad_spec, filter_spec, -1.0))
    dh_own = inverse_transform(spec_times(grad_spec, prod_spec, -1.0))
    du_own, dh_own = (du_own.astype(jnp.bfloat16), dh_own)
    du_back = lax.all_to_all(du_own, "ctx", split_axis=0, concat_axis=1, tiled=True)
    long_rows = long_back[0].T.astype(jnp.float32)
    mixer_out = (query_rows * long_rows).astype(jnp.bfloat16)[None]
    grad_prod = du_back[0].T.astype(jnp.float32)
    grad_short_out = jnp.concatenate(
        [cot_rows * long_rows, grad_prod * value_rows, grad_prod * key_rows], axis=1
    )
    right_rim = from_behind(grad_short_out[: tap_count - 1].astype(jnp.bfloat16), "ctx", -1).astype(
        jnp.float32
    )
    grad_padded = jnp.concatenate([grad_short_out, right_rim], axis=0)
    grad_rows = jnp.zeros((row_count, width_all), jnp.float32)
    for lag_index in range(tap_count):
        grad_rows = (
            grad_rows + tap_weights[lag_index] * grad_padded[lag_index : lag_index + row_count]
        )
    grad_qkv = grad_rows.astype(jnp.bfloat16)[None]
    lag_terms = []
    for lag_index in range(tap_count):
        start = tap_count - 1 - lag_index
        lag_terms.append(jnp.sum(grad_short_out * padded[start : start + row_count], axis=0))
    short_terms = jnp.stack(lag_terms).reshape(tap_count, -1, group_size).sum(axis=2) * grad_scale
    long_terms = dh_own.transpose(1, 0, 2).reshape(own_chans, ctx_count * row_count) * grad_scale
    grad_short = lax.psum(short_terms, ("dp", "ctx"))
    grad_long = lax.psum(long_terms.astype(jnp.bfloat16), "dp").astype(jnp.float32)
    return (mixer_out, grad_qkv, grad_long, grad_short)


def solution(mesh):
    return jax.shard_map(
        shards,
        mesh=mesh,
        in_specs=(P("dp", "ctx", None), P(), P("ctx", None), P("dp", "ctx", None)),
        out_specs=(P("dp", "ctx", None), P("dp", "ctx", None), P("ctx", None), P()),
        check_vma=False,
    )
```

profile of v0, /device:TPU:1, one launch (start us, length us, event | category | flops | bytes accessed | tf_op | source)
XLA Modules:
  0.0 534.2 jit_solution(974061488572454364)
XLA Ops:
  8.2 4.5 collective-permute-start
  15.1 5.7 %fusion.53 = f32[256,4096]{1,0:T(8,128)} fusion(f32[8,8,32,128]{3,2,1,0:T(8,128)S(1)} %bitcast.145, f32[128,64]{1,0:T(8,128)S(1)} %get-tuple-element.64, f32[128,64]{1,0:T(8,128)S(1)} %get-tuple-element.65), kind=kOutput, calls=%fused_computation.90 | convolution fusion | flops 805322752 | bytes 5308416 | tf_op jit(solution)/shard_map/dot_general | solution.py:24
  28.0 11.8 %multiply_add_fusion = f32[128,6144]{0,1:T(8,128)S(1)} fusion(f32[134,6144]{0,1:T(8,128)S(1)} %maximum_convert_fusion, f32[6144]{0:T(1024)S(1)} %broadcast_in_dim.60, f32[6144]{0:T(1024)S(1)} %broadcast_in_dim.58, f32[6144]{0:T(1024)S(1)} %broadcast_in_dim.56, f32[6144]{0:T(1024)S(1)} %broadcast_in_dim.54, f32[6144]{0:T(1024)S(1)} %broadcast_in_dim.52, ...), kind=kLoop, calls=%fused_computation.57 | loop fusion | flops 10223616 | bytes 25337856 | tf_op jit(solution)/shard_map/add | solution.py:121
  41.6 8.1 %copy.95 = bf16[1,2048,128]{2,0,1:T(2,128)(2,1)S(1)} copy(bf16[1,2048,128]{2,1,0:T(8,128)(2,1)S(1)} %fusion.62) | data formatting | bytes 1048576 | tf_op jit(solution)/shard_map/broadcast_in_dim | solution.py:127
  50.2 12.0 %reduce.18 = bf16[2048,128]{1,0:T(8,128)(2,1)S(1)} reduce(bf16[2048,1,128]{2,1,0:T(2,128)(2,1)S(1)} %bitcast.143, bf16[]{:T(256)} %broadcast.244), dimensions={1}, to_apply=%bitcast.134.reduce_sub_computation | reduce | bytes 1048578
  63.1 14.1 %all-to-all-start.2 = ((bf16[64,2,2048]{2,1,0:T(2,128)(2,1)}), bf16[64,2,2048]{2,1,0:T(2,128)(2,1)}, u32[]{:S(2)}, u32[]{:S(2)}) async-start(bf16[64,2,2048]{2,1,0:T(2,128)(2,1)} %reshape.246), calls=%async_computation.2 | async-start | bytes 1048576 | tf_op jit(solution)/shard_map/all_to_all | solution.py:135
  77.3 4.7 fusion.130
  94.4 3.6 reshape.247
  98.1 8.8 %bitcast_reduce_fusion.1 = bf16[2048,128]{1,0:T(8,128)(2,1)S(1)} fusion(bf16[2048,1,128]{2,1,0:T(2,128)(2,1)S(1)} %reshape.247), kind=kLoop, calls=%fused_computation.202 | loop fusion | bytes 1048576 | tf_op jit(solution)/shard_map/all_to_all | solution.py:135
  118.9 4.7 multiply_subtract_fusion.4
  133.0 3.9 fusion.16
  139.9 5.6 %copy.63 = f32[256,32,128]{0,2,1:T(8,128)} copy(f32[256,32,128]{2,0,1:T(8,128)} %pad_maximum_fusion.2) | data formatting | bytes 8388608 | tf_op jit(solution)/shard_map/concatenate | solution.py:76
  145.5 6.4 %fusion.49 = bf16[64,32,128]{2,0,1:T(8,128)(2,1)S(1)} fusion(f32[256,32,128]{0,2,1:T(8,128)} %copy.63, f32[64,128]{1,0:T(8,128)S(1)} %copy-done.20, f32[64,128]{1,0:T(8,128)S(1)} %copy-done.22), kind=kOutput, calls=%fused_computation.88 | convolution fusion | flops 805601280 | bytes 4784128 | tf_op jit(solution)/shard_map/dot_general | solution.py:24
  152.3 29.5 %all_to_all.16 = bf16[64,32,128]{2,1,0:T(8,128)(2,1)S(1)} all-to-all(bf16[64,32,128]{2,1,0:T(8,128)(2,1)S(1)} %copy.64), channel_id=1, replica_groups=mesh['dp'=4,'ctx'=64] {'ctx'}, dimensions={0} | all-to-all | bytes 1048576 | tf_op jit(solution)/shard_map/all_to_all | solution.py:140
  182.0 8.1 %copy.96 = bf16[1,2048,128]{2,0,1:T(2,128)(2,1)S(1)} copy(bf16[1,2048,128]{2,1,0:T(8,128)(2,1)S(1)} %get-tuple-element.57) | data formatting | bytes 1048576 | tf_op jit(solution)/shard_map/broadcast_in_dim | solution.py:126
  190.2 12.3 %reduce.19 = bf16[2048,128]{1,0:T(8,128)(2,1)} reduce(bf16[2048,1,128]{2,1,0:T(2,128)(2,1)S(1)} %bitcast.144, bf16[]{:T(256)} %broadcast.244), dimensions={1}, to_apply=%bitcast.135.reduce_sub_computation | reduce | bytes 1048578
  203.7 21.0 %all_to_all.17 = bf16[64,2,2048]{2,1,0:T(2,128)(2,1)} all-to-all(bf16[64,2,2048]{2,1,0:T(2,128)(2,1)S(1)} %reshape.248), channel_id=1, replica_groups=mesh['dp'=4,'ctx'=64] {'ctx'}, dimensions={0} | all-to-all | bytes 1048576 | tf_op jit(solution)/shard_map/all_to_all | solution.py:130
  228.3 9.6 %bitcast_reduce_fusion = bf16[2048,128]{1,0:T(8,128)(2,1)} fusion(bf16[2048,1,128]{2,1,0:T(2,128)(2,1)S(1)} %reshape.249), kind=kLoop, calls=%fused_computation.201 | loop fusion | bytes 1048576 | tf_op jit(solution)/shard_map/all_to_all | solution.py:130
  242.6 5.0 fusion
  247.7 6.2 %multiply_subtract_fusion.1 = (f32[128,32,128]{2,0,1:T(8,128)}, f32[128,32,128]{2,0,1:T(8,128)}, f32[128,32,128]{2,0,1:T(8,128)S(1)}, f32[128,32,128]{2,0,1:T(8,128)}) fusion(f32[128,32,256]{2,0,1:T(8,128)S(1)} %copy-done.4, f32[128,32,256]{2,0,1:T(8,128)} %fusion, f32[128,32,256]{2,0,1:T(8,128)S(1)} %copy-done.6), kind=kLoop, calls=%fused_computation.69 | loop fusion | flops 6815744 | bytes 20971520 | tf_op jit(solution)/shard_map/sub | solution.py:99
  253.9 5.7 %fusion.20 = f32[128,32,256]{2,0,1:T(8,128)S(1)} fusion(f32[128,32,128]{2,0,1:T(8,128)} %get-tuple-element.30, f32[128,32,128]{2,0,1:T(8,128)} %get-tuple-element.29, f32[128,128]{1,0:T(8,128)S(1)} %get-tuple-element.69, f32[128,128]{1,0:T(8,128)S(1)} %get-tuple-element.71, f32[128,128]{1,0:T(8,128)S(1)} %get-tuple-element.70), kind=kOutput, calls=%fused_computation.23 | convolution fusion | flops 3222470656 | bytes 8585216 | tf_op jit(solution)/shard_map/dot_general | solution.py:24
  268.5 5.6 %copy.53 = f32[256,32,128]{0,2,1:T(8,128)} copy(f32[256,32,128]{2,0,1:T(8,128)} %pad_maximum_fusion.1) | data formatting | bytes 8388608 | tf_op jit(solution)/shard_map/concatenate | solution.py:76
  274.1 6.2 %fusion.46 = bf16[64,32,128]{2,0,1:T(8,128)(2,1)S(1)} fusion(f32[256,32,128]{0,2,1:T(8,128)} %copy.53, f32[64,128]{1,0:T(8,128)S(1)} %copy-done.21, f32[64,128]{1,0:T(8,128)S(1)} %copy-done.23), kind=kOutput, calls=%fused_computation.87 | convolution fusion | flops 805601280 | bytes 4784128 | tf_op jit(solution)/shard_map/dot_general | solution.py:24
  281.4 9.5 %all-to-all-start.1 = ((bf16[64,32,128]{2,1,0:T(8,128)(2,1)}), bf16[64,32,128]{2,1,0:T(8,128)(2,1)}, u32[]{:S(2)}, u32[]{:S(2)}) async-start(bf16[64,32,128]{2,1,0:T(8,128)(2,1)} %copy.54), calls=%async_computation.1 | async-start | bytes 1048576 | tf_op jit(solution)/shard_map/all_to_all | solution.py:134
  291.0 4.7 pad_maximum_fusion.3
  295.7 6.0 %copy.67 = f32[256,32,128]{0,2,1:T(8,128)} copy(f32[256,32,128]{2,0,1:T(8,128)} %pad_maximum_fusion.3) | data formatting | bytes 8388608 | tf_op jit(solution)/shard_map/concatenate | solution.py:76
  301.7 6.2 %fusion.43 = bf16[64,32,128]{2,0,1:T(8,128)(2,1)S(1)} fusion(f32[256,32,128]{0,2,1:T(8,128)} %copy.67, f32[64,128]{1,0:T(8,128)S(1)} %copy-done.21, f32[64,128]{1,0:T(8,128)S(1)} %copy-done.23), kind=kOutput, calls=%fused_computation.86 | convolution fusion | flops 805863424 | bytes 4784128 | tf_op jit(solution)/shard_map/dot_general | solution.py:24
  309.0 55.1 %all-reduce.2.cloned.1.call-done = bf16[32,8192]{1,0:T(8,128)(2,1)} async-done(((bf16[32,8192]{1,0:T(8,128)(2,1)}), bf16[32,8192]{1,0:T(8,128)(2,1)}) %all-reduce.2.cloned.1.call-update) | async-done | bytes 524304 | tf_op jit(solution)/shard_map/psum | solution.py:164
  368.7 27.9 %multiply_reduce_fusion = (f32[6144]{0:T(1024)}, f32[6144]{0:T(1024)}, f32[6144]{0:T(1024)}, f32[6144]{0:T(1024)}, f32[6144]{0:T(1024)}, /*index=5*/f32[6144]{0:T(1024)}, f32[6144]{0:T(1024)}) fusion(f32[134,6144]{0,1:T(8,128)} %copy-done.2, f32[128,2048]{0,1:T(8,128)S(1)} %get-tuple-element.56, f32[128,2048]{0,1:T(8,128)S(1)} %get-tuple-element.55, ...), kind=kLoop, calls=%fused_computation.50 | loop fusion | flops 12539904 | bytes 25337856 | tf_op jit(solution)/shard_map/reduce_sum | solution.py:160
  413.0 4.6 collective-permute-start.1
  428.7 77.5 %psum.15 = f32[7,768]{1,0:T(8,128)} all-reduce(f32[7,768]{1,0:T(8,128)S(1)} %broadcast_multiply_fusion.1), channel_id=1, replica_groups=mesh['dp'=4,'ctx'=64] {'dp','ctx'}, use_global_device_ids=true, to_apply=%region_9.10 | all-reduce | flops 5376 | bytes 43008 | tf_op jit(solution)/shard_map/psum | solution.py:163
  510.8 13.7 %fusion.39 = bf16[1,128,6144]{1,2,0:T(8,128)(2,1)} fusion(f32[134,6144]{0,1:T(8,128)S(1)} %pad_maximum_fusion, f32[6144]{0:T(1024)S(1)} %copy-done.36, f32[6144]{0:T(1024)S(1)} %copy-done.38, f32[6144]{0:T(1024)S(1)} %copy-done.28, f32[6144]{0:T(1024)S(1)} %copy-done.30, f32[6144]{0:T(1024)S(1)} %copy-done.32, f32[6144]{0:T(1024)S(1)} %copy-done.34, ...), kind=kLoop, calls=%fused_computation.82 | loop fusion | flops 12582912 | bytes 23764992 | tf_op jit(solution)/shard_map/broadcast_in_dim | solution.py:156
  (177 shorter events, 110.7 us)
Async XLA Ops:
  7.2 7.7 %copy-start = (f32[32,8192]{1,0:T(8,128)S(1)}, f32[32,8192]{1,0:T(8,128)}, u32[]{:S(2)}) copy-start(f32[32,8192]{1,0:T(8,128)} %param.6) | copy-start | bytes 3145732
  8.2 15.6 %collective-permute-start = (bf16[6,6144]{1,0:T(8,128)(2,1)S(1)}, bf16[6,6144]{1,0:T(8,128)(2,1)S(1)}, u32[]{:S(2)}, u32[]{:S(2)}) collective-permute-start(bf16[6,6144]{1,0:T(8,128)(2,1)S(1)} %slice_bitcast_fusion.2), channel_id=1, source_target_pairs={{0,1},{1,2},{2,3},{3,4},{4,5},{5,6},{6,7},{7,8},{8,9},{9,10},{10,1... | collective-permute-start | bytes 221192 | tf_op jit(solution)/shard_map/ppermute | solution.py:14
  15.1 5.7 %copy-start.39 = (f32[7,768]{1,0:T(8,128)S(1)}, f32[7,768]{1,0:T(8,128)}, u32[]{:S(2)}) copy-start(f32[7,768]{1,0:T(8,128)} %param.5) | copy-start | bytes 64516
  20.8 2.7 copy-start.24
  21.2 6.8 %copy-start.25 = (f32[6144]{0:T(1024)}, f32[6144]{0:T(1024)S(1)}, u32[]{:S(2)}) copy-start(f32[6144]{0:T(1024)S(1)} %broadcast_in_dim.48) | copy-start | bytes 73732
  21.6 6.4 %copy-start.27 = (f32[6144]{0:T(1024)}, f32[6144]{0:T(1024)S(1)}, u32[]{:S(2)}) copy-start(f32[6144]{0:T(1024)S(1)} %broadcast_in_dim.56) | copy-start | bytes 73732
  22.0 6.0 %copy-start.29 = (f32[6144]{0:T(1024)}, f32[6144]{0:T(1024)S(1)}, u32[]{:S(2)}) copy-start(f32[6144]{0:T(1024)S(1)} %broadcast_in_dim.54) | copy-start | bytes 73732
  22.4 5.6 %copy-start.31 = (f32[6144]{0:T(1024)}, f32[6144]{0:T(1024)S(1)}, u32[]{:S(2)}) copy-start(f32[6144]{0:T(1024)S(1)} %broadcast_in_dim.52) | copy-start | bytes 73732
  22.7 5.3 copy-start.33
  23.1 4.9 copy-start.35
  23.5 4.5 copy-start.37
  23.8 16.1 %copy-start.11 = (bf16[1,128,2048]{1,2,0:T(8,128)(2,1)}, bf16[1,128,2048]{1,2,0:T(8,128)(2,1)S(1)}, u32[]{:S(2)}) copy-start(bf16[1,128,2048]{1,2,0:T(8,128)(2,1)S(1)} %copy.55) | copy-start | bytes 1572868
  28.0 11.9 %copy-start.2 = (f32[134,6144]{0,1:T(8,128)}, f32[134,6144]{0,1:T(8,128)S(1)}, u32[]{:S(2)}) copy-start(f32[134,6144]{0,1:T(8,128)S(1)} %maximum_convert_fusion) | copy-start | bytes 9879556
  63.1 31.3 %all-to-all-start.2 = ((bf16[64,2,2048]{2,1,0:T(2,128)(2,1)}), bf16[64,2,2048]{2,1,0:T(2,128)(2,1)}, u32[]{:S(2)}, u32[]{:S(2)}) async-start(bf16[64,2,2048]{2,1,0:T(2,128)(2,1)} %reshape.246), calls=%async_computation.2 | async-start | bytes 1048576 | tf_op jit(solution)/shard_map/all_to_all | solution.py:135
  118.9 4.7 copy-start.12
  118.9 4.7 copy-start.14
  127.3 3.6 copy-start.3
  133.0 3.9 copy-start.16
  139.9 5.6 %copy-start.20 = (f32[64,128]{1,0:T(8,128)S(1)}, f32[64,128]{1,0:T(8,128)}, u32[]{:S(2)}) copy-start(f32[64,128]{1,0:T(8,128)} %get-tuple-element.72) | copy-start | bytes 98308
  139.9 5.6 %copy-start.22 = (f32[64,128]{1,0:T(8,128)S(1)}, f32[64,128]{1,0:T(8,128)}, u32[]{:S(2)}) copy-start(f32[64,128]{1,0:T(8,128)} %get-tuple-element.73) | copy-start | bytes 98308
  145.5 36.3 %copy-start.9 = (f32[128,6144]{0,1:T(8,128)S(1)}, f32[128,6144]{0,1:T(8,128)}, u32[]{:S(2)}) copy-start(f32[128,6144]{0,1:T(8,128)} %copy-done.8) | copy-start | bytes 9437188
  242.6 5.0 copy-start.4
  242.6 5.0 copy-start.6
  253.9 5.7 %copy-start.10 = (f32[128,32,128]{2,0,1:T(8,128)S(1)}, f32[128,32,128]{2,0,1:T(8,128)}, u32[]{:S(2)}) copy-start(f32[128,32,128]{2,0,1:T(8,128)} %get-tuple-element.48) | copy-start | bytes 6291460
  259.6 3.6 copy-start.17
  268.5 5.6 %copy-start.21 = (f32[64,128]{1,0:T(8,128)S(1)}, f32[64,128]{1,0:T(8,128)}, u32[]{:S(2)}) copy-start(f32[64,128]{1,0:T(8,128)} %get-tuple-element.72) | copy-start | bytes 98308
  268.5 5.6 %copy-start.23 = (f32[64,128]{1,0:T(8,128)S(1)}, f32[64,128]{1,0:T(8,128)}, u32[]{:S(2)}) copy-start(f32[64,128]{1,0:T(8,128)} %get-tuple-element.73) | copy-start | bytes 98308
  281.4 84.8 %all-to-all-start.1 = ((bf16[64,32,128]{2,1,0:T(8,128)(2,1)}), bf16[64,32,128]{2,1,0:T(8,128)(2,1)}, u32[]{:S(2)}, u32[]{:S(2)}) async-start(bf16[64,32,128]{2,1,0:T(8,128)(2,1)} %copy.54), calls=%async_computation.1 | async-start | bytes 1048576 | tf_op jit(solution)/shard_map/all_to_all | solution.py:134
  290.9 73.2 %all-reduce.2.cloned.1.call-start = ((), (), s32[]{:S(2)}) async-start(), calls=%async_computation.4 | async-start | bytes 1048576 | tf_op jit(solution)/shard_map/psum | solution.py:164
  368.7 139.6 %copy-start.7 = (f32[128,2048]{0,1:T(8,128)}, f32[128,2048]{0,1:T(8,128)S(1)}, u32[]{:S(2)}) copy-start(f32[128,2048]{0,1:T(8,128)S(1)} %get-tuple-element.58) | copy-start | bytes 3145732
  413.0 93.2 %collective-permute-start.1 = (bf16[6,6144]{1,0:T(8,128)(2,1)S(1)}, bf16[6,6144]{1,0:T(8,128)(2,1)S(1)}, u32[]{:S(2)}, u32[]{:S(2)}) collective-permute-start(bf16[6,6144]{1,0:T(8,128)(2,1)S(1)} %copy.65), channel_id=1, source_target_pairs={{1,0},{2,1},{3,2},{4,3},{5,4},{6,5},{7,6},{8,7},{9,8},{10,9},{11,1... | collective-permute-start | bytes 221192 | tf_op jit(solution)/shard_map/ppermute | solution.py:14
  510.8 16.3 %copy-start.1 = (f32[32,8192]{1,0:T(8,128)S(1)}, f32[32,8192]{1,0:T(8,128)}, u32[]{:S(2)}) copy-start(f32[32,8192]{1,0:T(8,128)} %param.6) | copy-start | bytes 3145732
  (13 other events, 25.7 us)
Sparse Core Ops, SparseCore 0:
  309.2 54.9 all-reduce.1
where the time goes:
time: 545 us; the launch traced here: 534 us
  local copies, waits for them, and re-layouts  129 us (24%)
  blocking collectives  128 us (23%)
  other arithmetic  120 us (22%)
  waiting for transfers between devices  55.4 us (10%)
  matrix products  53.4 us (10%)
  starting transfers between devices  32.8 us (6%)
  between operations  15.1 us (3%)
    psum x1, blocking collectives, shards(): grad_short = lax.psum(short_terms, ('dp', 'ctx'))  77.5 us
    psum x1, waiting for transfers between devices, shards(): lax.psum(long_terms.astype(jnp.bfloat16), 'dp').astype(jnp.float32)  55.1 us
    dot_general x12, matrix products, matmul(): jnp.dot(left_side, right_side, precision=precise, preferred_element_type=...  53.4 us
    unnamed x97, local copies, waits for them, and re-layouts  30 us
    all_to_all x1, blocking collectives, shards(): lax.all_to_all(du_own, 'ctx', split_axis=0, concat_axis=1, tiled=True)  29.5 us
    reduce_sum x1, other arithmetic, shards(): jnp.sum(grad_short_out * padded[start:start + row_count], axis=0)  27.9 us
    unnamed x2, other arithmetic  24.3 us
    all_to_all x1, blocking collectives, shards(): lax.all_to_all(product, 'ctx', split_axis=1, concat_axis=0, tiled=True)  21 us
  transfers between devices with their start and end apart: 5, of which 2 were waited for; matrix products, arithmetic and copies ran while one was open for 11% of the time, Pallas kernels for 0%

commit v1 on v0

v1 whole, which is shorter than its diff:
```python
import functools
import math

import jax
import jax.numpy as jnp
import numpy as np
from jax import lax
from jax.experimental import pallas as pl
from jax.experimental.pallas import tpu as pltpu
from jax.sharding import PartitionSpec as P

F32 = jnp.float32
BF16 = jnp.bfloat16
LANES = 128
OWN = 8
HALO = 8
ROT = -0.25
VMEM_LIMIT = 56 * 1024 * 1024


def two_parts(table):
    high = jnp.asarray(table, F32).astype(BF16)
    low = (jnp.asarray(table, F32) - high.astype(F32)).astype(BF16)
    return high, low


def make_tables(rows, cols):
    total = rows * cols
    k1 = np.arange(rows, dtype=np.float64)[:, None] + ROT
    n1 = np.arange(rows, dtype=np.float64)[None, :]
    turn = 2.0 * np.pi * k1 * n1 / rows
    first = np.concatenate([np.cos(turn), -np.sin(turn)], axis=0)
    last = np.concatenate([np.cos(turn.T), -np.sin(turn.T)], axis=1) / total
    n2 = np.arange(cols, dtype=np.float64)
    twist = 2.0 * np.pi * k1 * n2[None, :] / total
    twist = np.concatenate([np.cos(twist), -np.sin(twist)], axis=1)
    inner = 2.0 * np.pi * ((n2[:, None] * n2[None, :]) % cols) / cols
    real, imag = np.cos(inner), -np.sin(inner)
    ahead = np.block([[real, imag], [-imag, real]])
    back = np.block([[real, -imag], [imag, real]])
    first = jnp.concatenate(two_parts(first), axis=1)
    last = jnp.concatenate(two_parts(last), axis=1)
    ahead = jnp.concatenate(two_parts(ahead), axis=0)
    back = jnp.concatenate(two_parts(back), axis=0)
    return first, last, jnp.asarray(twist, F32), ahead, back


def mxu(left, right):
    return jnp.dot(left, right, preferred_element_type=F32)


def twice(array, axis):
    return jnp.concatenate([array, array], axis=axis)


def to_spectra(signals, first, twist, ahead):
    rows, cols = signals[0].shape
    wide = jnp.concatenate(signals, axis=1).astype(BF16)
    mixed = mxu(first, twice(wide, 0))
    twist_real, twist_imag = twist[:, :cols], twist[:, cols:]
    turned = []
    for at in range(len(signals)):
        real = mixed[:rows, at * cols : (at + 1) * cols]
        imag = mixed[rows:, at * cols : (at + 1) * cols]
        turned.append(
            jnp.concatenate(
                [real * twist_real - imag * twist_imag, real * twist_imag + imag * twist_real], axis=1
            )
        )
    turned = jnp.concatenate(turned, axis=0).astype(BF16)
    return mxu(twice(turned, 1), ahead)


def from_spectra(spectra, last, twist, back):
    rows, cols = spectra[0].shape[0], spectra[0].shape[1] // 2
    tall = jnp.concatenate(spectra, axis=0).astype(BF16)
    mixed = mxu(twice(tall, 1), back)
    twist_real, twist_imag = twist[:, :cols], twist[:, cols:]
    turned = []
    for at in range(len(spectra)):
        real = mixed[at * rows : (at + 1) * rows, :cols]
        imag = mixed[at * rows : (at + 1) * rows, cols:]
        turned.append(
            jnp.concatenate(
                [real * twist_real + imag * twist_imag, imag * twist_real - real * twist_imag], axis=0
            )
        )
    turned = jnp.concatenate(turned, axis=1).astype(BF16)
    return mxu(last, twice(turned, 0))


def times(left, right, flip):
    cols = left.shape[1] // 2
    left_real, left_imag = left[:, :cols], left[:, cols:]
    right_real, right_imag = right[:, :cols], right[:, cols:]
    if flip:
        real = left_real * right_real + left_imag * right_imag
        imag = left_imag * right_real - left_real * right_imag
    else:
        real = left_real * right_real - left_imag * right_imag
        imag = left_real * right_imag + left_imag * right_real
    return jnp.concatenate([real, imag], axis=1)


def filter_kernel(rows, place_ref, taps_ref, first_ref, twist_ref, ahead_ref, out_ref, spread):
    base = pl.multiple_of(place_ref[0] * OWN, OWN)
    for row in range(rows):
        spread[row * OWN : (row + 1) * OWN, :] = taps_ref[
            pl.ds(base, OWN), row * LANES : (row + 1) * LANES
        ]
    first, twist, ahead = first_ref[...], twist_ref[...], ahead_ref[...]
    twist_real, twist_imag = twist[:, :LANES], twist[:, LANES:]
    for half in range(2):
        wide = jnp.concatenate(
            [spread[pl.ds(half * 4 + at, rows, stride=OWN), :] for at in range(4)], axis=1
        )
        high = wide.astype(BF16)
        low = (wide - high.astype(F32)).astype(BF16)
        mixed = mxu(first, twice(high, 0)) + mxu(first[:, :rows], low)
        turned = []
        for at in range(4):
            real = mixed[:rows, at * LANES : (at + 1) * LANES]
            imag = mixed[rows:, at * LANES : (at + 1) * LANES]
            turned.append(
                jnp.concatenate(
                    [real * twist_real - imag * twist_imag, real * twist_imag + imag * twist_real],
                    axis=1,
                )
            )
        turned = jnp.concatenate(turned, axis=0)
        high = turned.astype(BF16)
        low = (turned - high.astype(F32)).astype(BF16)
        spectra = mxu(twice(high, 1), ahead) + mxu(low, ahead[: 2 * LANES])
        for at in range(4):
            out_ref[half * 4 + at] = spectra[at * rows : (at + 1) * rows]


def mix_kernel(
    seqs,
    rows,
    got_ref,
    filt_ref,
    first_ref,
    last_ref,
    twist_ref,
    ahead_ref,
    back_ref,
    out_ref,
    corr_ref,
    spread,
    gather,
):
    pair = 2 * OWN
    for seq in range(seqs):
        spread[seq * rows * pair : (seq + 1) * rows * pair, :] = (
            got_ref[seq].astype(F32).reshape(rows * pair, LANES)
        )
    first, last, twist = first_ref[...], last_ref[...], twist_ref[...]
    for chan in range(OWN):
        signals = [
            spread[pl.ds(seq * rows * pair + part * OWN + chan, rows, stride=pair), :]
            for part in range(2)
            for seq in range(seqs)
        ]
        spectra = to_spectra(signals, first, twist, ahead_ref[...])
        filt = filt_ref[chan]
        ahead_specs, back_specs, total = [], [], None
        for seq in range(seqs):
            prod = spectra[seq * rows : (seq + 1) * rows]
            grad = spectra[(seqs + seq) * rows : (seqs + seq + 1) * rows]
            ahead_specs.append(times(prod, filt, False))
            back_specs.append(times(grad, filt, True))
            term = times(grad, prod, True)
            total = term if total is None else total + term
        corr_ref[chan] = total
        result = from_spectra(ahead_specs + back_specs, last, twist, back_ref[...])
        at = 0
        for part in range(2):
            for seq in range(seqs):
                gather[pl.ds(seq * rows * pair + part * OWN + chan, rows, stride=pair), :] = result[
                    :, at * LANES : (at + 1) * LANES
                ]
                at += 1
    for seq in range(seqs):
        out_ref[seq] = (
            gather[seq * rows * pair : (seq + 1) * rows * pair, :]
            .reshape(rows, pair, LANES)
            .astype(BF16)
        )


def taps_kernel(rows, scale, corr_ref, last_ref, twist_ref, back_ref, out_ref, gather):
    last, twist, back = last_ref[...], twist_ref[...], back_ref[...]
    for half in range(2):
        result = from_spectra([corr_ref[half * 4 + at] for at in range(4)], last, twist, back)
        for at in range(4):
            gather[pl.ds(half * 4 + at, rows, stride=OWN), :] = (
                result[:, at * LANES : (at + 1) * LANES] * scale
            )
    for row in range(rows):
        out_ref[:, row * LANES : (row + 1) * LANES] = gather[row * OWN : (row + 1) * OWN, :].astype(BF16)


def join_kernel(place_ref, own_ref, one_ref, two_ref, three_ref, out_ref):
    place = place_ref[0]
    for step, ref in enumerate((own_ref, one_ref, two_ref, three_ref)):
        row = pl.multiple_of((place ^ step) * OWN, OWN)
        out_ref[pl.ds(row, OWN), :] = ref[...].astype(F32)


def group_table(groups, group_size):
    rows = lax.broadcasted_iota(jnp.int32, (groups, groups * group_size), 0)
    cols = lax.broadcasted_iota(jnp.int32, (groups, groups * group_size), 1)
    return jnp.where(cols // group_size == rows, 1.0, 0.0).astype(F32)


def spread_taps(taps_ref, group_size, wide):
    groups = taps_ref.shape[1]
    table = group_table(LANES, group_size)
    for at in range(groups // LANES):
        wide[:, at * LANES * group_size : (at + 1) * LANES * group_size] = jnp.dot(
            taps_ref[:, at * LANES : (at + 1) * LANES],
            table,
            precision=lax.Precision.HIGHEST,
            preferred_element_type=F32,
        )


def short_kernel(
    tap_count, group_size, qkv_ref, rim_ref, taps_ref, cot_ref, feats_ref, out_ref, padded, wide
):
    rows, width_all = qkv_ref.shape
    width = width_all // 3
    spread_taps(taps_ref, group_size, wide)
    padded[0:HALO, :] = rim_ref[...].astype(F32)
    padded[HALO : HALO + rows, :] = qkv_ref[...].astype(F32)
    per_chunk = LANES // OWN // 4

    def chunk(at, _):
        parts = []
        for part in range(3):
            cols = pl.ds(pl.multiple_of(part * width + at * LANES, LANES), LANES)
            total = wide[0:1, cols] * padded[HALO : HALO + rows, cols]
            for lag in range(1, tap_count):
                total = total + wide[lag : lag + 1, cols] * padded[HALO - lag : HALO - lag + rows, cols]
            feats_ref[:, cols] = total
            parts.append(total)
        cols = pl.ds(pl.multiple_of(at * LANES, LANES), LANES)
        product = (parts[1] * parts[2]).T.reshape(LANES // OWN, OWN, LANES)
        grad_in = (cot_ref[:, cols].astype(F32) * parts[0]).T.reshape(LANES // OWN, OWN, LANES)
        both = jnp.concatenate([product, grad_in], axis=1).astype(BF16)
        both = both.reshape(per_chunk, 4, 2 * OWN, LANES)
        for seq in range(4):
            out_ref[seq, pl.ds(at * per_chunk, per_chunk)] = both[:, seq]
        return 0

    lax.fori_loop(0, width // LANES, chunk, 0)


def gate_kernel(
    tap_count,
    group_size,
    scale,
    got_ref,
    feats_ref,
    cot_ref,
    qkv_ref,
    rim_ref,
    mixer_ref,
    gso_ref,
    edge_ref,
    short_ref,
    padded,
    sums,
):
    rows, width_all = qkv_ref.shape
    width = width_all // 3
    padded[0:HALO, :] = rim_ref[...].astype(F32)
    padded[HALO : HALO + rows, :] = qkv_ref[...].astype(F32)
    per_chunk = LANES // OWN // 4

    def chunk(at, _):
        both = jnp.stack(
            [got_ref[seq, pl.ds(at * per_chunk, per_chunk)] for seq in range(4)], axis=1
        ).astype(F32)
        both = both.reshape(LANES // OWN, 2 * OWN, LANES)
        long_out = both[:, :OWN].reshape(LANES, LANES).T
        grad_product = both[:, OWN:].reshape(LANES, LANES).T
        cols = [
            pl.ds(pl.multiple_of(part * width + at * LANES, LANES), LANES) for part in range(3)
        ]
        mixer_ref[:, cols[0]] = (feats_ref[:, cols[0]] * long_out).astype(BF16)
        grads = (
            cot_ref[:, cols[0]].astype(F32) * long_out,
            grad_product * feats_ref[:, cols[2]],
            grad_product * feats_ref[:, cols[1]],
        )
        for part in range(3):
            gso_ref[:, cols[part]] = grads[part]
            edge_ref[:, cols[part]] = grads[part][:HALO].astype(BF16)
            for lag in range(tap_count):
                term = grads[part] * padded[HALO - lag : HALO - lag + rows, cols[part]]
                sums[lag * 8 : (lag + 1) * 8, cols[part]] = jnp.sum(
                    term.reshape(rows // 8, 8, LANES), axis=0
                )
        return 0

    lax.fori_loop(0, width // LANES, chunk, 0)
    table = group_table(LANES, group_size)
    block = LANES * group_size
    for at in range(width_all // block):
        lags = [
            jnp.sum(sums[lag * 8 : (lag + 1) * 8, at * block : (at + 1) * block], axis=0, keepdims=True)
            for lag in range(tap_count)
        ]
        lags = jnp.concatenate(lags + [jnp.zeros((8 - tap_count, block), F32)], axis=0)
        short_ref[:, at * LANES : (at + 1) * LANES] = (
            lax.dot_general(
                lags,
                table,
                (((1,), (1,)), ((), ())),
                precision=lax.Precision.HIGHEST,
                preferred_element_type=F32,
            )
            * scale
        )


def back_kernel(tap_count, group_size, gso_ref, rim_ref, taps_ref, out_ref, padded, wide):
    rows, width_all = gso_ref.shape
    spread_taps(taps_ref, group_size, wide)
    padded[rows - HALO : rows, :] = gso_ref[rows - HALO : rows, :]
    padded[rows : rows + HALO, :] = rim_ref[...].astype(F32)
    body = rows - HALO

    def chunk(at, _):
        cols = pl.ds(pl.multiple_of(at * LANES, LANES), LANES)
        total = wide[0:1, cols] * gso_ref[0:body, cols]
        tail = wide[0:1, cols] * padded[body:rows, cols]
        for lag in range(1, tap_count):
            total = total + wide[lag : lag + 1, cols] * gso_ref[lag : lag + body, cols]
            tail = tail + wide[lag : lag + 1, cols] * padded[body + lag : rows + lag, cols]
        out_ref[:, cols] = jnp.concatenate([total, tail], axis=0).astype(BF16)
        return 0

    lax.fori_loop(0, width_all // LANES, chunk, 0)


def call(kernel, outs, scratch, args, cost, scalars=0):
    vmem = pl.BlockSpec(memory_space=pltpu.VMEM)
    smem = pl.BlockSpec(memory_space=pltpu.SMEM)
    flops, moved = (int(value) for value in cost)
    return pl.pallas_call(
        kernel,
        out_shape=outs,
        in_specs=[smem] * scalars + [vmem] * (len(args) - scalars),
        out_specs=jax.tree.map(lambda _: vmem, outs),
        scratch_shapes=scratch,
        compiler_params=pltpu.CompilerParams(vmem_limit_bytes=VMEM_LIMIT),
        cost_estimate=pl.CostEstimate(flops=flops, bytes_accessed=moved, transcendentals=0),
    )(*args)


def shape(dims, kind):
    return jax.ShapeDtypeStruct(dims, kind)


def neighbours(array, by):
    devices = lax.axis_size("ctx")
    pairs = [(i, i + by) for i in range(devices) if 0 <= i + by < devices]
    return lax.ppermute(array, "ctx", pairs)


def partner(array, axis, mask):
    return lax.ppermute(array, axis, [(i, i ^ mask) for i in range(lax.axis_size(axis))])


def shards(qkv, short_filter, long_filter, cotangent):
    feats_in, cot = qkv[0], cotangent[0]
    rows, width_all = feats_in.shape
    width = width_all // 3
    tap_count, groups = short_filter.shape
    group_size = width_all // groups
    seqs, ctx_count = lax.axis_size("dp"), lax.axis_size("ctx")
    length = ctx_count * rows
    scale = 1.0 / math.sqrt(seqs * length)
    first, last, twist, ahead, back = make_tables(ctx_count, rows)
    place = lax.axis_index("dp").astype(jnp.int32).reshape(1)
    taps = jnp.concatenate([short_filter, jnp.zeros((8 - tap_count, groups), F32)], axis=0)
    left_rim = neighbours(feats_in[rows - HALO :], 1)
    pair = (seqs, ctx_count, 2 * OWN, rows)
    wide_pad = pltpu.VMEM((rows + HALO, width_all), F32)
    wide_taps = pltpu.VMEM((8, width_all), F32)
    filt = call(
        functools.partial(filter_kernel, ctx_count),
        shape((OWN, ctx_count, 2 * rows), F32),
        [pltpu.VMEM((length // rows * OWN, rows), F32)],
        (place, long_filter, first, twist, ahead),
        (4e9, 2e6),
        1,
    )
    feats, sent = call(
        functools.partial(short_kernel, tap_count, group_size),
        (shape((rows, width_all), F32), shape(pair, BF16)),
        [wide_pad, wide_taps],
        (feats_in, left_rim, taps, cot),
        (4e9, 6e6),
    )
    got = lax.all_to_all(
        sent.reshape(seqs * ctx_count, 2 * OWN, rows), ("dp", "ctx"), 0, 0, tiled=True
    ).reshape(pair)
    long_rows = pltpu.VMEM((seqs * ctx_count * 2 * OWN, rows), F32)
    mixed, corr = call(
        functools.partial(mix_kernel, seqs, ctx_count),
        (shape(pair, BF16), shape((OWN, ctx_count, 2 * rows), F32)),
        [long_rows, long_rows],
        (got, filt, first, last, twist, ahead, back),
        (8e9, 6e6),
    )
    returned = lax.all_to_all(
        mixed.reshape(seqs * ctx_count, 2 * OWN, rows), ("dp", "ctx"), 0, 0, tiled=True
    ).reshape(pair)
    own_taps = call(
        functools.partial(taps_kernel, ctx_count, scale),
        shape((OWN, length), BF16),
        [pltpu.VMEM((ctx_count * OWN, rows), F32)],
        (corr, last, twist, back),
        (2e9, 1e6),
    )
    others = [partner(own_taps, "dp", mask) for mask in (1, 2, 3)]
    mixer_out, gso, edge, short_part = call(
        functools.partial(gate_kernel, tap_count, group_size, scale),
        (
            shape((rows, width), BF16),
            shape((rows, width_all), F32),
            shape((HALO, width_all), BF16),
            shape((8, groups), F32),
        ),
        [wide_pad, pltpu.VMEM((tap_count * 8, width_all), F32)],
        (returned, feats, cot, feats_in, left_rim),
        (4e9, 9e6),
    )
    right_rim = neighbours(edge, -1)
    grad_rows = call(
        functools.partial(back_kernel, tap_count, group_size),
        shape((rows, width_all), BF16),
        [pltpu.VMEM((rows + HALO, width_all), F32), wide_taps],
        (gso, right_rim, taps),
        (4e9, 6e6),
    )
    for axis in ("ctx", "dp"):
        mask = 1
        while mask < lax.axis_size(axis):
            short_part = short_part + partner(short_part, axis, mask)
            mask *= 2
    grad_long = call(
        join_kernel,
        shape((seqs * OWN, length), F32),
        [],
        (place, own_taps, *others),
        (1e8, 2e6),
        1,
    )
    return mixer_out[None], grad_rows[None], grad_long, short_part[:tap_count]


def solution(mesh):
    return jax.shard_map(
        shards,
        mesh=mesh,
        in_specs=(P("dp", "ctx", None), P(), P("ctx", None), P("dp", "ctx", None)),
        out_specs=(P("dp", "ctx", None), P("dp", "ctx", None), P("ctx", None), P()),
        check_vma=False,
    )
```

time: 545 us -> 176 us (0.32)
  the two profiles are of different devices: /device:TPU:1 before, /device:TPU:8 now
where the time goes in v1:
time: 176 us; the launch traced here: 174 us
  waiting for transfers between devices  51.8 us (29%)
  Pallas kernels  44.5 us (25%)
  blocking collectives  39.5 us (22%)
  starting transfers between devices  30.4 us (17%)
  local copies, waits for them, and re-layouts  5.83 us (3%)
    pallas_call x7, Pallas kernels, call(): pl.pallas_call(kernel, out_shape=outs, in_specs=[smem] * scalars + [vmem]...  44.5 us
    all_to_all x1, blocking collectives, shards(): lax.all_to_all(mixed.reshape(seqs * ctx_count, 2 * OWN, rows), ('dp', 'ct...  39.5 us
    all_to_all x1, waiting for transfers between devices, shards(): lax.all_to_all(sent.reshape(seqs * ctx_count, 2 * OWN, rows), ('dp', 'ctx...  28.9 us
    ppermute x11, waiting for transfers between devices, partner(): lax.ppermute(array, axis, [(i, i ^ mask) for i in range(lax.axis_size(axi...  18.1 us
    all_to_all x1, starting transfers between devices, shards(): lax.all_to_all(sent.reshape(seqs * ctx_count, 2 * OWN, rows), ('dp', 'ctx...  16.1 us
    ppermute x11, starting transfers between devices, partner(): lax.ppermute(array, axis, [(i, i ^ mask) for i in range(lax.axis_size(axi...  10.5 us
    ppermute x2, waiting for transfers between devices, neighbours(): return lax.ppermute(array, 'ctx', pairs)  4.77 us
    ppermute x2, starting transfers between devices, neighbours(): return lax.ppermute(array, 'ctx', pairs)  3.82 us
  transfers between devices with their start and end apart: 14, of which 8 were waited for; matrix products, arithmetic and copies ran while one was open for 1% of the time, Pallas kernels for 9%

profile of v1, /device:TPU:8, one launch (start us, length us, event | category | flops | bytes accessed | tf_op | source)
XLA Modules:
  0.0 174.1 jit_solution(17781418440920999476)
XLA Ops:
  0.6 0.9 slice_bitcast_fusion
  1.5 1.9 %collective-permute-start = (bf16[8,6144]{1,0:T(8,128)(2,1)S(1)}, bf16[8,6144]{1,0:T(8,128)(2,1)S(1)}, u32[]{:S(2)}, u32[]{:S(2)}) collective-permute-start(bf16[8,6144]{1,0:T(8,128)(2,1)S(1)} %slice_bitcast_fusion), channel_id=1, source_target_pairs={{0,1},{1,2},{2,3},{3,4},{4,5},{5,6},{6,7},{7,8},{8,9},{9,10},{10,1... | collective-permute-start | bytes 294920 | tf_op jit(solution)/shard_map/ppermute | solution.py:371
  3.4 1.4 concatenate.15.taps_ref
  4.8 4.8 %collective-permute-done.rim_ref = bf16[8,6144]{1,0:T(8,128)(2,1)S(1)} collective-permute-done((bf16[8,6144]{1,0:T(8,128)(2,1)S(1)}, bf16[8,6144]{1,0:T(8,128)(2,1)S(1)}, u32[]{:S(2)}, u32[]{:S(2)}) %collective-permute-start) | collective-permute-done | bytes 98336 | tf_op jit(solution)/shard_map/ppermute | solution.py:371
  9.6 0.7 copy-done.6
  10.2 9.5 %shard_map.156 = (f32[128,6144]{1,0:T(8,128)}, bf16[4,64,16,128]{3,2,1,0:T(8,128)(2,1)}) custom-call(bf16[128,6144]{1,0:T(8,128)(2,1)} %bitcast.15, bf16[8,6144]{1,0:T(8,128)(2,1)} %copy-done.6, f32[8,768]{1,0:T(8,128)} %concatenate.15.taps_ref, bf16[128,2048]{1,0:T(8,128)(2,1)} %bitcast.17), custom_call_target="tpu_custom_call" | custom-call | flops 4000000000 | bytes 6000000 | tf_op jit(solution)/shard_map/pallas_call | solution.py:353
  19.7 16.1 %all-to-all-start = ((bf16[256,16,128]{2,1,0:T(8,128)(2,1)}), bf16[256,16,128]{2,1,0:T(8,128)(2,1)S(1)}, u32[]{:S(2)}, u32[]{:S(2)}) async-start(bf16[256,16,128]{2,1,0:T(8,128)(2,1)} %bitcast.12), calls=%async_computation | async-start | bytes 2097152 | tf_op jit(solution)/shard_map/all_to_all | solution.py:409
  35.9 2.8 %shard_map.157.filt_ref = f32[8,64,256]{2,1,0:T(8,128)} custom-call(s32[1]{0:T(128)} %bitcast.5.place_ref, f32[32,8192]{1,0:T(8,128)} %taps_ref.1, bf16[128,128]{1,0:T(8,128)(2,1)} %constant.32.first_ref, f32[64,256]{1,0:T(8,128)} %constant.22.clone.twist_ref, bf16[512,256]{1,0:T(8,128)(2,1)} %constant.37.ahead_ref), custom_call_target="tpu_custom_call" | custom-call | flops 4000000000 | bytes 2000000 | tf_op jit(solution)/shard_map/pallas_call | solution.py:353
  38.6 28.9 %all-to-all-done = bf16[256,16,128]{2,1,0:T(8,128)(2,1)S(1)} async-done(((bf16[256,16,128]{2,1,0:T(8,128)(2,1)}), bf16[256,16,128]{2,1,0:T(8,128)(2,1)S(1)}, u32[]{:S(2)}, u32[]{:S(2)}) %all-to-all-start) | async-done | bytes 1048608 | tf_op jit(solution)/shard_map/all_to_all | solution.py:409
  67.5 1.0 copy-done
  68.5 9.9 %shard_map.158 = (bf16[4,64,16,128]{3,2,1,0:T(8,128)(2,1)}, f32[8,64,256]{2,1,0:T(8,128)}) custom-call(bf16[4,64,16,128]{3,2,1,0:T(8,128)(2,1)} %bitcast.11, f32[8,64,256]{2,1,0:T(8,128)} %shard_map.157.filt_ref, bf16[128,128]{1,0:T(8,128)(2,1)} %constant.32.first_ref, bf16[64,256]{1,0:T(8,128)(2,1)} %constant.42.last_ref, ...), custom_call_target="tpu_custom_call" | custom-call | flops 8000000000 | bytes 6000000 | tf_op jit(solution)/shard_map/pallas_call | solution.py:353
  78.4 39.5 %all_to_all.10 = bf16[256,16,128]{2,1,0:T(8,128)(2,1)} all-to-all(bf16[256,16,128]{2,1,0:T(8,128)(2,1)} %bitcast.14), channel_id=1, replica_groups=mesh['dp'=4,'ctx'=64] {'dp','ctx'}, dimensions={0} | all-to-all | bytes 2097152 | tf_op jit(solution)/shard_map/all_to_all | solution.py:420
  117.9 10.2 %shard_map.159 = (bf16[128,2048]{1,0:T(8,128)(2,1)}, f32[128,6144]{1,0:T(8,128)}, bf16[8,6144]{1,0:T(8,128)(2,1)}, f32[8,768]{1,0:T(8,128)}) custom-call(bf16[4,64,16,128]{3,2,1,0:T(8,128)(2,1)} %bitcast.13, f32[128,6144]{1,0:T(8,128)} %get-tuple-element.14.feats_ref, bf16[128,2048]{1,0:T(8,128)(2,1)} %bitcast.18, bf16[128,6144]{1,0:T(8,128)(2,1)} %bitcast.16, ...), custom_call_target="tpu_custom_call" | custom-call | flops 4000000000 | bytes 9000000 | tf_op jit(solution)/shard_map/pallas_call | solution.py:353
  128.1 1.4 collective-permute-done.5
  129.4 0.7 add.26
  130.4 2.6 %shard_map.161.own_ref = bf16[8,8192]{1,0:T(8,128)(2,1)} custom-call(f32[8,64,256]{2,1,0:T(8,128)} %get-tuple-element.18.corr_ref, bf16[64,256]{1,0:T(8,128)(2,1)} %constant.42.last_ref, f32[64,256]{1,0:T(8,128)} %constant.22.clone.twist_ref, bf16[512,256]{1,0:T(8,128)(2,1)} %constant.47.back_ref), custom_call_target="tpu_custom_call" | custom-call | flops 2000000000 | bytes 1000000 | tf_op jit(solution)/shard_map/pallas_call | solution.py:353
  133.0 1.5 collective-permute-start.4
  134.5 0.8 collective-permute-start.3
  135.3 2.1 %collective-permute-start.2 = (bf16[8,8192]{1,0:T(8,128)(2,1)}, bf16[8,8192]{1,0:T(8,128)(2,1)S(1)}, u32[]{:S(2)}, u32[]{:S(2)}) collective-permute-start(bf16[8,8192]{1,0:T(8,128)(2,1)} %shard_map.161.own_ref), channel_id=1, source_target_pairs={{0,64},{64,0},{128,192},{192,128},{1,65},{65,1},{129,193},{193,129... | collective-permute-start | bytes 393224 | tf_op jit(solution)/shard_map/ppermute | solution.py:375
  137.4 1.6 collective-permute-start.7
  139.0 3.8 %collective-permute-done.7 = f32[8,768]{1,0:T(8,128)S(1)} collective-permute-done((f32[8,768]{1,0:T(8,128)S(1)}, f32[8,768]{1,0:T(8,128)S(1)}, u32[]{:S(2)}, u32[]{:S(2)}) %collective-permute-start.7) | collective-permute-done | bytes 24608 | tf_op jit(solution)/shard_map/ppermute | solution.py:375
  142.8 1.4 collective-permute-start.8
  144.2 1.9 %collective-permute-start.1 = (bf16[8,6144]{1,0:T(8,128)(2,1)S(1)}, bf16[8,6144]{1,0:T(8,128)(2,1)S(1)}, u32[]{:S(2)}, u32[]{:S(2)}) collective-permute-start(bf16[8,6144]{1,0:T(8,128)(2,1)S(1)} %copy-done.4), channel_id=1, source_target_pairs={{1,0},{2,1},{3,2},{4,3},{5,4},{6,5},{7,6},{8,7},{9,8},{10,9},{11,1... | collective-permute-start | bytes 294920 | tf_op jit(solution)/shard_map/ppermute | solution.py:371
  147.2 4.8 %collective-permute-done.9 = f32[8,768]{1,0:T(8,128)S(1)} collective-permute-done((f32[8,768]{1,0:T(8,128)S(1)}, f32[8,768]{1,0:T(8,128)S(1)}, u32[]{:S(2)}, u32[]{:S(2)}) %collective-permute-start.9) | collective-permute-done | bytes 24608 | tf_op jit(solution)/shard_map/ppermute | solution.py:375
  152.0 0.8 collective-permute-start.10
  152.8 7.2 %collective-permute-done.10 = f32[8,768]{1,0:T(8,128)S(1)} collective-permute-done((f32[8,768]{1,0:T(8,128)S(1)}, f32[8,768]{1,0:T(8,128)S(1)}, u32[]{:S(2)}, u32[]{:S(2)}) %collective-permute-start.10) | collective-permute-done | bytes 24608 | tf_op jit(solution)/shard_map/ppermute | solution.py:375
  160.7 0.7 copy-done.3
  161.4 2.1 %shard_map.162 = f32[32,8192]{1,0:T(8,128)} custom-call(s32[1]{0:T(128)} %bitcast.5.place_ref, bf16[8,8192]{1,0:T(8,128)(2,1)} %shard_map.161.own_ref, bf16[8,8192]{1,0:T(8,128)(2,1)} %copy-done.3, bf16[8,8192]{1,0:T(8,128)(2,1)} %copy-done.2, bf16[8,8192]{1,0:T(8,128)(2,1)} %copy-done.1), custom_call_target="tpu_custom_call" | custom-call | flops 100000000 | bytes 2000000 | tf_op jit(solution)/shard_map/pallas_call | solution.py:353
  163.8 1.6 collective-permute-start.12
  165.4 0.6 copy-done.5
  166.0 7.4 %shard_map.160 = bf16[128,6144]{1,0:T(8,128)(2,1)} custom-call(f32[128,6144]{1,0:T(8,128)} %get-tuple-element.16.gso_ref, bf16[8,6144]{1,0:T(8,128)(2,1)} %copy-done.5, f32[8,768]{1,0:T(8,128)} %concatenate.15.taps_ref), custom_call_target="tpu_custom_call" | custom-call | flops 4000000000 | bytes 6000000 | tf_op jit(solution)/shard_map/pallas_call | solution.py:353
  173.5 0.6 slice_add_fusion
  (28 shorter events, 2.3 us)
Async XLA Ops:
  1.5 8.0 %collective-permute-start = (bf16[8,6144]{1,0:T(8,128)(2,1)S(1)}, bf16[8,6144]{1,0:T(8,128)(2,1)S(1)}, u32[]{:S(2)}, u32[]{:S(2)}) collective-permute-start(bf16[8,6144]{1,0:T(8,128)(2,1)S(1)} %slice_bitcast_fusion), channel_id=1, source_target_pairs={{0,1},{1,2},{2,3},{3,4},{4,5},{5,6},{6,7},{7,8},{8,9},{9,10},{10,1... | collective-permute-start | bytes 294920 | tf_op jit(solution)/shard_map/ppermute | solution.py:371
  9.6 0.7 copy-start.6
  19.7 47.8 %all-to-all-start = ((bf16[256,16,128]{2,1,0:T(8,128)(2,1)}), bf16[256,16,128]{2,1,0:T(8,128)(2,1)S(1)}, u32[]{:S(2)}, u32[]{:S(2)}) async-start(bf16[256,16,128]{2,1,0:T(8,128)(2,1)} %bitcast.12), calls=%async_computation | async-start | bytes 2097152 | tf_op jit(solution)/shard_map/all_to_all | solution.py:409
  67.5 1.0 copy-start
  128.0 1.4 collective-permute-start.5
  130.2 7.2 %collective-permute-start.6 = (f32[8,768]{1,0:T(8,128)S(1)}, f32[8,768]{1,0:T(8,128)S(1)}, u32[]{:S(2)}, u32[]{:S(2)}) collective-permute-start(f32[8,768]{1,0:T(8,128)S(1)} %add.26), channel_id=1, source_target_pairs={{0,2},{1,3},{2,0},{3,1},{4,6},{5,7},{6,4},{7,5},{8,10},{9,11},{10,... | collective-permute-start | bytes 73736 | tf_op jit(solution)/shard_map/ppermute | solution.py:375
  130.4 13.9 %copy-start.4 = (bf16[8,6144]{1,0:T(8,128)(2,1)S(1)}, bf16[8,6144]{1,0:T(8,128)(2,1)}, u32[]{:S(2)}) copy-start(bf16[8,6144]{1,0:T(8,128)(2,1)} %get-tuple-element.17) | copy-start | bytes 294916
  133.0 27.0 %collective-permute-start.4 = (bf16[8,8192]{1,0:T(8,128)(2,1)}, bf16[8,8192]{1,0:T(8,128)(2,1)S(1)}, u32[]{:S(2)}, u32[]{:S(2)}) collective-permute-start(bf16[8,8192]{1,0:T(8,128)(2,1)} %shard_map.161.own_ref), channel_id=1, source_target_pairs={{0,192},{64,128},{128,64},{192,0},{1,193},{65,129},{129,65},{193,1... | collective-permute-start | bytes 393224 | tf_op jit(solution)/shard_map/ppermute | solution.py:375
  134.5 25.5 %collective-permute-start.3 = (bf16[8,8192]{1,0:T(8,128)(2,1)}, bf16[8,8192]{1,0:T(8,128)(2,1)S(1)}, u32[]{:S(2)}, u32[]{:S(2)}) collective-permute-start(bf16[8,8192]{1,0:T(8,128)(2,1)} %shard_map.161.own_ref), channel_id=1, source_target_pairs={{0,128},{64,192},{128,0},{192,64},{1,129},{65,193},{129,1},{193,65... | collective-permute-start | bytes 393224 | tf_op jit(solution)/shard_map/ppermute | solution.py:375
  135.3 24.8 %collective-permute-start.2 = (bf16[8,8192]{1,0:T(8,128)(2,1)}, bf16[8,8192]{1,0:T(8,128)(2,1)S(1)}, u32[]{:S(2)}, u32[]{:S(2)}) collective-permute-start(bf16[8,8192]{1,0:T(8,128)(2,1)} %shard_map.161.own_ref), channel_id=1, source_target_pairs={{0,64},{64,0},{128,192},{192,128},{1,65},{65,1},{129,193},{193,129... | collective-permute-start | bytes 393224 | tf_op jit(solution)/shard_map/ppermute | solution.py:375
  137.4 5.4 %collective-permute-start.7 = (f32[8,768]{1,0:T(8,128)S(1)}, f32[8,768]{1,0:T(8,128)S(1)}, u32[]{:S(2)}, u32[]{:S(2)}) collective-permute-start(f32[8,768]{1,0:T(8,128)S(1)} %add.27), channel_id=1, source_target_pairs={{0,4},{1,5},{2,6},{3,7},{4,0},{5,1},{6,2},{7,3},{8,12},{9,13},{10,... | collective-permute-start | bytes 73736 | tf_op jit(solution)/shard_map/ppermute | solution.py:375
  142.8 3.8 %collective-permute-start.8 = (f32[8,768]{1,0:T(8,128)S(1)}, f32[8,768]{1,0:T(8,128)S(1)}, u32[]{:S(2)}, u32[]{:S(2)}) collective-permute-start(f32[8,768]{1,0:T(8,128)S(1)} %add.28), channel_id=1, source_target_pairs={{0,8},{1,9},{2,10},{3,11},{4,12},{5,13},{6,14},{7,15},{8,0},{9,1},... | collective-permute-start | bytes 73736 | tf_op jit(solution)/shard_map/ppermute | solution.py:375
  144.2 21.2 %collective-permute-start.1 = (bf16[8,6144]{1,0:T(8,128)(2,1)S(1)}, bf16[8,6144]{1,0:T(8,128)(2,1)S(1)}, u32[]{:S(2)}, u32[]{:S(2)}) collective-permute-start(bf16[8,6144]{1,0:T(8,128)(2,1)S(1)} %copy-done.4), channel_id=1, source_target_pairs={{1,0},{2,1},{3,2},{4,3},{5,4},{6,5},{7,6},{8,7},{9,8},{10,9},{11,1... | collective-permute-start | bytes 294920 | tf_op jit(solution)/shard_map/ppermute | solution.py:371
  146.7 5.3 %collective-permute-start.9 = (f32[8,768]{1,0:T(8,128)S(1)}, f32[8,768]{1,0:T(8,128)S(1)}, u32[]{:S(2)}, u32[]{:S(2)}) collective-permute-start(f32[8,768]{1,0:T(8,128)S(1)} %add.29), channel_id=1, source_target_pairs={{0,16},{1,17},{2,18},{3,19},{4,20},{5,21},{6,22},{7,23},{8,24},{9,... | collective-permute-start | bytes 73736 | tf_op jit(solution)/shard_map/ppermute | solution.py:375
  152.0 8.0 %collective-permute-start.10 = (f32[8,768]{1,0:T(8,128)S(1)}, f32[8,768]{1,0:T(8,128)S(1)}, u32[]{:S(2)}, u32[]{:S(2)}) collective-permute-start(f32[8,768]{1,0:T(8,128)S(1)} %add.30), channel_id=1, source_target_pairs={{0,32},{1,33},{2,34},{3,35},{4,36},{5,37},{6,38},{7,39},{8,40},{9,... | collective-permute-start | bytes 73736 | tf_op jit(solution)/shard_map/ppermute | solution.py:375
  160.0 3.8 %collective-permute-start.11 = (f32[8,768]{1,0:T(8,128)S(1)}, f32[8,768]{1,0:T(8,128)S(1)}, u32[]{:S(2)}, u32[]{:S(2)}) collective-permute-start(f32[8,768]{1,0:T(8,128)S(1)} %add.31), channel_id=1, source_target_pairs={{0,64},{64,0},{128,192},{192,128},{1,65},{65,1},{129,193},{193,129... | collective-permute-start | bytes 73736 | tf_op jit(solution)/shard_map/ppermute | solution.py:375
  160.0 0.6 copy-start.1
  160.0 0.7 copy-start.2
  160.7 0.7 copy-start.3
  163.8 9.6 %collective-permute-start.12 = (f32[8,768]{1,0:T(8,128)S(1)}, f32[8,768]{1,0:T(8,128)S(1)}, u32[]{:S(2)}, u32[]{:S(2)}) collective-permute-start(f32[8,768]{1,0:T(8,128)S(1)} %add.32), channel_id=1, source_target_pairs={{0,128},{64,192},{128,0},{192,64},{1,129},{65,193},{129,1},{193,65... | collective-permute-start | bytes 73736 | tf_op jit(solution)/shard_map/ppermute | solution.py:375
  165.4 0.6 copy-start.5

commit v2 on v1

--- a/solution.py
+++ b/solution.py
@@ -15,7 +15,7 @@
 OWN = 8
 HALO = 8
 ROT = -0.25
-VMEM_LIMIT = 56 * 1024 * 1024
+VMEM_LIMIT = 16 * 1024 * 1024
 
 
 def two_parts(table):
@@ -215,19 +215,27 @@
 
 
 def spread_taps(taps_ref, group_size, wide):
-    groups = taps_ref.shape[1]
-    table = group_table(LANES, group_size)
-    for at in range(groups // LANES):
-        wide[:, at * LANES * group_size : (at + 1) * LANES * group_size] = jnp.dot(
-            taps_ref[:, at * LANES : (at + 1) * LANES],
-            table,
-            precision=lax.Precision.HIGHEST,
-            preferred_element_type=F32,
-        )
+    tap_count, groups = taps_ref.shape
+    blocks = groups // LANES
+    rows = jnp.concatenate(
+        [
+            jnp.concatenate([taps_ref[:, at * LANES : (at + 1) * LANES], jnp.zeros((8 - tap_count, LANES), F32)], axis=0)
+            for at in range(blocks)
+        ],
+        axis=0,
+    )
+    high = rows.astype(BF16)
+    rest = rows - high.astype(F32)
+    middle = rest.astype(BF16)
+    low = (rest - middle.astype(F32)).astype(BF16)
+    table = group_table(LANES, group_size).astype(BF16)
+    spread = mxu(high, table) + (mxu(middle, table) + mxu(low, table))
+    for at in range(blocks):
+        wide[:, at * LANES * group_size : (at + 1) * LANES * group_size] = spread[at * 8 : (at + 1) * 8]
 
 
 def short_kernel(
-    tap_count, group_size, qkv_ref, rim_ref, taps_ref, cot_ref, feats_ref, out_ref, padded, wide
+    tap_count, group_size, qkv_ref, rim_ref, taps_ref, cot_ref, feats_ref, out_ref, wide, padded
 ):
     rows, width_all = qkv_ref.shape
     width = width_all // 3
@@ -326,9 +334,8 @@
         )
 
 
-def back_kernel(tap_count, group_size, gso_ref, rim_ref, taps_ref, out_ref, padded, wide):
+def back_kernel(tap_count, gso_ref, rim_ref, wide, out_ref, padded):
     rows, width_all = gso_ref.shape
-    spread_taps(taps_ref, group_size, wide)
     padded[rows - HALO : rows, :] = gso_ref[rows - HALO : rows, :]
     padded[rows : rows + HALO, :] = rim_ref[...].astype(F32)
     body = rows - HALO
@@ -386,11 +393,9 @@
     scale = 1.0 / math.sqrt(seqs * length)
     first, last, twist, ahead, back = make_tables(ctx_count, rows)
     place = lax.axis_index("dp").astype(jnp.int32).reshape(1)
-    taps = jnp.concatenate([short_filter, jnp.zeros((8 - tap_count, groups), F32)], axis=0)
     left_rim = neighbours(feats_in[rows - HALO :], 1)
     pair = (seqs, ctx_count, 2 * OWN, rows)
     wide_pad = pltpu.VMEM((rows + HALO, width_all), F32)
-    wide_taps = pltpu.VMEM((8, width_all), F32)
     filt = call(
         functools.partial(filter_kernel, ctx_count),
         shape((OWN, ctx_count, 2 * rows), F32),
@@ -399,11 +404,11 @@
         (4e9, 2e6),
         1,
     )
-    feats, sent = call(
+    feats, sent, wide_taps = call(
         functools.partial(short_kernel, tap_count, group_size),
-        (shape((rows, width_all), F32), shape(pair, BF16)),
-        [wide_pad, wide_taps],
-        (feats_in, left_rim, taps, cot),
+        (shape((rows, width_all), F32), shape(pair, BF16), shape((8, width_all), F32)),
+        [wide_pad],
+        (feats_in, left_rim, short_filter, cot),
         (4e9, 6e6),
     )
     got = lax.all_to_all(
@@ -428,6 +433,15 @@
         (2e9, 1e6),
     )
     others = [partner(own_taps, "dp", mask) for mask in (1, 2, 3)]
+    grad_long = call(
+        join_kernel,
+        shape((seqs * OWN, length), F32),
+        [],
+        (place, own_taps, *others),
+        (1e8, 2e6),
+        1,
+    )
+    returned, grad_long = lax.optimization_barrier((returned, grad_long))
     mixer_out, gso, edge, short_part = call(
         functools.partial(gate_kernel, tap_count, group_size, scale),
         (
@@ -441,26 +455,20 @@
         (4e9, 9e6),
     )
     right_rim = neighbours(edge, -1)
-    grad_rows = call(
-        functools.partial(back_kernel, tap_count, group_size),
-        shape((rows, width_all), BF16),
-        [pltpu.VMEM((rows + HALO, width_all), F32), wide_taps],
-        (gso, right_rim, taps),
-        (4e9, 6e6),
-    )
-    for axis in ("ctx", "dp"):
-        mask = 1
-        while mask < lax.axis_size(axis):
-            short_part = short_part + partner(short_part, axis, mask)
-            mask *= 2
-    grad_long = call(
-        join_kernel,
-        shape((seqs * OWN, length), F32),
-        [],
-        (place, own_taps, *others),
-        (1e8, 2e6),
-        1,
-    )
+    masks = [(axis, 1 << bit) for axis in ("ctx", "dp") for bit in range((lax.axis_size(axis) - 1).bit_length())]
+    for axis, mask in masks:
+        if (axis, mask) == ("ctx", ctx_count // 2):
+            gso, right_rim, short_part = lax.optimization_barrier((gso, right_rim, short_part))
+            grad_rows = call(
+                functools.partial(back_kernel, tap_count),
+                shape((rows, width_all), BF16),
+                [wide_pad],
+                (gso, right_rim, wide_taps),
+                (4e9, 6e6),
+            )
+        short_part = short_part + partner(short_part, axis, mask)
+        if (axis, mask) == ("ctx", ctx_count // 2):
+            grad_rows, short_part = lax.optimization_barrier((grad_rows, short_part))
     return mixer_out[None], grad_rows[None], grad_long, short_part[:tap_count]
 
 

time: 176 us -> 171 us (0.972)
  blocking collectives: 39.5 us -> 0 us
  waiting for transfers between devices: 51.8 us -> 86.5 us
  Pallas kernels: 44.5 us -> 27.8 us
  starting transfers between devices: 30.4 us -> 45 us
  local copies, waits for them, and re-layouts: 5.83 us -> 9.47 us
    all_to_all x1 -> x0, blocking collectives: 39.5 us -> none  [shards(): lax.all_to_all(mixed.reshape(seqs * ctx_count, 2 * OWN, rows), ('dp', 'ct...]
    ppermute x11, waiting for transfers between devices: 18.1 us -> 50.2 us  [partner(): lax.ppermute(array, axis, [(i, i ^ mask) for i in range(lax.axis_size(axi...]
    pallas_call x7, Pallas kernels: 44.5 us -> 27.8 us  [call(): pl.pallas_call(kernel, out_shape=outs, in_specs=[smem] * scalars + [vmem]...]
    ppermute x11, starting transfers between devices: 10.5 us -> 17.1 us  [partner(): lax.ppermute(array, axis, [(i, i ^ mask) for i in range(lax.axis_size(axi...]
    all_to_all x0 -> x1, starting transfers between devices: none -> 6.46 us  [shards(): lax.all_to_all(mixed.reshape(seqs * ctx_count, 2 * OWN, rows), ('dp', 'ct...]
    unnamed x14 -> x30, local copies, waits for them, and re-layouts: 3.58 us -> 8.57 us
  transfers between devices with their start and end apart: 14 -> 15, of which waited for: 8 -> 10; matrix products, arithmetic and copies ran while one was open for 1% -> 0% of each run, Pallas kernels for 9% -> 4%
where the time goes in v2:
time: 171 us; the launch traced here: 170 us
  waiting for transfers between devices  86.5 us (51%)
  starting transfers between devices  45 us (26%)
  Pallas kernels  27.8 us (16%)
  local copies, waits for them, and re-layouts  9.47 us (6%)
    ppermute x11, waiting for transfers between devices, partner(): lax.ppermute(array, axis, [(i, i ^ mask) for i in range(lax.axis_size(axi...  50.2 us
    all_to_all x1, waiting for transfers between devices, shards(): lax.all_to_all(sent.reshape(seqs * ctx_count, 2 * OWN, rows), ('dp', 'ctx...  30.2 us
    pallas_call x7, Pallas kernels, call(): pl.pallas_call(kernel, out_shape=outs, in_specs=[smem] * scalars + [vmem]...  27.8 us
    ppermute x11, starting transfers between devices, partner(): lax.ppermute(array, axis, [(i, i ^ mask) for i in range(lax.axis_size(axi...  17.1 us
    all_to_all x1, starting transfers between devices, shards(): lax.all_to_all(sent.reshape(seqs * ctx_count, 2 * OWN, rows), ('dp', 'ctx...  16.1 us
    unnamed x30, local copies, waits for them, and re-layouts  8.57 us
    all_to_all x1, starting transfers between devices, shards(): lax.all_to_all(mixed.reshape(seqs * ctx_count, 2 * OWN, rows), ('dp', 'ct...  6.46 us
    ppermute x2, waiting for transfers between devices, neighbours(): return lax.ppermute(array, 'ctx', pairs)  6.12 us
  transfers between devices with their start and end apart: 15, of which 10 were waited for; matrix products, arithmetic and copies ran while one was open for 0% of the time, Pallas kernels for 4%

profile of v2, /device:TPU:8, one launch (start us, length us, event | category | flops | bytes accessed | tf_op | source)
XLA Modules:
  0.0 170.3 jit_solution(17504844079025904132)
XLA Ops:
  0.6 0.9 slice_bitcast_fusion
  1.5 1.9 %collective-permute-start = (bf16[8,6144]{1,0:T(8,128)(2,1)S(1)}, bf16[8,6144]{1,0:T(8,128)(2,1)S(1)}, u32[]{:S(2)}, u32[]{:S(2)}) collective-permute-start(bf16[8,6144]{1,0:T(8,128)(2,1)S(1)} %slice_bitcast_fusion), channel_id=1, source_target_pairs={{0,1},{1,2},{2,3},{3,4},{4,5},{5,6},{6,7},{7,8},{8,9},{9,10},{10,1... | collective-permute-start | bytes 294920 | tf_op jit(solution)/shard_map/ppermute | solution.py:378
  3.4 6.1 %collective-permute-done.rim_ref = bf16[8,6144]{1,0:T(8,128)(2,1)S(1)} collective-permute-done((bf16[8,6144]{1,0:T(8,128)(2,1)S(1)}, bf16[8,6144]{1,0:T(8,128)(2,1)S(1)}, u32[]{:S(2)}, u32[]{:S(2)}) %collective-permute-start) | collective-permute-done | bytes 98336 | tf_op jit(solution)/shard_map/ppermute | solution.py:378
  9.6 1.4 copy-done
  11.0 1.0 copy-done.3
  12.8 5.9 %shard_map.156 = (f32[128,6144]{1,0:T(8,128)S(1)}, bf16[4,64,16,128]{3,2,1,0:T(8,128)(2,1)}, f32[8,6144]{1,0:T(8,128)S(1)}) custom-call(bf16[128,6144]{1,0:T(8,128)(2,1)S(1)} %bitcast.13, bf16[8,6144]{1,0:T(8,128)(2,1)S(1)} %collective-permute-done.rim_ref, f32[7,768]{1,0:T(8,128)S(1)} %copy-done.5, bf16[128,2048]{1,0:T(8,128)(2,1)S(1)} %bitcast.15), custom_call_target="tpu_custom_call" | custom-call | flops 4000000000 | bytes 6000000 | tf_op jit(solution)/shard_map/pallas_call | solution.py:360
  18.7 1.6 copy-done.11
  20.3 16.1 %all-to-all-start = ((bf16[256,16,128]{2,1,0:T(8,128)(2,1)}), bf16[256,16,128]{2,1,0:T(8,128)(2,1)S(1)}, u32[]{:S(2)}, u32[]{:S(2)}) async-start(bf16[256,16,128]{2,1,0:T(8,128)(2,1)} %bitcast.3), calls=%async_computation | async-start | bytes 2097152 | tf_op jit(solution)/shard_map/all_to_all | solution.py:414
  37.2 0.8 copy-done.13
  38.0 30.2 %all-to-all-done = bf16[256,16,128]{2,1,0:T(8,128)(2,1)S(1)} async-done(((bf16[256,16,128]{2,1,0:T(8,128)(2,1)}), bf16[256,16,128]{2,1,0:T(8,128)(2,1)S(1)}, u32[]{:S(2)}, u32[]{:S(2)}) %all-to-all-start) | async-done | bytes 1048608 | tf_op jit(solution)/shard_map/all_to_all | solution.py:414
  68.2 1.0 copy-done.14
  69.2 8.3 %shard_map.158 = (bf16[4,64,16,128]{3,2,1,0:T(8,128)(2,1)}, f32[8,64,256]{2,1,0:T(8,128)S(1)}) custom-call(bf16[4,64,16,128]{3,2,1,0:T(8,128)(2,1)S(1)} %bitcast.12, f32[8,64,256]{2,1,0:T(8,128)S(1)} %copy-done.14, bf16[128,128]{1,0:T(8,128)(2,1)S(1)} %copy-done.10, bf16[64,256]{1,0:T(8,128)(2,1)S(1)} %copy-done.9, f32[64,256]{1,0:T(8,128)S(1)} %copy-done.8, ...), custom_call_target="tpu_custom_call" | custom-call | flops 8000000000 | bytes 6000000 | tf_op jit(solution)/shard_map/pallas_call | solution.py:360
  77.5 6.5 %all-to-all-start.1 = ((bf16[256,16,128]{2,1,0:T(8,128)(2,1)}), bf16[256,16,128]{2,1,0:T(8,128)(2,1)S(1)}, u32[]{:S(2)}, u32[]{:S(2)}) async-start(bf16[256,16,128]{2,1,0:T(8,128)(2,1)} %bitcast.6), calls=%async_computation.1 | async-start | bytes 2097152 | tf_op jit(solution)/shard_map/all_to_all | solution.py:425
  84.0 0.8 shard_map.159.own_ref
  84.8 4.2 %collective-permute-start.3 = (bf16[8,8192]{1,0:T(8,128)(2,1)S(1)}, bf16[8,8192]{1,0:T(8,128)(2,1)S(1)}, u32[]{:S(2)}, u32[]{:S(2)}) collective-permute-start(bf16[8,8192]{1,0:T(8,128)(2,1)S(1)} %shard_map.159.own_ref), channel_id=1, source_target_pairs={{0,192},{64,128},{128,64},{192,0},{1,193},{65,129},{129,65},{193,1... | collective-permute-start | bytes 393224 | tf_op jit(solution)/shard_map/ppermute | solution.py:382
  89.6 23.3 %collective-permute-done.3.three_ref = bf16[8,8192]{1,0:T(8,128)(2,1)S(1)} collective-permute-done((bf16[8,8192]{1,0:T(8,128)(2,1)S(1)}, bf16[8,8192]{1,0:T(8,128)(2,1)S(1)}, u32[]{:S(2)}, u32[]{:S(2)}) %collective-permute-start.3) | collective-permute-done | bytes 131104 | tf_op jit(solution)/shard_map/ppermute | solution.py:382
  112.9 7.0 %collective-permute-done.2.two_ref = bf16[8,8192]{1,0:T(8,128)(2,1)S(1)} collective-permute-done((bf16[8,8192]{1,0:T(8,128)(2,1)S(1)}, bf16[8,8192]{1,0:T(8,128)(2,1)S(1)}, u32[]{:S(2)}, u32[]{:S(2)}) %collective-permute-start.2) | collective-permute-done | bytes 131104 | tf_op jit(solution)/shard_map/ppermute | solution.py:382
  119.9 1.0 shard_map.160
  121.0 1.9 %copy-done.12 = f32[128,6144]{1,0:T(8,128)S(1)} copy-done((f32[128,6144]{1,0:T(8,128)S(1)}, f32[128,6144]{1,0:T(8,128)}, u32[]{:S(2)}) %copy-start.12) | copy-done | bytes 3145752
  122.9 6.7 %shard_map.161 = (bf16[128,2048]{1,0:T(8,128)(2,1)}, f32[128,6144]{1,0:T(8,128)S(1)}, bf16[8,6144]{1,0:T(8,128)(2,1)S(1)}, f32[8,768]{1,0:T(8,128)S(1)}) custom-call(bf16[4,64,16,128]{3,2,1,0:T(8,128)(2,1)S(1)} %bitcast.11, f32[128,6144]{1,0:T(8,128)S(1)} %copy-done.12, bf16[128,2048]{1,0:T(8,128)(2,1)S(1)} %bitcast.16, bf16[128,6144]{1,0:T(8,128)(2,1)S(1)} %bitcast.14, ...), custom_call_target="tpu_custom_call" | custom-call | flops 4000000000 | bytes 9000000 | tf_op jit(solution)/shard_map/pallas_call | solution.py:360
  129.6 1.2 collective-permute-done.5
  130.8 1.5 collective-permute-start.6
  132.3 3.4 %collective-permute-start.4 = (bf16[8,6144]{1,0:T(8,128)(2,1)S(1)}, bf16[8,6144]{1,0:T(8,128)(2,1)S(1)}, u32[]{:S(2)}, u32[]{:S(2)}) collective-permute-start(bf16[8,6144]{1,0:T(8,128)(2,1)S(1)} %get-tuple-element.27), channel_id=1, source_target_pairs={{1,0},{2,1},{3,2},{4,3},{5,4},{6,5},{7,6},{8,7},{9,8},{10,9},{11,1... | collective-permute-start | bytes 294920 | tf_op jit(solution)/shard_map/ppermute | solution.py:378
  135.7 1.9 %collective-permute-start.7 = (f32[8,768]{1,0:T(8,128)S(1)}, f32[8,768]{1,0:T(8,128)S(1)}, u32[]{:S(2)}, u32[]{:S(2)}) collective-permute-start(f32[8,768]{1,0:T(8,128)S(1)} %add.25), channel_id=1, source_target_pairs={{0,4},{1,5},{2,6},{3,7},{4,0},{5,1},{6,2},{7,3},{8,12},{9,13},{10,... | collective-permute-start | bytes 73736 | tf_op jit(solution)/shard_map/ppermute | solution.py:382
  137.6 3.5 %collective-permute-done.7 = f32[8,768]{1,0:T(8,128)S(1)} collective-permute-done((f32[8,768]{1,0:T(8,128)S(1)}, f32[8,768]{1,0:T(8,128)S(1)}, u32[]{:S(2)}, u32[]{:S(2)}) %collective-permute-start.7) | collective-permute-done | bytes 24608 | tf_op jit(solution)/shard_map/ppermute | solution.py:382
  141.1 3.8 %collective-permute-done.8 = f32[8,768]{1,0:T(8,128)S(1)} collective-permute-done((f32[8,768]{1,0:T(8,128)S(1)}, f32[8,768]{1,0:T(8,128)S(1)}, u32[]{:S(2)}, u32[]{:S(2)}) %collective-permute-start.8) | collective-permute-done | bytes 24608 | tf_op jit(solution)/shard_map/ppermute | solution.py:382
  145.0 2.5 %collective-permute-start.9 = (f32[8,768]{1,0:T(8,128)S(1)}, f32[8,768]{1,0:T(8,128)S(1)}, u32[]{:S(2)}, u32[]{:S(2)}) collective-permute-start(f32[8,768]{1,0:T(8,128)S(1)} %add.27), channel_id=1, source_target_pairs={{0,16},{1,17},{2,18},{3,19},{4,20},{5,21},{6,22},{7,23},{8,24},{9,... | collective-permute-start | bytes 73736 | tf_op jit(solution)/shard_map/ppermute | solution.py:382
  147.5 2.8 %collective-permute-done.9 = f32[8,768]{1,0:T(8,128)S(1)} collective-permute-done((f32[8,768]{1,0:T(8,128)S(1)}, f32[8,768]{1,0:T(8,128)S(1)}, u32[]{:S(2)}, u32[]{:S(2)}) %collective-permute-start.9) | collective-permute-done | bytes 24608 | tf_op jit(solution)/shard_map/ppermute | solution.py:382
  150.3 6.3 %collective-permute-start.10 = (f32[8,768]{1,0:T(8,128)S(1)}, f32[8,768]{1,0:T(8,128)S(1)}, u32[]{:S(2)}, u32[]{:S(2)}) collective-permute-start(f32[8,768]{1,0:T(8,128)S(1)} %add.28), channel_id=1, source_target_pairs={{0,32},{1,33},{2,34},{3,35},{4,36},{5,37},{6,38},{7,39},{8,40},{9,... | collective-permute-start | bytes 73736 | tf_op jit(solution)/shard_map/ppermute | solution.py:382
  156.6 4.4 %shard_map.162 = bf16[128,6144]{1,0:T(8,128)(2,1)} custom-call(f32[128,6144]{1,0:T(8,128)S(1)} %get-tuple-element.29.gso_ref, bf16[8,6144]{1,0:T(8,128)(2,1)S(1)} %collective-permute-done.4.rim_ref, f32[8,6144]{1,0:T(8,128)S(1)} %get-tuple-element.31.wide), custom_call_target="tpu_custom_call" | custom-call | flops 4000000000 | bytes 6000000 | tf_op jit(solution)/shard_map/pallas_call | solution.py:360
  161.1 3.8 %collective-permute-done.11 = f32[8,768]{1,0:T(8,128)S(1)} collective-permute-done((f32[8,768]{1,0:T(8,128)S(1)}, f32[8,768]{1,0:T(8,128)S(1)}, u32[]{:S(2)}, u32[]{:S(2)}) %collective-permute-start.11) | collective-permute-done | bytes 24608 | tf_op jit(solution)/shard_map/ppermute | solution.py:382
  164.9 4.7 %collective-permute-done.12 = f32[8,768]{1,0:T(8,128)S(1)} collective-permute-done((f32[8,768]{1,0:T(8,128)S(1)}, f32[8,768]{1,0:T(8,128)S(1)}, u32[]{:S(2)}, u32[]{:S(2)}) %collective-permute-start.12) | collective-permute-done | bytes 24608 | tf_op jit(solution)/shard_map/ppermute | solution.py:382
  (44 shorter events, 2.9 us)
Async XLA Ops:
  1.5 8.0 %collective-permute-start = (bf16[8,6144]{1,0:T(8,128)(2,1)S(1)}, bf16[8,6144]{1,0:T(8,128)(2,1)S(1)}, u32[]{:S(2)}, u32[]{:S(2)}) collective-permute-start(bf16[8,6144]{1,0:T(8,128)(2,1)S(1)} %slice_bitcast_fusion), channel_id=1, source_target_pairs={{0,1},{1,2},{2,3},{3,4},{4,5},{5,6},{6,7},{7,8},{8,9},{9,10},{10,1... | collective-permute-start | bytes 294920 | tf_op jit(solution)/shard_map/ppermute | solution.py:378
  9.6 1.4 copy-start
  11.0 1.0 copy-start.3
  12.0 0.7 copy-start.5
  18.7 1.6 copy-start.11
  20.3 16.2 %copy-start.2 = (f32[32,8192]{1,0:T(8,128)S(1)}, f32[32,8192]{1,0:T(8,128)}, u32[]{:S(2)}) copy-start(f32[32,8192]{1,0:T(8,128)} %taps_ref.3) | copy-start | bytes 3145732
  20.3 16.2 %copy-start.7 = (bf16[512,256]{1,0:T(8,128)(2,1)S(1)}, bf16[512,256]{1,0:T(8,128)(2,1)}, u32[]{:S(2)}) copy-start(bf16[512,256]{1,0:T(8,128)(2,1)} %constant.33.ahead_ref) | copy-start | bytes 786436
  20.3 16.2 %copy-start.8 = (f32[64,256]{1,0:T(8,128)S(1)}, f32[64,256]{1,0:T(8,128)}, u32[]{:S(2)}) copy-start(f32[64,256]{1,0:T(8,128)} %constant.20.clone.twist_ref) | copy-start | bytes 196612
  20.3 16.2 %copy-start.10 = (bf16[128,128]{1,0:T(8,128)(2,1)S(1)}, bf16[128,128]{1,0:T(8,128)(2,1)}, u32[]{:S(2)}) copy-start(bf16[128,128]{1,0:T(8,128)(2,1)} %constant.28.first_ref) | copy-start | bytes 98308
  20.3 47.9 %all-to-all-start = ((bf16[256,16,128]{2,1,0:T(8,128)(2,1)}), bf16[256,16,128]{2,1,0:T(8,128)(2,1)S(1)}, u32[]{:S(2)}, u32[]{:S(2)}) async-start(bf16[256,16,128]{2,1,0:T(8,128)(2,1)} %bitcast.3), calls=%async_computation | async-start | bytes 2097152 | tf_op jit(solution)/shard_map/all_to_all | solution.py:414
  36.5 31.7 %copy-start.6 = (bf16[512,256]{1,0:T(8,128)(2,1)S(1)}, bf16[512,256]{1,0:T(8,128)(2,1)}, u32[]{:S(2)}) copy-start(bf16[512,256]{1,0:T(8,128)(2,1)} %constant.43.back_ref) | copy-start | bytes 786436
  36.5 31.6 %copy-start.9 = (bf16[64,256]{1,0:T(8,128)(2,1)S(1)}, bf16[64,256]{1,0:T(8,128)(2,1)}, u32[]{:S(2)}) copy-start(bf16[64,256]{1,0:T(8,128)(2,1)} %constant.38.last_ref) | copy-start | bytes 98308
  37.2 0.8 copy-start.13
  68.2 1.0 copy-start.14
  77.5 43.4 %all-to-all-start.1 = ((bf16[256,16,128]{2,1,0:T(8,128)(2,1)}), bf16[256,16,128]{2,1,0:T(8,128)(2,1)S(1)}, u32[]{:S(2)}, u32[]{:S(2)}) async-start(bf16[256,16,128]{2,1,0:T(8,128)(2,1)} %bitcast.6), calls=%async_computation.1 | async-start | bytes 2097152 | tf_op jit(solution)/shard_map/all_to_all | solution.py:425
  84.0 37.0 %copy-start.4 = (bf16[1,128,2048]{2,1,0:T(8,128)(2,1)S(1)}, bf16[1,128,2048]{2,1,0:T(8,128)(2,1)}, u32[]{:S(2)}) copy-start(bf16[1,128,2048]{2,1,0:T(8,128)(2,1)} %param.16) | copy-start | bytes 1572868
  84.8 36.2 %copy-start.1 = (bf16[1,128,6144]{2,1,0:T(8,128)(2,1)S(1)}, bf16[1,128,6144]{2,1,0:T(8,128)(2,1)}, u32[]{:S(2)}) copy-start(bf16[1,128,6144]{2,1,0:T(8,128)(2,1)} %param.13) | copy-start | bytes 4718596
  84.8 28.1 %collective-permute-start.3 = (bf16[8,8192]{1,0:T(8,128)(2,1)S(1)}, bf16[8,8192]{1,0:T(8,128)(2,1)S(1)}, u32[]{:S(2)}, u32[]{:S(2)}) collective-permute-start(bf16[8,8192]{1,0:T(8,128)(2,1)S(1)} %shard_map.159.own_ref), channel_id=1, source_target_pairs={{0,192},{64,128},{128,64},{192,0},{1,193},{65,129},{129,65},{193,1... | collective-permute-start | bytes 393224 | tf_op jit(solution)/shard_map/ppermute | solution.py:382
  89.0 31.0 %collective-permute-start.2 = (bf16[8,8192]{1,0:T(8,128)(2,1)S(1)}, bf16[8,8192]{1,0:T(8,128)(2,1)S(1)}, u32[]{:S(2)}, u32[]{:S(2)}) collective-permute-start(bf16[8,8192]{1,0:T(8,128)(2,1)S(1)} %shard_map.159.own_ref), channel_id=1, source_target_pairs={{0,128},{64,192},{128,0},{192,64},{1,129},{65,193},{129,1},{193,65... | collective-permute-start | bytes 393224 | tf_op jit(solution)/shard_map/ppermute | solution.py:382
  89.0 31.0 %collective-permute-start.1 = (bf16[8,8192]{1,0:T(8,128)(2,1)S(1)}, bf16[8,8192]{1,0:T(8,128)(2,1)S(1)}, u32[]{:S(2)}, u32[]{:S(2)}) collective-permute-start(bf16[8,8192]{1,0:T(8,128)(2,1)S(1)} %shard_map.159.own_ref), channel_id=1, source_target_pairs={{0,64},{64,0},{128,192},{192,128},{1,65},{65,1},{129,193},{193,129... | collective-permute-start | bytes 393224 | tf_op jit(solution)/shard_map/ppermute | solution.py:382
  121.0 1.9 %copy-start.12 = (f32[128,6144]{1,0:T(8,128)S(1)}, f32[128,6144]{1,0:T(8,128)}, u32[]{:S(2)}) copy-start(f32[128,6144]{1,0:T(8,128)} %copy-done.11) | copy-start | bytes 9437188
  129.6 1.2 collective-permute-start.5
  130.8 4.9 %collective-permute-start.6 = (f32[8,768]{1,0:T(8,128)S(1)}, f32[8,768]{1,0:T(8,128)S(1)}, u32[]{:S(2)}, u32[]{:S(2)}) collective-permute-start(f32[8,768]{1,0:T(8,128)S(1)} %add.24), channel_id=1, source_target_pairs={{0,2},{1,3},{2,0},{3,1},{4,6},{5,7},{6,4},{7,5},{8,10},{9,11},{10,... | collective-permute-start | bytes 73736 | tf_op jit(solution)/shard_map/ppermute | solution.py:382
  132.3 18.0 %collective-permute-start.4 = (bf16[8,6144]{1,0:T(8,128)(2,1)S(1)}, bf16[8,6144]{1,0:T(8,128)(2,1)S(1)}, u32[]{:S(2)}, u32[]{:S(2)}) collective-permute-start(bf16[8,6144]{1,0:T(8,128)(2,1)S(1)} %get-tuple-element.27), channel_id=1, source_target_pairs={{1,0},{2,1},{3,2},{4,3},{5,4},{6,5},{7,6},{8,7},{9,8},{10,9},{11,1... | collective-permute-start | bytes 294920 | tf_op jit(solution)/shard_map/ppermute | solution.py:378
  135.7 5.4 %collective-permute-start.7 = (f32[8,768]{1,0:T(8,128)S(1)}, f32[8,768]{1,0:T(8,128)S(1)}, u32[]{:S(2)}, u32[]{:S(2)}) collective-permute-start(f32[8,768]{1,0:T(8,128)S(1)} %add.25), channel_id=1, source_target_pairs={{0,4},{1,5},{2,6},{3,7},{4,0},{5,1},{6,2},{7,3},{8,12},{9,13},{10,... | collective-permute-start | bytes 73736 | tf_op jit(solution)/shard_map/ppermute | solution.py:382
  141.1 3.8 %collective-permute-start.8 = (f32[8,768]{1,0:T(8,128)S(1)}, f32[8,768]{1,0:T(8,128)S(1)}, u32[]{:S(2)}, u32[]{:S(2)}) collective-permute-start(f32[8,768]{1,0:T(8,128)S(1)} %add.26), channel_id=1, source_target_pairs={{0,8},{1,9},{2,10},{3,11},{4,12},{5,13},{6,14},{7,15},{8,0},{9,1},... | collective-permute-start | bytes 73736 | tf_op jit(solution)/shard_map/ppermute | solution.py:382
  145.0 5.3 %collective-permute-start.9 = (f32[8,768]{1,0:T(8,128)S(1)}, f32[8,768]{1,0:T(8,128)S(1)}, u32[]{:S(2)}, u32[]{:S(2)}) collective-permute-start(f32[8,768]{1,0:T(8,128)S(1)} %add.27), channel_id=1, source_target_pairs={{0,16},{1,17},{2,18},{3,19},{4,20},{5,21},{6,22},{7,23},{8,24},{9,... | collective-permute-start | bytes 73736 | tf_op jit(solution)/shard_map/ppermute | solution.py:382
  150.3 10.7 %collective-permute-start.10 = (f32[8,768]{1,0:T(8,128)S(1)}, f32[8,768]{1,0:T(8,128)S(1)}, u32[]{:S(2)}, u32[]{:S(2)}) collective-permute-start(f32[8,768]{1,0:T(8,128)S(1)} %add.28), channel_id=1, source_target_pairs={{0,32},{1,33},{2,34},{3,35},{4,36},{5,37},{6,38},{7,39},{8,40},{9,... | collective-permute-start | bytes 73736 | tf_op jit(solution)/shard_map/ppermute | solution.py:382
  161.0 3.9 %collective-permute-start.11 = (f32[8,768]{1,0:T(8,128)S(1)}, f32[8,768]{1,0:T(8,128)S(1)}, u32[]{:S(2)}, u32[]{:S(2)}) collective-permute-start(f32[8,768]{1,0:T(8,128)S(1)} %add.29), channel_id=1, source_target_pairs={{0,64},{64,0},{128,192},{192,128},{1,65},{65,1},{129,193},{193,129... | collective-permute-start | bytes 73736 | tf_op jit(solution)/shard_map/ppermute | solution.py:382
  164.9 4.7 %collective-permute-start.12 = (f32[8,768]{1,0:T(8,128)S(1)}, f32[8,768]{1,0:T(8,128)S(1)}, u32[]{:S(2)}, u32[]{:S(2)}) collective-permute-start(f32[8,768]{1,0:T(8,128)S(1)} %add.30), channel_id=1, source_target_pairs={{0,128},{64,192},{128,0},{192,64},{1,129},{65,193},{129,1},{193,65... | collective-permute-start | bytes 73736 | tf_op jit(solution)/shard_map/ppermute | solution.py:382

commit v3 on v2

--- a/solution.py
+++ b/solution.py
@@ -13,9 +13,11 @@
 BF16 = jnp.bfloat16
 LANES = 128
 OWN = 8
+TAPS = 7
 HALO = 8
 ROT = -0.25
-VMEM_LIMIT = 16 * 1024 * 1024
+GRANT = 16 * 1024 * 1024
+BLOCK = 512
 
 
 def two_parts(table):
@@ -102,13 +104,11 @@
     return jnp.concatenate([real, imag], axis=1)
 
 
-def filter_kernel(rows, place_ref, taps_ref, first_ref, twist_ref, ahead_ref, out_ref, spread):
-    base = pl.multiple_of(place_ref[0] * OWN, OWN)
+def filter_spectra(rows, base, taps_ref, first, twist, ahead, out_ref, spread):
     for row in range(rows):
         spread[row * OWN : (row + 1) * OWN, :] = taps_ref[
             pl.ds(base, OWN), row * LANES : (row + 1) * LANES
         ]
-    first, twist, ahead = first_ref[...], twist_ref[...], ahead_ref[...]
     twist_real, twist_imag = twist[:, :LANES], twist[:, LANES:]
     for half in range(2):
         wide = jnp.concatenate(
@@ -138,8 +138,9 @@
 def mix_kernel(
     seqs,
     rows,
+    place_ref,
     got_ref,
-    filt_ref,
+    taps_ref,
     first_ref,
     last_ref,
     twist_ref,
@@ -149,8 +150,19 @@
     corr_ref,
     spread,
     gather,
+    filt_ref,
 ):
     pair = 2 * OWN
+    filter_spectra(
+        rows,
+        pl.multiple_of(place_ref[0] * OWN, OWN),
+        taps_ref,
+        first_ref[...],
+        twist_ref[...],
+        ahead_ref[...],
+        filt_ref,
+        gather,
+    )
     for seq in range(seqs):
         spread[seq * rows * pair : (seq + 1) * rows * pair, :] = (
             got_ref[seq].astype(F32).reshape(rows * pair, LANES)
@@ -234,39 +246,70 @@
         wide[:, at * LANES * group_size : (at + 1) * LANES * group_size] = spread[at * 8 : (at + 1) * 8]
 
 
+def short_rows(padded, wide, cols, first_row, rows):
+    start = first_row + HALO
+    total = wide(0) * padded[start : start + rows, cols]
+    for lag in range(1, TAPS):
+        total = total + wide(lag) * padded[start - lag : start - lag + rows, cols]
+    return total
+
+
+def owner_tiles(product, grad_in):
+    tiles = [array.reshape(LANES // OWN, OWN, LANES) for array in (product, grad_in)]
+    return jnp.concatenate(tiles, axis=1).astype(BF16).reshape(LANES // OWN // 4, 4, 2 * OWN, LANES)
+
+
 def short_kernel(
-    tap_count, group_size, qkv_ref, rim_ref, taps_ref, cot_ref, feats_ref, out_ref, wide, padded
+    group_size, width, q_ref, k_ref, v_ref, cot_ref, taps_ref, feats_ref, out_ref, wide_ref, padded
 ):
-    rows, width_all = qkv_ref.shape
-    width = width_all // 3
-    spread_taps(taps_ref, group_size, wide)
-    padded[0:HALO, :] = rim_ref[...].astype(F32)
-    padded[HALO : HALO + rows, :] = qkv_ref[...].astype(F32)
+    step = pl.program_id(0)
+    rows, block = q_ref.shape
+
+    @pl.when(step == 0)
+    def _():
+        spread_taps(taps_ref, group_size, wide_ref)
+        padded[0:HALO, :] = jnp.zeros((HALO, 3 * block), F32)
+
+    for part, ref in enumerate((q_ref, k_ref, v_ref)):
+        padded[HALO : HALO + rows, part * block : (part + 1) * block] = ref[...].astype(F32)
     per_chunk = LANES // OWN // 4
-
-    def chunk(at, _):
+    for at in range(block // LANES):
+        here = slice(at * LANES, (at + 1) * LANES)
         parts = []
         for part in range(3):
-            cols = pl.ds(pl.multiple_of(part * width + at * LANES, LANES), LANES)
-            total = wide[0:1, cols] * padded[HALO : HALO + rows, cols]
-            for lag in range(1, tap_count):
-                total = total + wide[lag : lag + 1, cols] * padded[HALO - lag : HALO - lag + rows, cols]
-            feats_ref[:, cols] = total
+            lanes = pl.ds(pl.multiple_of(part * width + step * block + at * LANES, LANES), LANES)
+            cols = slice(part * block + at * LANES, part * block + (at + 1) * LANES)
+            total = short_rows(padded, lambda lag: wide_ref[lag : lag + 1, lanes], cols, 0, rows)
+            feats_ref[part, :, here] = total
             parts.append(total)
-        cols = pl.ds(pl.multiple_of(at * LANES, LANES), LANES)
-        product = (parts[1] * parts[2]).T.reshape(LANES // OWN, OWN, LANES)
-        grad_in = (cot_ref[:, cols].astype(F32) * parts[0]).T.reshape(LANES // OWN, OWN, LANES)
-        both = jnp.concatenate([product, grad_in], axis=1).astype(BF16)
-        both = both.reshape(per_chunk, 4, 2 * OWN, LANES)
+        tiles = owner_tiles((parts[1] * parts[2]).T, (cot_ref[:, here].astype(F32) * parts[0]).T)
         for seq in range(4):
-            out_ref[seq, pl.ds(at * per_chunk, per_chunk)] = both[:, seq]
-        return 0
-
-    lax.fori_loop(0, width // LANES, chunk, 0)
+            out_ref[seq, at * per_chunk : (at + 1) * per_chunk] = tiles[:, seq]
+
+
+def rim_kernel(width, top_ref, rim_ref, cot_ref, wide_ref, feats_in, sent_in, feats_ref, out_ref, padded):
+    padded[0:HALO, :] = rim_ref[...].astype(F32)
+    padded[HALO : 2 * HALO, :] = top_ref[...].astype(F32)[:HALO]
+    per_chunk = LANES // OWN // 4
+    fresh = lax.broadcasted_iota(jnp.int32, (per_chunk, 2 * OWN, LANES), 2) < HALO
+    blank = jnp.zeros((LANES - HALO, LANES), F32)
+    for at in range(width // LANES):
+        parts = []
+        for part in range(3):
+            cols = slice(part * width + at * LANES, part * width + (at + 1) * LANES)
+            total = short_rows(padded, lambda lag: wide_ref[lag : lag + 1, cols], cols, 0, HALO)
+            feats_ref[part, :, at * LANES : (at + 1) * LANES] = total
+            parts.append(total)
+        cot = cot_ref[:, at * LANES : (at + 1) * LANES].astype(F32)[:HALO]
+        product = jnp.concatenate([parts[1] * parts[2], blank], axis=0).T
+        grad_in = jnp.concatenate([cot * parts[0], blank], axis=0).T
+        tiles = owner_tiles(product, grad_in)
+        here = slice(at * per_chunk, (at + 1) * per_chunk)
+        for seq in range(4):
+            out_ref[seq, here] = jnp.where(fresh, tiles[:, seq], sent_in[seq, here])
 
 
 def gate_kernel(
-    tap_count,
     group_size,
     scale,
     got_ref,
@@ -288,66 +331,70 @@
     per_chunk = LANES // OWN // 4
 
     def chunk(at, _):
+        here = pl.ds(pl.multiple_of(at * LANES, LANES), LANES)
         both = jnp.stack(
             [got_ref[seq, pl.ds(at * per_chunk, per_chunk)] for seq in range(4)], axis=1
         ).astype(F32)
         both = both.reshape(LANES // OWN, 2 * OWN, LANES)
         long_out = both[:, :OWN].reshape(LANES, LANES).T
         grad_product = both[:, OWN:].reshape(LANES, LANES).T
-        cols = [
-            pl.ds(pl.multiple_of(part * width + at * LANES, LANES), LANES) for part in range(3)
-        ]
-        mixer_ref[:, cols[0]] = (feats_ref[:, cols[0]] * long_out).astype(BF16)
+        mixer_ref[:, here] = (feats_ref[0, :, here] * long_out).astype(BF16)
         grads = (
-            cot_ref[:, cols[0]].astype(F32) * long_out,
-            grad_product * feats_ref[:, cols[2]],
-            grad_product * feats_ref[:, cols[1]],
+            cot_ref[:, here].astype(F32) * long_out,
+            grad_product * feats_ref[2, :, here],
+            grad_product * feats_ref[1, :, here],
         )
         for part in range(3):
-            gso_ref[:, cols[part]] = grads[part]
-            edge_ref[:, cols[part]] = grads[part][:HALO].astype(BF16)
-            for lag in range(tap_count):
-                term = grads[part] * padded[HALO - lag : HALO - lag + rows, cols[part]]
-                sums[lag * 8 : (lag + 1) * 8, cols[part]] = jnp.sum(
+            cols = pl.ds(pl.multiple_of(part * width + at * LANES, LANES), LANES)
+            gso_ref[:, cols] = grads[part]
+            edge_ref[:, cols] = grads[part][:HALO].astype(BF16)
+            for lag in range(TAPS):
+                term = grads[part] * padded[HALO - lag : HALO - lag + rows, cols]
+                sums[lag * 8 : (lag + 1) * 8, cols] = jnp.sum(
                     term.reshape(rows // 8, 8, LANES), axis=0
                 )
         return 0
 
     lax.fori_loop(0, width // LANES, chunk, 0)
-    table = group_table(LANES, group_size)
-    block = LANES * group_size
-    for at in range(width_all // block):
-        lags = [
-            jnp.sum(sums[lag * 8 : (lag + 1) * 8, at * block : (at + 1) * block], axis=0, keepdims=True)
-            for lag in range(tap_count)
+    span = LANES * group_size
+    blocks = width_all // span
+    lags = []
+    for at in range(blocks):
+        lags += [
+            jnp.sum(sums[lag * 8 : (lag + 1) * 8, at * span : (at + 1) * span], axis=0, keepdims=True)
+            for lag in range(TAPS)
         ]
-        lags = jnp.concatenate(lags + [jnp.zeros((8 - tap_count, block), F32)], axis=0)
-        short_ref[:, at * LANES : (at + 1) * LANES] = (
-            lax.dot_general(
-                lags,
-                table,
-                (((1,), (1,)), ((), ())),
-                precision=lax.Precision.HIGHEST,
-                preferred_element_type=F32,
-            )
-            * scale
-        )
-
-
-def back_kernel(tap_count, gso_ref, rim_ref, wide, out_ref, padded):
+        lags.append(jnp.zeros((8 - TAPS, span), F32))
+    lags = jnp.concatenate(lags, axis=0)
+    high = lags.astype(BF16)
+    rest = lags - high.astype(F32)
+    middle = rest.astype(BF16)
+    low = (rest - middle.astype(F32)).astype(BF16)
+    table = group_table(LANES, group_size).astype(BF16)
+    dims = (((1,), (1,)), ((), ()))
+    total = lax.dot_general(
+        jnp.concatenate([high, middle, low], axis=0), table, dims, preferred_element_type=F32
+    )
+    count = blocks * 8
+    total = total[:count] + (total[count : 2 * count] + total[2 * count :])
+    for at in range(blocks):
+        short_ref[:, at * LANES : (at + 1) * LANES] = total[at * 8 : (at + 1) * 8] * scale
+
+
+def back_kernel(gso_ref, rim_ref, wide_ref, out_ref, tail):
     rows, width_all = gso_ref.shape
-    padded[rows - HALO : rows, :] = gso_ref[rows - HALO : rows, :]
-    padded[rows : rows + HALO, :] = rim_ref[...].astype(F32)
     body = rows - HALO
+    tail[0:HALO, :] = gso_ref[body:rows, :]
+    tail[HALO : 2 * HALO, :] = rim_ref[...].astype(F32)
 
     def chunk(at, _):
         cols = pl.ds(pl.multiple_of(at * LANES, LANES), LANES)
-        total = wide[0:1, cols] * gso_ref[0:body, cols]
-        tail = wide[0:1, cols] * padded[body:rows, cols]
-        for lag in range(1, tap_count):
-            total = total + wide[lag : lag + 1, cols] * gso_ref[lag : lag + body, cols]
-            tail = tail + wide[lag : lag + 1, cols] * padded[body + lag : rows + lag, cols]
-        out_ref[:, cols] = jnp.concatenate([total, tail], axis=0).astype(BF16)
+        total = wide_ref[0:1, cols] * gso_ref[0:body, cols]
+        end = wide_ref[0:1, cols] * tail[0:HALO, cols]
+        for lag in range(1, TAPS):
+            total = total + wide_ref[lag : lag + 1, cols] * gso_ref[lag : lag + body, cols]
+            end = end + wide_ref[lag : lag + 1, cols] * tail[lag : lag + HALO, cols]
+        out_ref[:, cols] = jnp.concatenate([total, end], axis=0).astype(BF16)
         return 0
 
     lax.fori_loop(0, width_all // LANES, chunk, 0)
@@ -356,15 +403,32 @@
 def call(kernel, outs, scratch, args, cost, scalars=0):
     vmem = pl.BlockSpec(memory_space=pltpu.VMEM)
     smem = pl.BlockSpec(memory_space=pltpu.SMEM)
-    flops, moved = (int(value) for value in cost)
     return pl.pallas_call(
         kernel,
         out_shape=outs,
         in_specs=[smem] * scalars + [vmem] * (len(args) - scalars),
         out_specs=jax.tree.map(lambda _: vmem, outs),
         scratch_shapes=scratch,
-        compiler_params=pltpu.CompilerParams(vmem_limit_bytes=VMEM_LIMIT),
-        cost_estimate=pl.CostEstimate(flops=flops, bytes_accessed=moved, transcendentals=0),
+        compiler_params=pltpu.CompilerParams(vmem_limit_bytes=GRANT),
+        cost_estimate=estimate(*cost),
+    )(*args)
+
+
+def estimate(flops, moved):
+    return pl.CostEstimate(flops=int(flops), bytes_accessed=int(moved), transcendentals=0)
+
+
+def grid_call(kernel, steps, outs, out_specs, scratch, args, in_specs, cost, aliases=None):
+    return pl.pallas_call(
+        kernel,
+        grid=(steps,),
+        out_shape=outs,
+        in_specs=in_specs,
+        out_specs=out_specs,
+        scratch_shapes=scratch,
+        input_output_aliases=aliases or {},
+        compiler_params=pltpu.CompilerParams(vmem_limit_bytes=GRANT),
+        cost_estimate=estimate(*cost),
     )(*args)
 
 
@@ -395,32 +459,59 @@
     place = lax.axis_index("dp").astype(jnp.int32).reshape(1)
     left_rim = neighbours(feats_in[rows - HALO :], 1)
     pair = (seqs, ctx_count, 2 * OWN, rows)
-    wide_pad = pltpu.VMEM((rows + HALO, width_all), F32)
-    filt = call(
-        functools.partial(filter_kernel, ctx_count),
-        shape((OWN, ctx_count, 2 * rows), F32),
-        [pltpu.VMEM((length // rows * OWN, rows), F32)],
-        (place, long_filter, first, twist, ahead),
-        (4e9, 2e6),
+    block = BLOCK
+    steps = width // block
+    owners = block // OWN // seqs
+    lanes = [
+        pl.BlockSpec((rows, block), lambda i, part=part: (0, part * steps + i)) for part in range(3)
+    ]
+    triple = pl.BlockSpec((3, rows, block), lambda i: (0, 0, i))
+    tiles = pl.BlockSpec((seqs, owners, 2 * OWN, rows), lambda i: (0, i, 0, 0))
+    padded = pltpu.VMEM((rows + HALO, 3 * block), F32)
+    whole = lambda *dims: pl.BlockSpec(dims, lambda i: (0,) * len(dims))
+    feats_shape = shape((3, rows, width), F32)
+    feats, sent, wide_taps = grid_call(
+        functools.partial(short_kernel, group_size, width),
+        steps,
+        (feats_shape, shape(pair, BF16), shape((8, width_all), F32)),
+        (triple, tiles, whole(8, width_all)),
+        [padded],
+        (feats_in, feats_in, feats_in, cot, short_filter),
+        [*lanes, lanes[0], whole(tap_count, groups)],
+        (1e9, 6e6),
+    )
+    top = pl.BlockSpec((2 * HALO, width_all), lambda i: (0, 0))
+    rows_top = pl.BlockSpec((3, HALO, width), lambda i: (0, 0, 0))
+    feats, sent = grid_call(
+        functools.partial(rim_kernel, width),
         1,
-    )
-    feats, sent, wide_taps = call(
-        functools.partial(short_kernel, tap_count, group_size),
-        (shape((rows, width_all), F32), shape(pair, BF16), shape((8, width_all), F32)),
-        [wide_pad],
-        (feats_in, left_rim, short_filter, cot),
-        (4e9, 6e6),
+        (feats_shape, shape(pair, BF16)),
+        (rows_top, whole(*pair)),
+        [pltpu.VMEM((2 * HALO, width_all), F32)],
+        (feats_in, left_rim, cot, wide_taps, feats, sent),
+        [
+            top,
+            whole(HALO, width_all),
+            pl.BlockSpec((2 * HALO, width), lambda i: (0, 0)),
+            whole(8, width_all),
+            rows_top,
+            whole(*pair),
+        ],
+        (1e8, 2e6),
+        {4: 0, 5: 1},
     )
     got = lax.all_to_all(
         sent.reshape(seqs * ctx_count, 2 * OWN, rows), ("dp", "ctx"), 0, 0, tiled=True
     ).reshape(pair)
     long_rows = pltpu.VMEM((seqs * ctx_count * 2 * OWN, rows), F32)
+    spectra = (OWN, ctx_count, 2 * rows)
     mixed, corr = call(
         functools.partial(mix_kernel, seqs, ctx_count),
-        (shape(pair, BF16), shape((OWN, ctx_count, 2 * rows), F32)),
-        [long_rows, long_rows],
-        (got, filt, first, last, twist, ahead, back),
+        (shape(pair, BF16), shape(spectra, F32)),
+        [long_rows, long_rows, pltpu.VMEM(spectra, F32)],
+        (place, got, long_filter, first, last, twist, ahead, back),
         (8e9, 6e6),
+        1,
     )
     returned = lax.all_to_all(
         mixed.reshape(seqs * ctx_count, 2 * OWN, rows), ("dp", "ctx"), 0, 0, tiled=True
@@ -430,44 +521,52 @@
         shape((OWN, length), BF16),
         [pltpu.VMEM((ctx_count * OWN, rows), F32)],
         (corr, last, twist, back),
-        (2e9, 1e6),
-    )
-    others = [partner(own_taps, "dp", mask) for mask in (1, 2, 3)]
-    grad_long = call(
-        join_kernel,
-        shape((seqs * OWN, length), F32),
-        [],
-        (place, own_taps, *others),
-        (1e8, 2e6),
-        1,
-    )
-    returned, grad_long = lax.optimization_barrier((returned, grad_long))
+        (1e9, 1e6),
+    )
+    returned, own_taps = lax.optimization_barrier((returned, own_taps))
     mixer_out, gso, edge, short_part = call(
-        functools.partial(gate_kernel, tap_count, group_size, scale),
+        functools.partial(gate_kernel, group_size, scale),
         (
             shape((rows, width), BF16),
             shape((rows, width_all), F32),
             shape((HALO, width_all), BF16),
             shape((8, groups), F32),
         ),
-        [wide_pad, pltpu.VMEM((tap_count * 8, width_all), F32)],
+        [pltpu.VMEM((rows + HALO, width_all), F32), pltpu.VMEM((tap_count * 8, width_all), F32)],
         (returned, feats, cot, feats_in, left_rim),
-        (4e9, 9e6),
+        (1e9, 9e6),
     )
     right_rim = neighbours(edge, -1)
-    masks = [(axis, 1 << bit) for axis in ("ctx", "dp") for bit in range((lax.axis_size(axis) - 1).bit_length())]
-    for axis, mask in masks:
-        if (axis, mask) == ("ctx", ctx_count // 2):
+    masks = [
+        (axis, 1 << bit)
+        for axis in ("ctx", "dp")
+        for bit in range((lax.axis_size(axis) - 1).bit_length())
+    ]
+    for at, (axis, mask) in enumerate(masks):
+        if at == 2:
+            own_taps, short_part = lax.optimization_barrier((own_taps, short_part))
+            others = [partner(own_taps, "dp", step) for step in (1, 2, 3)]
+        if at == 5:
             gso, right_rim, short_part = lax.optimization_barrier((gso, right_rim, short_part))
             grad_rows = call(
-                functools.partial(back_kernel, tap_count),
+                back_kernel,
                 shape((rows, width_all), BF16),
-                [wide_pad],
+                [pltpu.VMEM((2 * HALO, width_all), F32)],
                 (gso, right_rim, wide_taps),
-                (4e9, 6e6),
+                (1e9, 6e6),
+            )
+        if at == 7:
+            others, short_part = lax.optimization_barrier((others, short_part))
+            grad_long = call(
+                join_kernel,
+                shape((seqs * OWN, length), F32),
+                [],
+                (place, own_taps, *others),
+                (1e8, 2e6),
+                1,
             )
         short_part = short_part + partner(short_part, axis, mask)
-        if (axis, mask) == ("ctx", ctx_count // 2):
+        if at == 5:
             grad_rows, short_part = lax.optimization_barrier((grad_rows, short_part))
     return mixer_out[None], grad_rows[None], grad_long, short_part[:tap_count]
 

time: 171 us -> 158 us (0.924)
  waiting for transfers between devices: 86.5 us -> 73.8 us
  starting transfers between devices: 45 us -> 42 us
  local copies, waits for them, and re-layouts: 9.47 us -> 12 us
    ppermute x11, waiting for transfers between devices: 50.2 us -> 13.7 us  [partner(): lax.ppermute(array, axis, [(i, i ^ mask) for i in range(lax.axis_size(axi...]
    all_to_all x1, waiting for transfers between devices: 0.01 us -> 28.3 us  [shards(): lax.all_to_all(mixed.reshape(seqs * ctx_count, 2 * OWN, rows), ('dp', 'ct...]
    pallas_call x7 -> x5, Pallas kernels: 27.8 us -> 18.9 us  [call(): pl.pallas_call(kernel, out_shape=outs, in_specs=[smem] * scalars + [vmem]...]
    pallas_call x0 -> x2, Pallas kernels: none -> 8.14 us  [grid_call(): pl.pallas_call(kernel, grid=(steps,), out_shape=outs, in_specs=in_specs,...]
    ppermute x2, waiting for transfers between devices: 6.12 us -> 0.01 us  [neighbours(): return lax.ppermute(array, 'ctx', pairs)]
    unnamed x30 -> x38, local copies, waits for them, and re-layouts: 8.57 us -> 11.1 us
    ppermute x11, starting transfers between devices: 17.1 us -> 14.8 us  [partner(): lax.ppermute(array, axis, [(i, i ^ mask) for i in range(lax.axis_size(axi...]
  transfers between devices with their start and end apart: 15 -> 15, of which waited for: 10 -> 9; matrix products, arithmetic and copies ran while one was open for 0% -> 0% of each run, Pallas kernels for 4% -> 7%
where the time goes in v3:
time: 158 us; the launch traced here: 156 us
  waiting for transfers between devices  73.8 us (47%)
  starting transfers between devices  42 us (27%)
  Pallas kernels  27 us (17%)
  local copies, waits for them, and re-layouts  12 us (8%)
    all_to_all x1, waiting for transfers between devices, shards(): lax.all_to_all(sent.reshape(seqs * ctx_count, 2 * OWN, rows), ('dp', 'ctx...  31.7 us
    all_to_all x1, waiting for transfers between devices, shards(): lax.all_to_all(mixed.reshape(seqs * ctx_count, 2 * OWN, rows), ('dp', 'ct...  28.3 us
    pallas_call x5, Pallas kernels, call(): pl.pallas_call(kernel, out_shape=outs, in_specs=[smem] * scalars + [vmem]...  18.9 us
    all_to_all x1, starting transfers between devices, shards(): lax.all_to_all(sent.reshape(seqs * ctx_count, 2 * OWN, rows), ('dp', 'ctx...  15.5 us
    ppermute x11, starting transfers between devices, partner(): lax.ppermute(array, axis, [(i, i ^ mask) for i in range(lax.axis_size(axi...  14.8 us
    ppermute x11, waiting for transfers between devices, partner(): lax.ppermute(array, axis, [(i, i ^ mask) for i in range(lax.axis_size(axi...  13.7 us
    unnamed x38, local copies, waits for them, and re-layouts  11.1 us
    pallas_call x2, Pallas kernels, grid_call(): pl.pallas_call(kernel, grid=(steps,), out_shape=outs, in_specs=in_specs,...  8.14 us
  transfers between devices with their start and end apart: 15, of which 9 were waited for; matrix products, arithmetic and copies ran while one was open for 0% of the time, Pallas kernels for 7%

profile of v3, /device:TPU:8, one launch (start us, length us, event | category | flops | bytes accessed | tf_op | source)
XLA Modules:
  0.0 156.3 jit_solution(10020587184559239533)
XLA Ops:
  0.6 0.9 slice_bitcast_fusion
  1.5 1.9 %collective-permute-start = (bf16[8,6144]{1,0:T(8,128)(2,1)S(1)}, bf16[8,6144]{1,0:T(8,128)(2,1)S(1)}, u32[]{:S(2)}, u32[]{:S(2)}) collective-permute-start(bf16[8,6144]{1,0:T(8,128)(2,1)S(1)} %slice_bitcast_fusion), channel_id=1, source_target_pairs={{0,1},{1,2},{2,3},{3,4},{4,5},{5,6},{6,7},{7,8},{8,9},{9,10},{10,1... | collective-permute-start | bytes 294920 | tf_op jit(solution)/shard_map/ppermute | solution.py:442
  3.5 1.4 copy-done
  4.9 1.0 copy-done.4
  6.6 5.3 %shard_map.156 = (f32[3,128,2048]{2,1,0:T(8,128)S(1)}, bf16[4,64,16,128]{3,2,1,0:T(8,128)(2,1)}, f32[8,6144]{1,0:T(8,128)S(1)}) custom-call(bf16[128,6144]{1,0:T(8,128)(2,1)S(1)} %bitcast.11, bf16[128,6144]{1,0:T(8,128)(2,1)S(1)} %bitcast.12, bf16[128,6144]{1,0:T(8,128)(2,1)S(1)} %bitcast.13, bf16[128,2048]{1,0:T(8,128)(2,1)S(1)} %bitcast.16, ...), custom_call_target="tpu_custom_call" | custom-call | flops 1000000000 | bytes 6000000 | tf_op jit(solution)/shard_map/pallas_call | solution.py:422
  12.0 2.8 %shard_map.157 = (f32[3,128,2048]{2,1,0:T(8,128)S(1)}, bf16[4,64,16,128]{3,2,1,0:T(8,128)(2,1)}) custom-call(bf16[128,6144]{1,0:T(8,128)(2,1)S(1)} %bitcast.14, bf16[8,6144]{1,0:T(8,128)(2,1)S(1)} %collective-permute-done.rim_ref, bf16[128,2048]{1,0:T(8,128)(2,1)S(1)} %bitcast.17, ...), custom_call_target="tpu_custom_call", output_to_operand_aliasing={{0}: (4, {}), {1}: (5, {})} | custom-call | flops 100000000 | bytes 2000000 | tf_op jit(solution)/shard_map/pallas_call | solution.py:422
  14.8 1.6 %copy-done.2 = f32[3,128,2048]{2,1,0:T(8,128)} copy-done((f32[3,128,2048]{2,1,0:T(8,128)}, f32[3,128,2048]{2,1,0:T(8,128)S(1)}, u32[]{:S(2)}) %copy-start.2) | copy-done | bytes 3145752
  16.5 15.5 %all-to-all-start = ((bf16[256,16,128]{2,1,0:T(8,128)(2,1)}), bf16[256,16,128]{2,1,0:T(8,128)(2,1)S(1)}, u32[]{:S(2)}, u32[]{:S(2)}) async-start(bf16[256,16,128]{2,1,0:T(8,128)(2,1)} %bitcast.4), calls=%async_computation | async-start | bytes 2097152 | tf_op jit(solution)/shard_map/all_to_all | solution.py:503
  32.0 31.7 %all-to-all-done = bf16[256,16,128]{2,1,0:T(8,128)(2,1)S(1)} async-done(((bf16[256,16,128]{2,1,0:T(8,128)(2,1)}), bf16[256,16,128]{2,1,0:T(8,128)(2,1)S(1)}, u32[]{:S(2)}, u32[]{:S(2)}) %all-to-all-start) | async-done | bytes 1048608 | tf_op jit(solution)/shard_map/all_to_all | solution.py:503
  63.7 7.7 %shard_map.158 = (bf16[4,64,16,128]{3,2,1,0:T(8,128)(2,1)S(1)}, f32[8,64,256]{2,1,0:T(8,128)S(1)}) custom-call(s32[1]{0:T(128)} %bitcast.place_ref, bf16[4,64,16,128]{3,2,1,0:T(8,128)(2,1)S(1)} %bitcast.20, f32[32,8192]{1,0:T(8,128)S(1)} %copy-done.10, bf16[128,128]{1,0:T(8,128)(2,1)S(1)} %copy-done.16, bf16[64,256]{1,0:T(8,128)(2,1)S(1)} %copy-done.15, ...), custom_call_target="tpu_custom_call" | custom-call | flops 8000000000 | bytes 6000000 | tf_op jit(solution)/shard_map/pallas_call | solution.py:406
  72.2 1.0 copy-done.6
  73.2 6.6 %all-to-all-start.1 = ((bf16[256,16,128]{2,1,0:T(8,128)(2,1)}), bf16[256,16,128]{2,1,0:T(8,128)(2,1)S(1)}, u32[]{:S(2)}, u32[]{:S(2)}) async-start(bf16[256,16,128]{2,1,0:T(8,128)(2,1)} %bitcast.21), calls=%async_computation.1 | async-start | bytes 2097152 | tf_op jit(solution)/shard_map/all_to_all | solution.py:516
  79.8 0.9 copy-done.12
  80.7 1.0 copy-done.18
  83.2 28.3 %all-to-all-done.1 = bf16[256,16,128]{2,1,0:T(8,128)(2,1)S(1)} async-done(((bf16[256,16,128]{2,1,0:T(8,128)(2,1)}), bf16[256,16,128]{2,1,0:T(8,128)(2,1)S(1)}, u32[]{:S(2)}, u32[]{:S(2)}) %all-to-all-start.1) | async-done | bytes 1048608 | tf_op jit(solution)/shard_map/all_to_all | solution.py:516
  111.6 1.9 %copy-done.3 = f32[3,128,2048]{2,1,0:T(8,128)S(1)} copy-done((f32[3,128,2048]{2,1,0:T(8,128)S(1)}, f32[3,128,2048]{2,1,0:T(8,128)}, u32[]{:S(2)}) %copy-start.3) | copy-done | bytes 3145752
  113.5 5.0 %shard_map.160 = (bf16[128,2048]{1,0:T(8,128)(2,1)}, f32[128,6144]{1,0:T(8,128)S(1)}, bf16[8,6144]{1,0:T(8,128)(2,1)S(1)}, f32[8,768]{1,0:T(8,128)S(1)}) custom-call(bf16[4,64,16,128]{3,2,1,0:T(8,128)(2,1)S(1)} %bitcast.19, f32[3,128,2048]{2,1,0:T(8,128)S(1)} %copy-done.3, bf16[128,2048]{1,0:T(8,128)(2,1)S(1)} %bitcast.18, bf16[128,6144]{1,0:T(8,128)(2,1)S(1)} %bitcast.15, ...), custom_call_target="tpu_custom_call" | custom-call | flops 1000000000 | bytes 9000000 | tf_op jit(solution)/shard_map/pallas_call | solution.py:406
  118.5 1.2 collective-permute-done.2
  119.9 3.2 %collective-permute-start.1 = (bf16[8,6144]{1,0:T(8,128)(2,1)S(1)}, bf16[8,6144]{1,0:T(8,128)(2,1)S(1)}, u32[]{:S(2)}, u32[]{:S(2)}) collective-permute-start(bf16[8,6144]{1,0:T(8,128)(2,1)S(1)} %get-tuple-element.38), channel_id=1, source_target_pairs={{1,0},{2,1},{3,2},{4,3},{5,4},{6,5},{7,6},{8,7},{9,8},{10,9},{11,1... | collective-permute-start | bytes 294920 | tf_op jit(solution)/shard_map/ppermute | solution.py:442
  123.5 1.8 %collective-permute-start.4 = (f32[8,768]{1,0:T(8,128)S(1)}, f32[8,768]{1,0:T(8,128)S(1)}, u32[]{:S(2)}, u32[]{:S(2)}) collective-permute-start(f32[8,768]{1,0:T(8,128)S(1)} %add.25), channel_id=1, source_target_pairs={{0,4},{1,5},{2,6},{3,7},{4,0},{5,1},{6,2},{7,3},{8,12},{9,13},{10,... | collective-permute-start | bytes 73736 | tf_op jit(solution)/shard_map/ppermute | solution.py:446
  125.3 3.6 %collective-permute-done.4 = f32[8,768]{1,0:T(8,128)S(1)} collective-permute-done((f32[8,768]{1,0:T(8,128)S(1)}, f32[8,768]{1,0:T(8,128)S(1)}, u32[]{:S(2)}, u32[]{:S(2)}) %collective-permute-start.4) | collective-permute-done | bytes 24608 | tf_op jit(solution)/shard_map/ppermute | solution.py:446
  128.8 1.4 collective-permute-start.5
  130.2 2.5 %collective-permute-done.5 = f32[8,768]{1,0:T(8,128)S(1)} collective-permute-done((f32[8,768]{1,0:T(8,128)S(1)}, f32[8,768]{1,0:T(8,128)S(1)}, u32[]{:S(2)}, u32[]{:S(2)}) %collective-permute-start.5) | collective-permute-done | bytes 24608 | tf_op jit(solution)/shard_map/ppermute | solution.py:446
  133.1 1.2 collective-permute-start.10
  135.2 2.3 %collective-permute-start.9 = (bf16[8,8192]{1,0:T(8,128)(2,1)S(1)}, bf16[8,8192]{1,0:T(8,128)(2,1)S(1)}, u32[]{:S(2)}, u32[]{:S(2)}) collective-permute-start(bf16[8,8192]{1,0:T(8,128)(2,1)S(1)} %copy-done.8), channel_id=1, source_target_pairs={{0,128},{64,192},{128,0},{192,64},{1,129},{65,193},{129,1},{193,65... | collective-permute-start | bytes 393224 | tf_op jit(solution)/shard_map/ppermute | solution.py:446
  138.0 4.5 %collective-permute-start.7 = (f32[8,768]{1,0:T(8,128)S(1)}, f32[8,768]{1,0:T(8,128)S(1)}, u32[]{:S(2)}, u32[]{:S(2)}) collective-permute-start(f32[8,768]{1,0:T(8,128)S(1)} %add.28), channel_id=1, source_target_pairs={{0,32},{1,33},{2,34},{3,35},{4,36},{5,37},{6,38},{7,39},{8,40},{9,... | collective-permute-start | bytes 73736 | tf_op jit(solution)/shard_map/ppermute | solution.py:446
  142.5 4.4 %shard_map.161 = bf16[128,6144]{1,0:T(8,128)(2,1)} custom-call(f32[128,6144]{1,0:T(8,128)S(1)} %get-tuple-element.42.gso_ref, bf16[8,6144]{1,0:T(8,128)(2,1)S(1)} %collective-permute-done.1.rim_ref, f32[8,6144]{1,0:T(8,128)S(1)} %get-tuple-element.28.wide_ref), custom_call_target="tpu_custom_call" | custom-call | flops 1000000000 | bytes 6000000 | tf_op jit(solution)/shard_map/pallas_call | solution.py:406
  146.9 1.1 collective-permute-start.11
  148.0 2.8 %collective-permute-done.11 = f32[8,768]{1,0:T(8,128)S(1)} collective-permute-done((f32[8,768]{1,0:T(8,128)S(1)}, f32[8,768]{1,0:T(8,128)S(1)}, u32[]{:S(2)}, u32[]{:S(2)}) %collective-permute-start.11) | collective-permute-done | bytes 24608 | tf_op jit(solution)/shard_map/ppermute | solution.py:446
  150.9 0.9 collective-permute-start.12
  151.8 1.0 shard_map.162
  152.9 2.8 %collective-permute-done.12 = f32[8,768]{1,0:T(8,128)S(1)} collective-permute-done((f32[8,768]{1,0:T(8,128)S(1)}, f32[8,768]{1,0:T(8,128)S(1)}, u32[]{:S(2)}, u32[]{:S(2)}) %collective-permute-start.12) | collective-permute-done | bytes 24608 | tf_op jit(solution)/shard_map/ppermute | solution.py:446
  (52 shorter events, 6.1 us)
Async XLA Ops:
  1.5 10.4 %collective-permute-start = (bf16[8,6144]{1,0:T(8,128)(2,1)S(1)}, bf16[8,6144]{1,0:T(8,128)(2,1)S(1)}, u32[]{:S(2)}, u32[]{:S(2)}) collective-permute-start(bf16[8,6144]{1,0:T(8,128)(2,1)S(1)} %slice_bitcast_fusion), channel_id=1, source_target_pairs={{0,1},{1,2},{2,3},{3,4},{4,5},{5,6},{6,7},{7,8},{8,9},{9,10},{10,1... | collective-permute-start | bytes 294920 | tf_op jit(solution)/shard_map/ppermute | solution.py:442
  3.4 1.4 copy-start
  4.9 1.0 copy-start.4
  11.9 51.7 %copy-start.10 = (f32[32,8192]{1,0:T(8,128)S(1)}, f32[32,8192]{1,0:T(8,128)}, u32[]{:S(2)}) copy-start(f32[32,8192]{1,0:T(8,128)} %taps_ref.3) | copy-start | bytes 3145732
  11.9 51.7 %copy-start.11 = (bf16[512,256]{1,0:T(8,128)(2,1)S(1)}, bf16[512,256]{1,0:T(8,128)(2,1)}, u32[]{:S(2)}) copy-start(bf16[512,256]{1,0:T(8,128)(2,1)} %constant.43.back_ref) | copy-start | bytes 786436
  11.9 51.7 %copy-start.13 = (bf16[512,256]{1,0:T(8,128)(2,1)S(1)}, bf16[512,256]{1,0:T(8,128)(2,1)}, u32[]{:S(2)}) copy-start(bf16[512,256]{1,0:T(8,128)(2,1)} %constant.38.ahead_ref) | copy-start | bytes 786436
  12.0 51.7 %copy-start.14 = (f32[64,256]{1,0:T(8,128)S(1)}, f32[64,256]{1,0:T(8,128)}, u32[]{:S(2)}) copy-start(f32[64,256]{1,0:T(8,128)} %constant.20.clone.twist_ref) | copy-start | bytes 196612
  12.0 51.7 %copy-start.15 = (bf16[64,256]{1,0:T(8,128)(2,1)S(1)}, bf16[64,256]{1,0:T(8,128)(2,1)}, u32[]{:S(2)}) copy-start(bf16[64,256]{1,0:T(8,128)(2,1)} %constant.33.last_ref) | copy-start | bytes 98308
  12.0 51.7 %copy-start.16 = (bf16[128,128]{1,0:T(8,128)(2,1)S(1)}, bf16[128,128]{1,0:T(8,128)(2,1)}, u32[]{:S(2)}) copy-start(bf16[128,128]{1,0:T(8,128)(2,1)} %constant.28.first_ref) | copy-start | bytes 98308
  14.8 1.6 %copy-start.2 = (f32[3,128,2048]{2,1,0:T(8,128)}, f32[3,128,2048]{2,1,0:T(8,128)S(1)}, u32[]{:S(2)}) copy-start(f32[3,128,2048]{2,1,0:T(8,128)S(1)} %get-tuple-element.35.feats_ref) | copy-start | bytes 9437188
  16.5 47.2 %all-to-all-start = ((bf16[256,16,128]{2,1,0:T(8,128)(2,1)}), bf16[256,16,128]{2,1,0:T(8,128)(2,1)S(1)}, u32[]{:S(2)}, u32[]{:S(2)}) async-start(bf16[256,16,128]{2,1,0:T(8,128)(2,1)} %bitcast.4), calls=%async_computation | async-start | bytes 2097152 | tf_op jit(solution)/shard_map/all_to_all | solution.py:503
  71.4 0.8 copy-start.17
  72.2 1.0 copy-start.6
  72.2 39.3 %copy-start.1 = (bf16[1,128,6144]{2,1,0:T(8,128)(2,1)S(1)}, bf16[1,128,6144]{2,1,0:T(8,128)(2,1)}, u32[]{:S(2)}) copy-start(bf16[1,128,6144]{2,1,0:T(8,128)(2,1)} %param.13) | copy-start | bytes 4718596
  72.2 39.3 %copy-start.5 = (bf16[1,128,2048]{2,1,0:T(8,128)(2,1)S(1)}, bf16[1,128,2048]{2,1,0:T(8,128)(2,1)}, u32[]{:S(2)}) copy-start(bf16[1,128,2048]{2,1,0:T(8,128)(2,1)} %param.16) | copy-start | bytes 1572868
  73.2 38.4 %all-to-all-start.1 = ((bf16[256,16,128]{2,1,0:T(8,128)(2,1)}), bf16[256,16,128]{2,1,0:T(8,128)(2,1)S(1)}, u32[]{:S(2)}, u32[]{:S(2)}) async-start(bf16[256,16,128]{2,1,0:T(8,128)(2,1)} %bitcast.21), calls=%async_computation.1 | async-start | bytes 2097152 | tf_op jit(solution)/shard_map/all_to_all | solution.py:516
  79.8 1.0 copy-start.12
  80.7 1.0 copy-start.18
  111.6 1.9 %copy-start.3 = (f32[3,128,2048]{2,1,0:T(8,128)S(1)}, f32[3,128,2048]{2,1,0:T(8,128)}, u32[]{:S(2)}) copy-start(f32[3,128,2048]{2,1,0:T(8,128)} %copy-done.2) | copy-start | bytes 9437188
  113.5 19.7 %copy-start.8 = (bf16[8,8192]{1,0:T(8,128)(2,1)S(1)}, bf16[8,8192]{1,0:T(8,128)(2,1)}, u32[]{:S(2)}) copy-start(bf16[8,8192]{1,0:T(8,128)(2,1)} %copy-done.7) | copy-start | bytes 393220
  118.5 1.2 collective-permute-start.2
  119.7 3.8 %collective-permute-start.3 = (f32[8,768]{1,0:T(8,128)S(1)}, f32[8,768]{1,0:T(8,128)S(1)}, u32[]{:S(2)}, u32[]{:S(2)}) collective-permute-start(f32[8,768]{1,0:T(8,128)S(1)} %add.24), channel_id=1, source_target_pairs={{0,2},{1,3},{2,0},{3,1},{4,6},{5,7},{6,4},{7,5},{8,10},{9,11},{10,... | collective-permute-start | bytes 73736 | tf_op jit(solution)/shard_map/ppermute | solution.py:446
  119.9 18.1 %collective-permute-start.1 = (bf16[8,6144]{1,0:T(8,128)(2,1)S(1)}, bf16[8,6144]{1,0:T(8,128)(2,1)S(1)}, u32[]{:S(2)}, u32[]{:S(2)}) collective-permute-start(bf16[8,6144]{1,0:T(8,128)(2,1)S(1)} %get-tuple-element.38), channel_id=1, source_target_pairs={{1,0},{2,1},{3,2},{4,3},{5,4},{6,5},{7,6},{8,7},{9,8},{10,9},{11,1... | collective-permute-start | bytes 294920 | tf_op jit(solution)/shard_map/ppermute | solution.py:442
  123.5 5.3 %collective-permute-start.4 = (f32[8,768]{1,0:T(8,128)S(1)}, f32[8,768]{1,0:T(8,128)S(1)}, u32[]{:S(2)}, u32[]{:S(2)}) collective-permute-start(f32[8,768]{1,0:T(8,128)S(1)} %add.25), channel_id=1, source_target_pairs={{0,4},{1,5},{2,6},{3,7},{4,0},{5,1},{6,2},{7,3},{8,12},{9,13},{10,... | collective-permute-start | bytes 73736 | tf_op jit(solution)/shard_map/ppermute | solution.py:446
  128.8 3.8 %collective-permute-start.5 = (f32[8,768]{1,0:T(8,128)S(1)}, f32[8,768]{1,0:T(8,128)S(1)}, u32[]{:S(2)}, u32[]{:S(2)}) collective-permute-start(f32[8,768]{1,0:T(8,128)S(1)} %add.26), channel_id=1, source_target_pairs={{0,8},{1,9},{2,10},{3,11},{4,12},{5,13},{6,14},{7,15},{8,0},{9,1},... | collective-permute-start | bytes 73736 | tf_op jit(solution)/shard_map/ppermute | solution.py:446
  132.7 5.3 %collective-permute-start.6 = (f32[8,768]{1,0:T(8,128)S(1)}, f32[8,768]{1,0:T(8,128)S(1)}, u32[]{:S(2)}, u32[]{:S(2)}) collective-permute-start(f32[8,768]{1,0:T(8,128)S(1)} %add.27), channel_id=1, source_target_pairs={{0,16},{1,17},{2,18},{3,19},{4,20},{5,21},{6,22},{7,23},{8,24},{9,... | collective-permute-start | bytes 73736 | tf_op jit(solution)/shard_map/ppermute | solution.py:446
  133.1 17.7 %collective-permute-start.10 = (bf16[8,8192]{1,0:T(8,128)(2,1)S(1)}, bf16[8,8192]{1,0:T(8,128)(2,1)S(1)}, u32[]{:S(2)}, u32[]{:S(2)}) collective-permute-start(bf16[8,8192]{1,0:T(8,128)(2,1)S(1)} %copy-done.8), channel_id=1, source_target_pairs={{0,192},{64,128},{128,64},{192,0},{1,193},{65,129},{129,65},{193,1... | collective-permute-start | bytes 393224 | tf_op jit(solution)/shard_map/ppermute | solution.py:446
  134.3 16.5 %collective-permute-start.8 = (bf16[8,8192]{1,0:T(8,128)(2,1)S(1)}, bf16[8,8192]{1,0:T(8,128)(2,1)S(1)}, u32[]{:S(2)}, u32[]{:S(2)}) collective-permute-start(bf16[8,8192]{1,0:T(8,128)(2,1)S(1)} %copy-done.8), channel_id=1, source_target_pairs={{0,64},{64,0},{128,192},{192,128},{1,65},{65,1},{129,193},{193,129... | collective-permute-start | bytes 393224 | tf_op jit(solution)/shard_map/ppermute | solution.py:446
  135.2 15.7 %collective-permute-start.9 = (bf16[8,8192]{1,0:T(8,128)(2,1)S(1)}, bf16[8,8192]{1,0:T(8,128)(2,1)S(1)}, u32[]{:S(2)}, u32[]{:S(2)}) collective-permute-start(bf16[8,8192]{1,0:T(8,128)(2,1)S(1)} %copy-done.8), channel_id=1, source_target_pairs={{0,128},{64,192},{128,0},{192,64},{1,129},{65,193},{129,1},{193,65... | collective-permute-start | bytes 393224 | tf_op jit(solution)/shard_map/ppermute | solution.py:446
  138.0 8.9 %collective-permute-start.7 = (f32[8,768]{1,0:T(8,128)S(1)}, f32[8,768]{1,0:T(8,128)S(1)}, u32[]{:S(2)}, u32[]{:S(2)}) collective-permute-start(f32[8,768]{1,0:T(8,128)S(1)} %add.28), channel_id=1, source_target_pairs={{0,32},{1,33},{2,34},{3,35},{4,36},{5,37},{6,38},{7,39},{8,40},{9,... | collective-permute-start | bytes 73736 | tf_op jit(solution)/shard_map/ppermute | solution.py:446
  146.9 3.9 %collective-permute-start.11 = (f32[8,768]{1,0:T(8,128)S(1)}, f32[8,768]{1,0:T(8,128)S(1)}, u32[]{:S(2)}, u32[]{:S(2)}) collective-permute-start(f32[8,768]{1,0:T(8,128)S(1)} %add.29), channel_id=1, source_target_pairs={{0,64},{64,0},{128,192},{192,128},{1,65},{65,1},{129,193},{193,129... | collective-permute-start | bytes 73736 | tf_op jit(solution)/shard_map/ppermute | solution.py:446
  150.9 4.8 %collective-permute-start.12 = (f32[8,768]{1,0:T(8,128)S(1)}, f32[8,768]{1,0:T(8,128)S(1)}, u32[]{:S(2)}, u32[]{:S(2)}) collective-permute-start(f32[8,768]{1,0:T(8,128)S(1)} %add.30), channel_id=1, source_target_pairs={{0,128},{64,192},{128,0},{192,64},{1,129},{65,193},{129,1},{193,65... | collective-permute-start | bytes 73736 | tf_op jit(solution)/shard_map/ppermute | solution.py:446
  (2 other events, 1.4 us)

commit v4 on v3

--- a/solution.py
+++ b/solution.py
@@ -17,6 +17,7 @@
 HALO = 8
 ROT = -0.25
 GRANT = 16 * 1024 * 1024
+FIRST_GRANT = 16 * 1024 * 1024
 BLOCK = 512
 
 
@@ -58,7 +59,7 @@
 def to_spectra(signals, first, twist, ahead):
     rows, cols = signals[0].shape
     wide = jnp.concatenate(signals, axis=1).astype(BF16)
-    mixed = mxu(first, twice(wide, 0))
+    mixed = mxu(first[:, :rows], wide)
     twist_real, twist_imag = twist[:, :cols], twist[:, cols:]
     turned = []
     for at in range(len(signals)):
@@ -70,13 +71,13 @@
             )
         )
     turned = jnp.concatenate(turned, axis=0).astype(BF16)
-    return mxu(twice(turned, 1), ahead)
+    return mxu(turned, ahead[: 2 * cols])
 
 
 def from_spectra(spectra, last, twist, back):
     rows, cols = spectra[0].shape[0], spectra[0].shape[1] // 2
     tall = jnp.concatenate(spectra, axis=0).astype(BF16)
-    mixed = mxu(twice(tall, 1), back)
+    mixed = mxu(tall, back[: 2 * cols])
     twist_real, twist_imag = twist[:, :cols], twist[:, cols:]
     turned = []
     for at in range(len(spectra)):
@@ -88,7 +89,7 @@
             )
         )
     turned = jnp.concatenate(turned, axis=1).astype(BF16)
-    return mxu(last, twice(turned, 0))
+    return mxu(last[:, : 2 * rows], turned)
 
 
 def times(left, right, flip):
@@ -138,6 +139,7 @@
 def mix_kernel(
     seqs,
     rows,
+    scale,
     place_ref,
     got_ref,
     taps_ref,
@@ -147,10 +149,11 @@
     ahead_ref,
     back_ref,
     out_ref,
-    corr_ref,
+    grad_ref,
     spread,
     gather,
     filt_ref,
+    corr_ref,
 ):
     pair = 2 * OWN
     filter_spectra(
@@ -199,18 +202,16 @@
             .reshape(rows, pair, LANES)
             .astype(BF16)
         )
-
-
-def taps_kernel(rows, scale, corr_ref, last_ref, twist_ref, back_ref, out_ref, gather):
-    last, twist, back = last_ref[...], twist_ref[...], back_ref[...]
     for half in range(2):
-        result = from_spectra([corr_ref[half * 4 + at] for at in range(4)], last, twist, back)
+        result = from_spectra([corr_ref[half * 4 + at] for at in range(4)], last, twist, back_ref[...])
         for at in range(4):
-            gather[pl.ds(half * 4 + at, rows, stride=OWN), :] = (
+            spread[pl.ds(half * 4 + at, rows, stride=OWN), :] = (
                 result[:, at * LANES : (at + 1) * LANES] * scale
             )
     for row in range(rows):
-        out_ref[:, row * LANES : (row + 1) * LANES] = gather[row * OWN : (row + 1) * OWN, :].astype(BF16)
+        grad_ref[:, row * LANES : (row + 1) * LANES] = spread[row * OWN : (row + 1) * OWN, :].astype(
+            BF16
+        )
 
 
 def join_kernel(place_ref, own_ref, one_ref, two_ref, three_ref, out_ref):
@@ -260,26 +261,49 @@
 
 
 def short_kernel(
-    group_size, width, q_ref, k_ref, v_ref, cot_ref, taps_ref, feats_ref, out_ref, wide_ref, padded
+    group_size,
+    taps_hbm,
+    qkv_hbm,
+    cot_hbm,
+    feats_ref,
+    out_ref,
+    wide_ref,
+    taps_ref,
+    qkv_ref,
+    cot_ref,
+    padded,
+    sems,
 ):
-    step = pl.program_id(0)
-    rows, block = q_ref.shape
-
-    @pl.when(step == 0)
-    def _():
-        spread_taps(taps_ref, group_size, wide_ref)
-        padded[0:HALO, :] = jnp.zeros((HALO, 3 * block), F32)
-
-    for part, ref in enumerate((q_ref, k_ref, v_ref)):
-        padded[HALO : HALO + rows, part * block : (part + 1) * block] = ref[...].astype(F32)
+    rows, width_all = qkv_ref.shape
+    width = width_all // 3
+    steps = width // BLOCK
+    copies = [(taps_hbm, taps_ref)]
+    for step in range(steps):
+        for part in range(3):
+            cols = pl.ds(part * width + step * BLOCK, BLOCK)
+            copies.append((qkv_hbm.at[:, cols], qkv_ref.at[:, cols]))
+        cols = pl.ds(step * BLOCK, BLOCK)
+        copies.append((cot_hbm.at[:, cols], cot_ref.at[:, cols]))
+    copies = [
+        pltpu.make_async_copy(source, target, sems.at[at]) for at, (source, target) in enumerate(copies)
+    ]
+    for copy in copies:
+        copy.start()
+    copies[0].wait()
+    spread_taps(taps_ref, group_size, wide_ref)
+    padded[0:HALO, :] = jnp.zeros((HALO, width_all), F32)
     per_chunk = LANES // OWN // 4
-    for at in range(block // LANES):
+    per_step = BLOCK // LANES
+    for at in range(width // LANES):
+        if at % per_step == 0:
+            for copy in copies[at // per_step * 4 + 1 : at // per_step * 4 + 5]:
+                copy.wait()
         here = slice(at * LANES, (at + 1) * LANES)
         parts = []
         for part in range(3):
-            lanes = pl.ds(pl.multiple_of(part * width + step * block + at * LANES, LANES), LANES)
-            cols = slice(part * block + at * LANES, part * block + (at + 1) * LANES)
-            total = short_rows(padded, lambda lag: wide_ref[lag : lag + 1, lanes], cols, 0, rows)
+            cols = slice(part * width + at * LANES, part * width + (at + 1) * LANES)
+            padded[HALO : HALO + rows, cols] = qkv_ref[:, cols].astype(F32)
+            total = short_rows(padded, lambda lag: wide_ref[lag : lag + 1, cols], cols, 0, rows)
             feats_ref[part, :, here] = total
             parts.append(total)
         tiles = owner_tiles((parts[1] * parts[2]).T, (cot_ref[:, here].astype(F32) * parts[0]).T)
@@ -418,7 +442,7 @@
     return pl.CostEstimate(flops=int(flops), bytes_accessed=int(moved), transcendentals=0)
 
 
-def grid_call(kernel, steps, outs, out_specs, scratch, args, in_specs, cost, aliases=None):
+def grid_call(kernel, steps, outs, out_specs, scratch, args, in_specs, cost, limit, aliases=None):
     return pl.pallas_call(
         kernel,
         grid=(steps,),
@@ -427,7 +451,7 @@
         out_specs=out_specs,
         scratch_shapes=scratch,
         input_output_aliases=aliases or {},
-        compiler_params=pltpu.CompilerParams(vmem_limit_bytes=GRANT),
+        compiler_params=pltpu.CompilerParams(vmem_limit_bytes=limit),
         cost_estimate=estimate(*cost),
     )(*args)
 
@@ -443,7 +467,8 @@
 
 
 def partner(array, axis, mask):
-    return lax.ppermute(array, axis, [(i, i ^ mask) for i in range(lax.axis_size(axis))])
+    devices = lax.axis_size(axis)
+    return lax.ppermute(array, axis, [(i, i ^ mask) for i in range(devices)])
 
 
 def shards(qkv, short_filter, long_filter, cotangent):
@@ -459,26 +484,26 @@
     place = lax.axis_index("dp").astype(jnp.int32).reshape(1)
     left_rim = neighbours(feats_in[rows - HALO :], 1)
     pair = (seqs, ctx_count, 2 * OWN, rows)
-    block = BLOCK
-    steps = width // block
-    owners = block // OWN // seqs
-    lanes = [
-        pl.BlockSpec((rows, block), lambda i, part=part: (0, part * steps + i)) for part in range(3)
-    ]
-    triple = pl.BlockSpec((3, rows, block), lambda i: (0, 0, i))
-    tiles = pl.BlockSpec((seqs, owners, 2 * OWN, rows), lambda i: (0, i, 0, 0))
-    padded = pltpu.VMEM((rows + HALO, 3 * block), F32)
+    vmem = pl.BlockSpec(memory_space=pltpu.VMEM)
     whole = lambda *dims: pl.BlockSpec(dims, lambda i: (0,) * len(dims))
     feats_shape = shape((3, rows, width), F32)
+    hbm = pl.BlockSpec(memory_space=pltpu.HBM)
     feats, sent, wide_taps = grid_call(
-        functools.partial(short_kernel, group_size, width),
-        steps,
+        functools.partial(short_kernel, group_size),
+        1,
         (feats_shape, shape(pair, BF16), shape((8, width_all), F32)),
-        (triple, tiles, whole(8, width_all)),
-        [padded],
-        (feats_in, feats_in, feats_in, cot, short_filter),
-        [*lanes, lanes[0], whole(tap_count, groups)],
+        (vmem, vmem, vmem),
+        [
+            pltpu.VMEM((tap_count, groups), F32),
+            pltpu.VMEM((rows, width_all), BF16),
+            pltpu.VMEM((rows, width), BF16),
+            pltpu.VMEM((rows + HALO, width_all), F32),
+            pltpu.SemaphoreType.DMA((4 * width // BLOCK + 1,)),
+        ],
+        [pltpu.with_memory_space_constraint(arg, pltpu.HBM) for arg in (short_filter, feats_in, cot)],
+        [hbm, hbm, hbm],
         (1e9, 6e6),
+        FIRST_GRANT,
     )
     top = pl.BlockSpec((2 * HALO, width_all), lambda i: (0, 0))
     rows_top = pl.BlockSpec((3, HALO, width), lambda i: (0, 0, 0))
@@ -498,17 +523,19 @@
             whole(*pair),
         ],
         (1e8, 2e6),
+        GRANT,
         {4: 0, 5: 1},
     )
+    sent, place = lax.optimization_barrier((sent, place))
     got = lax.all_to_all(
         sent.reshape(seqs * ctx_count, 2 * OWN, rows), ("dp", "ctx"), 0, 0, tiled=True
     ).reshape(pair)
     long_rows = pltpu.VMEM((seqs * ctx_count * 2 * OWN, rows), F32)
     spectra = (OWN, ctx_count, 2 * rows)
-    mixed, corr = call(
-        functools.partial(mix_kernel, seqs, ctx_count),
-        (shape(pair, BF16), shape(spectra, F32)),
-        [long_rows, long_rows, pltpu.VMEM(spectra, F32)],
+    mixed, own_taps = call(
+        functools.partial(mix_kernel, seqs, ctx_count, scale),
+        (shape(pair, BF16), shape((OWN, length), BF16)),
+        [long_rows, long_rows, pltpu.VMEM(spectra, F32), pltpu.VMEM(spectra, F32)],
         (place, got, long_filter, first, last, twist, ahead, back),
         (8e9, 6e6),
         1,
@@ -516,14 +543,6 @@
     returned = lax.all_to_all(
         mixed.reshape(seqs * ctx_count, 2 * OWN, rows), ("dp", "ctx"), 0, 0, tiled=True
     ).reshape(pair)
-    own_taps = call(
-        functools.partial(taps_kernel, ctx_count, scale),
-        shape((OWN, length), BF16),
-        [pltpu.VMEM((ctx_count * OWN, rows), F32)],
-        (corr, last, twist, back),
-        (1e9, 1e6),
-    )
-    returned, own_taps = lax.optimization_barrier((returned, own_taps))
     mixer_out, gso, edge, short_part = call(
         functools.partial(gate_kernel, group_size, scale),
         (
@@ -537,12 +556,10 @@
         (1e9, 9e6),
     )
     right_rim = neighbours(edge, -1)
-    masks = [
-        (axis, 1 << bit)
-        for axis in ("ctx", "dp")
-        for bit in range((lax.axis_size(axis) - 1).bit_length())
-    ]
-    for at, (axis, mask) in enumerate(masks):
+    far = ctx_count // 2
+    hops = [("ctx", 1), ("ctx", 2), ("ctx", 6), ("ctx", 8), ("ctx", 24)]
+    hops += [(("dp", "ctx"), (seqs - 1) * ctx_count + far), ("dp", 1), ("dp", 2)]
+    for at, (axis, mask) in enumerate(hops):
         if at == 2:
             own_taps, short_part = lax.optimization_barrier((own_taps, short_part))
             others = [partner(own_taps, "dp", step) for step in (1, 2, 3)]

time: 158 us -> 144 us (0.911)
  blocking collectives: 0 us -> 85.7 us
  waiting for transfers between devices: 73.8 us -> 12.9 us
  starting transfers between devices: 42 us -> 18.7 us
  local copies, waits for them, and re-layouts: 12 us -> 1.09 us
  Pallas kernels: 27 us -> 22.2 us
    all_to_all x0 -> x2, blocking collectives: none -> 85.7 us  [the longest x1 47.6 us: shards(): lax.all_to_all(sent.reshape(seqs * ctx_count, 2 * OWN, rows), ('dp', 'ctx...]
    all_to_all x2 -> x0, waiting for transfers between devices: 60 us -> none  [the longest x1 31.7 us: shards(): lax.all_to_all(sent.reshape(seqs * ctx_count, 2 * OWN, rows), ('dp', 'ctx...]
    all_to_all x2 -> x0, starting transfers between devices: 22.1 us -> none  [the longest x1 15.5 us: shards(): lax.all_to_all(sent.reshape(seqs * ctx_count, 2 * OWN, rows), ('dp', 'ctx...]
    unnamed x38 -> x16, local copies, waits for them, and re-layouts: 11.1 us -> 0.05 us
    pallas_call x5 -> x4, Pallas kernels: 18.9 us -> 16.3 us  [call(): pl.pallas_call(kernel, out_shape=outs, in_specs=[smem] * scalars + [vmem]...]
    pallas_call x2, Pallas kernels: 8.14 us -> 5.92 us  [grid_call(): pl.pallas_call(kernel, grid=(steps,), out_shape=outs, in_specs=in_specs,...]
    ppermute x11, waiting for transfers between devices: 13.7 us -> 11.9 us  [partner(): return lax.ppermute(array, axis, [(i, i ^ mask) for i in range(devices)])]
  transfers between devices with their start and end apart: 15 -> 13, of which waited for: 9 -> 7; matrix products, arithmetic and copies ran while one was open for 0% -> 0% of each run, Pallas kernels for 7% -> 7%
where the time goes in v4:
time: 144 us; the launch traced here: 142 us
  blocking collectives  85.7 us (60%)
  Pallas kernels  22.2 us (15%)
  starting transfers between devices  18.7 us (13%)
  waiting for transfers between devices  12.9 us (9%)
    all_to_all x1, blocking collectives, shards(): lax.all_to_all(sent.reshape(seqs * ctx_count, 2 * OWN, rows), ('dp', 'ctx...  47.6 us
    all_to_all x1, blocking collectives, shards(): lax.all_to_all(mixed.reshape(seqs * ctx_count, 2 * OWN, rows), ('dp', 'ct...  38.1 us
    pallas_call x4, Pallas kernels, call(): pl.pallas_call(kernel, out_shape=outs, in_specs=[smem] * scalars + [vmem]...  16.3 us
    ppermute x11, starting transfers between devices, partner(): return lax.ppermute(array, axis, [(i, i ^ mask) for i in range(devices)])  13.6 us
    ppermute x11, waiting for transfers between devices, partner(): return lax.ppermute(array, axis, [(i, i ^ mask) for i in range(devices)])  11.9 us
    pallas_call x2, Pallas kernels, grid_call(): pl.pallas_call(kernel, grid=(steps,), out_shape=outs, in_specs=in_specs,...  5.92 us
    ppermute x2, starting transfers between devices, neighbours(): return lax.ppermute(array, 'ctx', pairs)  5.15 us
  transfers between devices with their start and end apart: 13, of which 7 were waited for; matrix products, arithmetic and copies ran while one was open for 0% of the time, Pallas kernels for 7%

profile of v4, /device:TPU:8, one launch (start us, length us, event | category | flops | bytes accessed | tf_op | source)
XLA Modules:
  0.0 142.1 jit_solution(5554354626109691844)
XLA Ops:
  0.6 0.0 copy-start
  0.7 1.0 slice_bitcast_fusion
  1.7 1.9 %collective-permute-start = (bf16[8,6144]{1,0:T(8,128)(2,1)S(1)}, bf16[8,6144]{1,0:T(8,128)(2,1)S(1)}, u32[]{:S(2)}, u32[]{:S(2)}) collective-permute-start(bf16[8,6144]{1,0:T(8,128)(2,1)S(1)} %slice_bitcast_fusion), channel_id=1, source_target_pairs={{0,1},{1,2},{2,3},{3,4},{4,5},{5,6},{6,7},{7,8},{8,9},{9,10},{10,1... | collective-permute-start | bytes 294920 | tf_op jit(solution)/shard_map/ppermute | solution.py:466
  3.6 5.1 %shard_map.156 = (f32[3,128,2048]{2,1,0:T(8,128)S(1)}, bf16[4,64,16,128]{3,2,1,0:T(8,128)(2,1)S(1)}, f32[8,6144]{1,0:T(8,128)S(1)}) custom-call(f32[7,768]{1,0:T(8,128)} %taps_hbm.1, bf16[128,6144]{1,0:T(8,128)(2,1)} %bitcast.11, bf16[128,2048]{1,0:T(8,128)(2,1)} %bitcast.16), custom_call_target="tpu_custom_call" | custom-call | flops 1000000000 | bytes 6000000 | tf_op jit(solution)/shard_map/pallas_call | solution.py:446
  8.8 1.0 collective-permute-done.rim_ref
  9.8 0.0 copy-start.4
  9.8 0.8 shard_map.157
  10.6 47.6 %all_to_all.10 = bf16[256,16,128]{2,1,0:T(8,128)(2,1)S(1)} all-to-all(bf16[256,16,128]{2,1,0:T(8,128)(2,1)S(1)} %bitcast.14), channel_id=1, replica_groups=mesh['dp'=4,'ctx'=64] {'dp','ctx'}, dimensions={0} | all-to-all | bytes 2097152 | tf_op jit(solution)/shard_map/all_to_all | solution.py:530
  58.3 5.9 %shard_map.158 = (bf16[4,64,16,128]{3,2,1,0:T(8,128)(2,1)S(1)}, bf16[8,8192]{1,0:T(8,128)(2,1)S(1)}) custom-call(s32[1]{0:T(128)} %bitcast.3.place_ref, bf16[4,64,16,128]{3,2,1,0:T(8,128)(2,1)S(1)} %bitcast.19, f32[32,8192]{1,0:T(8,128)S(1)} %copy-done.2, bf16[128,128]{1,0:T(8,128)(2,1)S(1)} %copy-done.6, bf16[64,256]{1,0:T(8,128)(2,1)S(1)} %copy-done.7, ...), custom_call_target="tpu_custom_call" | custom-call | flops 8000000000 | bytes 6000000 | tf_op jit(solution)/shard_map/pallas_call | solution.py:430
  64.2 38.1 %all_to_all.11 = bf16[256,16,128]{2,1,0:T(8,128)(2,1)S(1)} all-to-all(bf16[256,16,128]{2,1,0:T(8,128)(2,1)S(1)} %bitcast.20), channel_id=1, replica_groups=mesh['dp'=4,'ctx'=64] {'dp','ctx'}, dimensions={0} | all-to-all | bytes 2097152 | tf_op jit(solution)/shard_map/all_to_all | solution.py:543
  102.3 5.0 %shard_map.159 = (bf16[128,2048]{1,0:T(8,128)(2,1)}, f32[128,6144]{1,0:T(8,128)S(1)}, bf16[8,6144]{1,0:T(8,128)(2,1)S(1)}, f32[8,768]{1,0:T(8,128)S(1)}) custom-call(bf16[4,64,16,128]{3,2,1,0:T(8,128)(2,1)S(1)} %bitcast.15, f32[3,128,2048]{2,1,0:T(8,128)S(1)} %get-tuple-element.35.feats_ref, bf16[128,2048]{1,0:T(8,128)(2,1)S(1)} %bitcast.18, ...), custom_call_target="tpu_custom_call" | custom-call | flops 1000000000 | bytes 9000000 | tf_op jit(solution)/shard_map/pallas_call | solution.py:430
  107.2 0.0 collective-permute-start.2
  107.3 1.2 collective-permute-done.2
  108.5 0.2 collective-permute-start.3
  108.7 3.2 %collective-permute-start.1 = (bf16[8,6144]{1,0:T(8,128)(2,1)S(1)}, bf16[8,6144]{1,0:T(8,128)(2,1)S(1)}, u32[]{:S(2)}, u32[]{:S(2)}) collective-permute-start(bf16[8,6144]{1,0:T(8,128)(2,1)S(1)} %get-tuple-element.38), channel_id=1, source_target_pairs={{1,0},{2,1},{3,2},{4,3},{5,4},{6,5},{7,6},{8,7},{9,8},{10,9},{11,1... | collective-permute-start | bytes 294920 | tf_op jit(solution)/shard_map/ppermute | solution.py:466
  111.9 0.4 collective-permute-done.3
  112.3 0.2 collective-permute-start.4
  112.5 4.8 %collective-permute-done.4 = f32[8,768]{1,0:T(8,128)S(1)} collective-permute-done((f32[8,768]{1,0:T(8,128)S(1)}, f32[8,768]{1,0:T(8,128)S(1)}, u32[]{:S(2)}, u32[]{:S(2)}) %collective-permute-start.4) | collective-permute-done | bytes 24608 | tf_op jit(solution)/shard_map/ppermute | solution.py:471
  117.3 1.4 collective-permute-start.5
  118.7 2.5 %collective-permute-done.5 = f32[8,768]{1,0:T(8,128)S(1)} collective-permute-done((f32[8,768]{1,0:T(8,128)S(1)}, f32[8,768]{1,0:T(8,128)S(1)}, u32[]{:S(2)}, u32[]{:S(2)}) %collective-permute-start.5) | collective-permute-done | bytes 24608 | tf_op jit(solution)/shard_map/ppermute | solution.py:471
  121.2 0.3 collective-permute-start.6
  121.4 1.1 collective-permute-start.10
  122.5 0.2 collective-permute-start.8
  122.7 3.1 %collective-permute-start.9 = (bf16[8,8192]{1,0:T(8,128)(2,1)S(1)}, bf16[8,8192]{1,0:T(8,128)(2,1)S(1)}, u32[]{:S(2)}, u32[]{:S(2)}) collective-permute-start(bf16[8,8192]{1,0:T(8,128)(2,1)S(1)} %get-tuple-element.46.own_ref), channel_id=1, source_target_pairs={{0,128},{64,192},{128,0},{192,64},{1,129},{65,193},{129,1},{193,65... | collective-permute-start | bytes 393224 | tf_op jit(solution)/shard_map/ppermute | solution.py:471
  125.8 2.3 %collective-permute-start.7 = (f32[8,768]{1,0:T(8,128)S(1)}, f32[8,768]{1,0:T(8,128)S(1)}, u32[]{:S(2)}, u32[]{:S(2)}) collective-permute-start(f32[8,768]{1,0:T(8,128)S(1)} %add.28), channel_id=1, source_target_pairs={{0,224},{1,225},{2,226},{3,227},{4,228},{5,229},{6,230},{7,231},{8... | collective-permute-start | bytes 73736 | tf_op jit(solution)/shard_map/ppermute | solution.py:471
  128.2 4.4 %shard_map.160 = bf16[128,6144]{1,0:T(8,128)(2,1)} custom-call(f32[128,6144]{1,0:T(8,128)S(1)} %get-tuple-element.42.gso_ref, bf16[8,6144]{1,0:T(8,128)(2,1)S(1)} %collective-permute-done.1.rim_ref, f32[8,6144]{1,0:T(8,128)S(1)} %get-tuple-element.28.wide_ref), custom_call_target="tpu_custom_call" | custom-call | flops 1000000000 | bytes 6000000 | tf_op jit(solution)/shard_map/pallas_call | solution.py:430
  132.6 2.3 %collective-permute-start.11 = (f32[8,768]{1,0:T(8,128)S(1)}, f32[8,768]{1,0:T(8,128)S(1)}, u32[]{:S(2)}, u32[]{:S(2)}) collective-permute-start(f32[8,768]{1,0:T(8,128)S(1)} %add.29), channel_id=1, source_target_pairs={{0,64},{64,0},{128,192},{192,128},{1,65},{65,1},{129,193},{193,129... | collective-permute-start | bytes 73736 | tf_op jit(solution)/shard_map/ppermute | solution.py:471
  134.8 1.8 %collective-permute-done.11 = f32[8,768]{1,0:T(8,128)S(1)} collective-permute-done((f32[8,768]{1,0:T(8,128)S(1)}, f32[8,768]{1,0:T(8,128)S(1)}, u32[]{:S(2)}, u32[]{:S(2)}) %collective-permute-start.11) | collective-permute-done | bytes 24608 | tf_op jit(solution)/shard_map/ppermute | solution.py:471
  136.6 2.5 %collective-permute-start.12 = (f32[8,768]{1,0:T(8,128)S(1)}, f32[8,768]{1,0:T(8,128)S(1)}, u32[]{:S(2)}, u32[]{:S(2)}) collective-permute-start(f32[8,768]{1,0:T(8,128)S(1)} %add.30), channel_id=1, source_target_pairs={{0,128},{64,192},{128,0},{192,64},{1,129},{65,193},{129,1},{193,65... | collective-permute-start | bytes 73736 | tf_op jit(solution)/shard_map/ppermute | solution.py:471
  139.2 1.0 shard_map.161
  140.2 1.2 collective-permute-done.12
  141.5 0.6 slice_add_fusion
  (27 shorter events, 0.1 us)
Async XLA Ops:
  0.6 9.1 %copy-start = (bf16[1,128,6144]{2,1,0:T(8,128)(2,1)S(1)}, bf16[1,128,6144]{2,1,0:T(8,128)(2,1)}, u32[]{:S(2)}) copy-start(bf16[1,128,6144]{2,1,0:T(8,128)(2,1)} %param.13) | copy-start | bytes 4718596
  0.6 9.1 %copy-start.1 = (bf16[1,128,2048]{2,1,0:T(8,128)(2,1)S(1)}, bf16[1,128,2048]{2,1,0:T(8,128)(2,1)}, u32[]{:S(2)}) copy-start(bf16[1,128,2048]{2,1,0:T(8,128)(2,1)} %param.16) | copy-start | bytes 1572868
  1.7 8.0 %collective-permute-start = (bf16[8,6144]{1,0:T(8,128)(2,1)S(1)}, bf16[8,6144]{1,0:T(8,128)(2,1)S(1)}, u32[]{:S(2)}, u32[]{:S(2)}) collective-permute-start(bf16[8,6144]{1,0:T(8,128)(2,1)S(1)} %slice_bitcast_fusion), channel_id=1, source_target_pairs={{0,1},{1,2},{2,3},{3,4},{4,5},{5,6},{6,7},{7,8},{8,9},{9,10},{10,1... | collective-permute-start | bytes 294920 | tf_op jit(solution)/shard_map/ppermute | solution.py:466
  9.7 48.5 %copy-start.2 = (f32[32,8192]{1,0:T(8,128)S(1)}, f32[32,8192]{1,0:T(8,128)}, u32[]{:S(2)}) copy-start(f32[32,8192]{1,0:T(8,128)} %taps_ref.1) | copy-start | bytes 3145732
  9.7 48.5 %copy-start.3 = (bf16[512,256]{1,0:T(8,128)(2,1)S(1)}, bf16[512,256]{1,0:T(8,128)(2,1)}, u32[]{:S(2)}) copy-start(bf16[512,256]{1,0:T(8,128)(2,1)} %constant.38.ahead_ref) | copy-start | bytes 786436
  9.8 48.5 %copy-start.4 = (bf16[512,256]{1,0:T(8,128)(2,1)S(1)}, bf16[512,256]{1,0:T(8,128)(2,1)}, u32[]{:S(2)}) copy-start(bf16[512,256]{1,0:T(8,128)(2,1)} %constant.43.back_ref) | copy-start | bytes 786436
  9.8 48.5 %copy-start.5 = (f32[64,256]{1,0:T(8,128)S(1)}, f32[64,256]{1,0:T(8,128)}, u32[]{:S(2)}) copy-start(f32[64,256]{1,0:T(8,128)} %constant.20.clone.twist_ref) | copy-start | bytes 196612
  9.8 48.5 %copy-start.6 = (bf16[128,128]{1,0:T(8,128)(2,1)S(1)}, bf16[128,128]{1,0:T(8,128)(2,1)}, u32[]{:S(2)}) copy-start(bf16[128,128]{1,0:T(8,128)(2,1)} %constant.28.first_ref) | copy-start | bytes 98308
  9.8 48.5 %copy-start.7 = (bf16[64,256]{1,0:T(8,128)(2,1)S(1)}, bf16[64,256]{1,0:T(8,128)(2,1)}, u32[]{:S(2)}) copy-start(bf16[64,256]{1,0:T(8,128)(2,1)} %constant.33.last_ref) | copy-start | bytes 98308
  107.2 1.2 collective-permute-start.2
  108.5 3.8 %collective-permute-start.3 = (f32[8,768]{1,0:T(8,128)S(1)}, f32[8,768]{1,0:T(8,128)S(1)}, u32[]{:S(2)}, u32[]{:S(2)}) collective-permute-start(f32[8,768]{1,0:T(8,128)S(1)} %add.24), channel_id=1, source_target_pairs={{0,2},{1,3},{2,0},{3,1},{4,6},{5,7},{6,4},{7,5},{8,10},{9,11},{10,... | collective-permute-start | bytes 73736 | tf_op jit(solution)/shard_map/ppermute | solution.py:471
  108.7 17.2 %collective-permute-start.1 = (bf16[8,6144]{1,0:T(8,128)(2,1)S(1)}, bf16[8,6144]{1,0:T(8,128)(2,1)S(1)}, u32[]{:S(2)}, u32[]{:S(2)}) collective-permute-start(bf16[8,6144]{1,0:T(8,128)(2,1)S(1)} %get-tuple-element.38), channel_id=1, source_target_pairs={{1,0},{2,1},{3,2},{4,3},{5,4},{6,5},{7,6},{8,7},{9,8},{10,9},{11,1... | collective-permute-start | bytes 294920 | tf_op jit(solution)/shard_map/ppermute | solution.py:466
  112.3 5.0 %collective-permute-start.4 = (f32[8,768]{1,0:T(8,128)S(1)}, f32[8,768]{1,0:T(8,128)S(1)}, u32[]{:S(2)}, u32[]{:S(2)}) collective-permute-start(f32[8,768]{1,0:T(8,128)S(1)} %add.25), channel_id=1, source_target_pairs={{0,6},{1,7},{2,4},{3,5},{4,2},{5,3},{6,0},{7,1},{8,14},{9,15},{10,... | collective-permute-start | bytes 73736 | tf_op jit(solution)/shard_map/ppermute | solution.py:471
  117.3 3.8 %collective-permute-start.5 = (f32[8,768]{1,0:T(8,128)S(1)}, f32[8,768]{1,0:T(8,128)S(1)}, u32[]{:S(2)}, u32[]{:S(2)}) collective-permute-start(f32[8,768]{1,0:T(8,128)S(1)} %add.26), channel_id=1, source_target_pairs={{0,8},{1,9},{2,10},{3,11},{4,12},{5,13},{6,14},{7,15},{8,0},{9,1},... | collective-permute-start | bytes 73736 | tf_op jit(solution)/shard_map/ppermute | solution.py:471
  121.2 4.7 %collective-permute-start.6 = (f32[8,768]{1,0:T(8,128)S(1)}, f32[8,768]{1,0:T(8,128)S(1)}, u32[]{:S(2)}, u32[]{:S(2)}) collective-permute-start(f32[8,768]{1,0:T(8,128)S(1)} %add.27), channel_id=1, source_target_pairs={{0,24},{1,25},{2,26},{3,27},{4,28},{5,29},{6,30},{7,31},{8,16},{9,... | collective-permute-start | bytes 73736 | tf_op jit(solution)/shard_map/ppermute | solution.py:471
  121.4 15.2 %collective-permute-start.10 = (bf16[8,8192]{1,0:T(8,128)(2,1)S(1)}, bf16[8,8192]{1,0:T(8,128)(2,1)S(1)}, u32[]{:S(2)}, u32[]{:S(2)}) collective-permute-start(bf16[8,8192]{1,0:T(8,128)(2,1)S(1)} %get-tuple-element.46.own_ref), channel_id=1, source_target_pairs={{0,192},{64,128},{128,64},{192,0},{1,193},{65,129},{129,65},{193,1... | collective-permute-start | bytes 393224 | tf_op jit(solution)/shard_map/ppermute | solution.py:471
  122.5 14.1 %collective-permute-start.8 = (bf16[8,8192]{1,0:T(8,128)(2,1)S(1)}, bf16[8,8192]{1,0:T(8,128)(2,1)S(1)}, u32[]{:S(2)}, u32[]{:S(2)}) collective-permute-start(bf16[8,8192]{1,0:T(8,128)(2,1)S(1)} %get-tuple-element.46.own_ref), channel_id=1, source_target_pairs={{0,64},{64,0},{128,192},{192,128},{1,65},{65,1},{129,193},{193,129... | collective-permute-start | bytes 393224 | tf_op jit(solution)/shard_map/ppermute | solution.py:471
  122.7 13.9 %collective-permute-start.9 = (bf16[8,8192]{1,0:T(8,128)(2,1)S(1)}, bf16[8,8192]{1,0:T(8,128)(2,1)S(1)}, u32[]{:S(2)}, u32[]{:S(2)}) collective-permute-start(bf16[8,8192]{1,0:T(8,128)(2,1)S(1)} %get-tuple-element.46.own_ref), channel_id=1, source_target_pairs={{0,128},{64,192},{128,0},{192,64},{1,129},{65,193},{129,1},{193,65... | collective-permute-start | bytes 393224 | tf_op jit(solution)/shard_map/ppermute | solution.py:471
  125.8 6.7 %collective-permute-start.7 = (f32[8,768]{1,0:T(8,128)S(1)}, f32[8,768]{1,0:T(8,128)S(1)}, u32[]{:S(2)}, u32[]{:S(2)}) collective-permute-start(f32[8,768]{1,0:T(8,128)S(1)} %add.28), channel_id=1, source_target_pairs={{0,224},{1,225},{2,226},{3,227},{4,228},{5,229},{6,230},{7,231},{8... | collective-permute-start | bytes 73736 | tf_op jit(solution)/shard_map/ppermute | solution.py:471
  132.6 4.1 %collective-permute-start.11 = (f32[8,768]{1,0:T(8,128)S(1)}, f32[8,768]{1,0:T(8,128)S(1)}, u32[]{:S(2)}, u32[]{:S(2)}) collective-permute-start(f32[8,768]{1,0:T(8,128)S(1)} %add.29), channel_id=1, source_target_pairs={{0,64},{64,0},{128,192},{192,128},{1,65},{65,1},{129,193},{193,129... | collective-permute-start | bytes 73736 | tf_op jit(solution)/shard_map/ppermute | solution.py:471
  136.6 4.8 %collective-permute-start.12 = (f32[8,768]{1,0:T(8,128)S(1)}, f32[8,768]{1,0:T(8,128)S(1)}, u32[]{:S(2)}, u32[]{:S(2)}) collective-permute-start(f32[8,768]{1,0:T(8,128)S(1)} %add.30), channel_id=1, source_target_pairs={{0,128},{64,192},{128,0},{192,64},{1,129},{65,193},{129,1},{193,65... | collective-permute-start | bytes 73736 | tf_op jit(solution)/shard_map/ppermute | solution.py:471

commit v5 on v4

--- a/solution.py
+++ b/solution.py
@@ -18,13 +18,18 @@
 ROT = -0.25
 GRANT = 16 * 1024 * 1024
 FIRST_GRANT = 16 * 1024 * 1024
-BLOCK = 512
+BLOCK = 1024
 
 
 def two_parts(table):
     high = jnp.asarray(table, F32).astype(BF16)
     low = (jnp.asarray(table, F32) - high.astype(F32)).astype(BF16)
     return high, low
+
+
+def phase_order(rows):
+    place = np.arange(rows)
+    return (place % 8) * (rows // 8) + place // 8
 
 
 def make_tables(rows, cols):
@@ -36,16 +41,17 @@
     last = np.concatenate([np.cos(turn.T), -np.sin(turn.T)], axis=1) / total
     n2 = np.arange(cols, dtype=np.float64)
     twist = 2.0 * np.pi * k1 * n2[None, :] / total
-    twist = np.concatenate([np.cos(twist), -np.sin(twist)], axis=1)
     inner = 2.0 * np.pi * ((n2[:, None] * n2[None, :]) % cols) / cols
     real, imag = np.cos(inner), -np.sin(inner)
-    ahead = np.block([[real, imag], [-imag, real]])
+    order = phase_order(cols)
+    high, low = two_parts(np.block([[real, imag], [-imag, real]]))
     back = np.block([[real, -imag], [imag, real]])
-    first = jnp.concatenate(two_parts(first), axis=1)
-    last = jnp.concatenate(two_parts(last), axis=1)
-    ahead = jnp.concatenate(two_parts(ahead), axis=0)
-    back = jnp.concatenate(two_parts(back), axis=0)
-    return first, last, jnp.asarray(twist, F32), ahead, back
+    ahead_phases = np.block([[real[order], imag[order]], [-imag[order], real[order]]])
+    back_phases = np.block([[real[:, order], -imag[:, order]], [imag[:, order], real[:, order]]])
+    outer = jnp.concatenate([jnp.concatenate(two_parts(first), axis=1), two_parts(last)[0]], axis=0)
+    inner = [high, low] + [two_parts(table)[0] for table in (back, ahead_phases, back_phases)]
+    twists = [np.cos(twist), -np.sin(twist), np.cos(twist[:, order]), -np.sin(twist[:, order])]
+    return outer, jnp.concatenate(inner, axis=0), jnp.asarray(np.concatenate(twists, axis=1), F32)
 
 
 def mxu(left, right):
@@ -59,7 +65,7 @@
 def to_spectra(signals, first, twist, ahead):
     rows, cols = signals[0].shape
     wide = jnp.concatenate(signals, axis=1).astype(BF16)
-    mixed = mxu(first[:, :rows], wide)
+    mixed = mxu(first, wide)
     twist_real, twist_imag = twist[:, :cols], twist[:, cols:]
     turned = []
     for at in range(len(signals)):
@@ -71,13 +77,13 @@
             )
         )
     turned = jnp.concatenate(turned, axis=0).astype(BF16)
-    return mxu(turned, ahead[: 2 * cols])
+    return mxu(turned, ahead)
 
 
 def from_spectra(spectra, last, twist, back):
     rows, cols = spectra[0].shape[0], spectra[0].shape[1] // 2
     tall = jnp.concatenate(spectra, axis=0).astype(BF16)
-    mixed = mxu(tall, back[: 2 * cols])
+    mixed = mxu(tall, back)
     twist_real, twist_imag = twist[:, :cols], twist[:, cols:]
     turned = []
     for at in range(len(spectra)):
@@ -89,7 +95,7 @@
             )
         )
     turned = jnp.concatenate(turned, axis=1).astype(BF16)
-    return mxu(last[:, : 2 * rows], turned)
+    return mxu(last, turned)
 
 
 def times(left, right, flip):
@@ -143,11 +149,9 @@
     place_ref,
     got_ref,
     taps_ref,
-    first_ref,
-    last_ref,
+    outer_ref,
+    inner_ref,
     twist_ref,
-    ahead_ref,
-    back_ref,
     out_ref,
     grad_ref,
     spread,
@@ -156,13 +160,14 @@
     corr_ref,
 ):
     pair = 2 * OWN
+    side = 2 * LANES
     filter_spectra(
         rows,
         pl.multiple_of(place_ref[0] * OWN, OWN),
         taps_ref,
-        first_ref[...],
-        twist_ref[...],
-        ahead_ref[...],
+        outer_ref[: 2 * rows],
+        twist_ref[:, :side],
+        inner_ref[: 2 * side],
         filt_ref,
         gather,
     )
@@ -170,14 +175,17 @@
         spread[seq * rows * pair : (seq + 1) * rows * pair, :] = (
             got_ref[seq].astype(F32).reshape(rows * pair, LANES)
         )
-    first, last, twist = first_ref[...], last_ref[...], twist_ref[...]
+    first, last = outer_ref[: 2 * rows, :rows], outer_ref[2 * rows :]
+    back = inner_ref[2 * side : 3 * side]
+    ahead_phases, back_phases = inner_ref[3 * side : 4 * side], inner_ref[4 * side :]
+    twist, twist_phases = twist_ref[:, :side], twist_ref[:, side:]
     for chan in range(OWN):
         signals = [
             spread[pl.ds(seq * rows * pair + part * OWN + chan, rows, stride=pair), :]
             for part in range(2)
             for seq in range(seqs)
         ]
-        spectra = to_spectra(signals, first, twist, ahead_ref[...])
+        spectra = to_spectra(signals, first, twist_phases, ahead_phases)
         filt = filt_ref[chan]
         ahead_specs, back_specs, total = [], [], None
         for seq in range(seqs):
@@ -188,7 +196,7 @@
             term = times(grad, prod, True)
             total = term if total is None else total + term
         corr_ref[chan] = total
-        result = from_spectra(ahead_specs + back_specs, last, twist, back_ref[...])
+        result = from_spectra(ahead_specs + back_specs, last, twist_phases, back_phases)
         at = 0
         for part in range(2):
             for seq in range(seqs):
@@ -203,7 +211,7 @@
             .astype(BF16)
         )
     for half in range(2):
-        result = from_spectra([corr_ref[half * 4 + at] for at in range(4)], last, twist, back_ref[...])
+        result = from_spectra([corr_ref[half * 4 + at] for at in range(4)], last, twist, back)
         for at in range(4):
             spread[pl.ds(half * 4 + at, rows, stride=OWN), :] = (
                 result[:, at * LANES : (at + 1) * LANES] * scale
@@ -247,12 +255,18 @@
         wide[:, at * LANES * group_size : (at + 1) * LANES * group_size] = spread[at * 8 : (at + 1) * 8]
 
 
-def short_rows(padded, wide, cols, first_row, rows):
-    start = first_row + HALO
-    total = wide(0) * padded[start : start + rows, cols]
-    for lag in range(1, TAPS):
-        total = total + wide(lag) * padded[start - lag : start - lag + rows, cols]
-    return total
+def phased(stage, first, count):
+    reach = (stage.shape[0] - HALO) // 8
+    return jnp.concatenate(
+        [stage[pl.ds(HALO + first + at, 8, stride=reach), :] for at in range(count)], axis=0
+    )
+
+
+def unphased(stage, array):
+    reach = array.shape[0] // 8
+    for at in range(reach):
+        stage[pl.ds(at, 8, stride=reach), :] = array[at * 8 : (at + 1) * 8]
+    return stage[...]
 
 
 def owner_tiles(product, grad_in):
@@ -271,7 +285,7 @@
     taps_ref,
     qkv_ref,
     cot_ref,
-    padded,
+    stages,
     sems,
 ):
     rows, width_all = qkv_ref.shape
@@ -291,43 +305,59 @@
         copy.start()
     copies[0].wait()
     spread_taps(taps_ref, group_size, wide_ref)
-    padded[0:HALO, :] = jnp.zeros((HALO, width_all), F32)
+    for at in range(8):
+        stages[at, 0:HALO, :] = jnp.zeros((HALO, LANES), F32)
     per_chunk = LANES // OWN // 4
     per_step = BLOCK // LANES
     for at in range(width // LANES):
         if at % per_step == 0:
             for copy in copies[at // per_step * 4 + 1 : at // per_step * 4 + 5]:
                 copy.wait()
-        here = slice(at * LANES, (at + 1) * LANES)
+        parts = []
+        for part in range(3):
+            stage = stages.at[at % 2 * 4 + part]
+            cols = slice(part * width + at * LANES, part * width + (at + 1) * LANES)
+            stage[HALO:, :] = qkv_ref[:, cols].astype(F32)
+            shifted = phased(stage, 1 - TAPS, rows // 8 + TAPS - 1)
+            total = wide_ref[0:1, cols] * shifted[(TAPS - 1) * 8 :]
+            for lag in range(1, TAPS):
+                start = (TAPS - 1 - lag) * 8
+                total = total + wide_ref[lag : lag + 1, cols] * shifted[start : start + rows]
+            feats_ref[part * (width // LANES) + at] = total
+            parts.append(total)
+        stage = stages.at[at % 2 * 4 + 3]
+        stage[HALO:, :] = cot_ref[:, at * LANES : (at + 1) * LANES].astype(F32)
+        cot = phased(stage, 0, rows // 8)
+        tiles = owner_tiles((parts[1] * parts[2]).T, (cot * parts[0]).T)
+        for seq in range(4):
+            out_ref[seq, at * per_chunk : (at + 1) * per_chunk] = tiles[:, seq]
+
+
+def rim_kernel(
+    width, top_ref, rim_ref, cot_ref, wide_ref, feats_in, sent_in, feats_ref, out_ref, padded, first_rows
+):
+    padded[0:HALO, :] = rim_ref[...].astype(F32)
+    padded[HALO : 2 * HALO, :] = top_ref[...].astype(F32)[:HALO]
+    per_chunk = LANES // OWN // 4
+    chunks = width // LANES
+    lane = lax.broadcasted_iota(jnp.int32, (per_chunk, 2 * OWN, LANES), 2)
+    fresh = (lane % 8 == 0) & (lane < 8 * HALO)
+    fresh_rows = lax.broadcasted_iota(jnp.int32, (8 * HALO, LANES), 0) % 8 == 0
+    for at in range(chunks):
         parts = []
         for part in range(3):
             cols = slice(part * width + at * LANES, part * width + (at + 1) * LANES)
-            padded[HALO : HALO + rows, cols] = qkv_ref[:, cols].astype(F32)
-            total = short_rows(padded, lambda lag: wide_ref[lag : lag + 1, cols], cols, 0, rows)
-            feats_ref[part, :, here] = total
-            parts.append(total)
-        tiles = owner_tiles((parts[1] * parts[2]).T, (cot_ref[:, here].astype(F32) * parts[0]).T)
-        for seq in range(4):
-            out_ref[seq, at * per_chunk : (at + 1) * per_chunk] = tiles[:, seq]
-
-
-def rim_kernel(width, top_ref, rim_ref, cot_ref, wide_ref, feats_in, sent_in, feats_ref, out_ref, padded):
-    padded[0:HALO, :] = rim_ref[...].astype(F32)
-    padded[HALO : 2 * HALO, :] = top_ref[...].astype(F32)[:HALO]
-    per_chunk = LANES // OWN // 4
-    fresh = lax.broadcasted_iota(jnp.int32, (per_chunk, 2 * OWN, LANES), 2) < HALO
-    blank = jnp.zeros((LANES - HALO, LANES), F32)
-    for at in range(width // LANES):
-        parts = []
-        for part in range(3):
-            cols = slice(part * width + at * LANES, part * width + (at + 1) * LANES)
-            total = short_rows(padded, lambda lag: wide_ref[lag : lag + 1, cols], cols, 0, HALO)
-            feats_ref[part, :, at * LANES : (at + 1) * LANES] = total
+            total = wide_ref[0:1, cols] * padded[HALO : 2 * HALO, cols]
+            for lag in range(1, TAPS):
+                total = total + wide_ref[lag : lag + 1, cols] * padded[HALO - lag : 2 * HALO - lag, cols]
             parts.append(total)
         cot = cot_ref[:, at * LANES : (at + 1) * LANES].astype(F32)[:HALO]
-        product = jnp.concatenate([parts[1] * parts[2], blank], axis=0).T
-        grad_in = jnp.concatenate([cot * parts[0], blank], axis=0).T
-        tiles = owner_tiles(product, grad_in)
+        for index, array in enumerate(parts + [parts[1] * parts[2], cot * parts[0]]):
+            first_rows[index, pl.ds(0, HALO, stride=8), :] = array
+        for part in range(3):
+            chunk = part * chunks + at
+            feats_ref[chunk] = jnp.where(fresh_rows, first_rows[part, : 8 * HALO], feats_in[chunk])
+        tiles = owner_tiles(first_rows[3].T, first_rows[4].T)
         here = slice(at * per_chunk, (at + 1) * per_chunk)
         for seq in range(4):
             out_ref[seq, here] = jnp.where(fresh, tiles[:, seq], sent_in[seq, here])
@@ -341,18 +371,19 @@
     cot_ref,
     qkv_ref,
     rim_ref,
-    mixer_ref,
+    mixer_hbm,
     gso_ref,
     edge_ref,
     short_ref,
-    padded,
+    mixer_ref,
+    stages,
     sums,
+    sems,
 ):
     rows, width_all = qkv_ref.shape
     width = width_all // 3
-    padded[0:HALO, :] = rim_ref[...].astype(F32)
-    padded[HALO : HALO + rows, :] = qkv_ref[...].astype(F32)
     per_chunk = LANES // OWN // 4
+    chunks = width // LANES
 
     def chunk(at, _):
         here = pl.ds(pl.multiple_of(at * LANES, LANES), LANES)
@@ -362,24 +393,34 @@
         both = both.reshape(LANES // OWN, 2 * OWN, LANES)
         long_out = both[:, :OWN].reshape(LANES, LANES).T
         grad_product = both[:, OWN:].reshape(LANES, LANES).T
-        mixer_ref[:, here] = (feats_ref[0, :, here] * long_out).astype(BF16)
+        stages[3, HALO:, :] = cot_ref[:, here].astype(F32)
+        mixed = feats_ref[at] * long_out
+        mixer_ref[:, here] = unphased(stages.at[4, pl.ds(0, rows)], mixed).astype(BF16)
         grads = (
-            cot_ref[:, here].astype(F32) * long_out,
-            grad_product * feats_ref[2, :, here],
-            grad_product * feats_ref[1, :, here],
+            phased(stages.at[3], 0, rows // 8) * long_out,
+            grad_product * feats_ref[2 * chunks + at],
+            grad_product * feats_ref[chunks + at],
         )
         for part in range(3):
             cols = pl.ds(pl.multiple_of(part * width + at * LANES, LANES), LANES)
-            gso_ref[:, cols] = grads[part]
-            edge_ref[:, cols] = grads[part][:HALO].astype(BF16)
+            stages[part, 0:HALO, :] = rim_ref[:, cols].astype(F32)
+            stages[part, HALO:, :] = qkv_ref[:, cols].astype(F32)
+            shifted = phased(stages.at[part], 1 - TAPS, rows // 8 + TAPS - 1)
+            gso_ref[part * chunks + at] = grads[part]
+            edge_ref[:, cols] = gso_ref[part * chunks + at, pl.ds(0, HALO, stride=8), :].astype(BF16)
             for lag in range(TAPS):
-                term = grads[part] * padded[HALO - lag : HALO - lag + rows, cols]
+                start = (TAPS - 1 - lag) * 8
+                term = grads[part] * shifted[start : start + rows]
                 sums[lag * 8 : (lag + 1) * 8, cols] = jnp.sum(
                     term.reshape(rows // 8, 8, LANES), axis=0
                 )
         return 0
 
-    lax.fori_loop(0, width // LANES, chunk, 0)
+    per_copy = BLOCK // LANES
+    copies = []
+    for at in range(width // BLOCK):
+        lax.fori_loop(at * per_copy, (at + 1) * per_copy, chunk, 0)
+        copies.append(copy_out(mixer_ref, mixer_hbm, at, sems))
     span = LANES * group_size
     blocks = width_all // span
     lags = []
@@ -403,39 +444,60 @@
     total = total[:count] + (total[count : 2 * count] + total[2 * count :])
     for at in range(blocks):
         short_ref[:, at * LANES : (at + 1) * LANES] = total[at * 8 : (at + 1) * 8] * scale
-
-
-def back_kernel(gso_ref, rim_ref, wide_ref, out_ref, tail):
-    rows, width_all = gso_ref.shape
-    body = rows - HALO
-    tail[0:HALO, :] = gso_ref[body:rows, :]
-    tail[HALO : 2 * HALO, :] = rim_ref[...].astype(F32)
+    for copy in copies:
+        copy.wait()
+
+
+def copy_out(source, target, at, sems):
+    cols = pl.ds(at * BLOCK, BLOCK)
+    copy = pltpu.make_async_copy(source.at[:, cols], target.at[:, cols], sems.at[at])
+    copy.start()
+    return copy
+
+
+def back_kernel(gso_ref, rim_ref, wide_ref, out_hbm, out_ref, last_rows, stage, sems):
+    chunks, rows, _ = gso_ref.shape
+    more = (TAPS - 1) * 8
+    end = lax.broadcasted_iota(jnp.int32, (more, LANES), 0) % 8 == 7
 
     def chunk(at, _):
         cols = pl.ds(pl.multiple_of(at * LANES, LANES), LANES)
-        total = wide_ref[0:1, cols] * gso_ref[0:body, cols]
-        end = wide_ref[0:1, cols] * tail[0:HALO, cols]
+        last_rows[pl.ds(7, HALO, stride=8), :] = rim_ref[:, cols].astype(F32)
+        here = gso_ref[at]
+        after = jnp.where(end, last_rows[:more], gso_ref[at, 1 : more + 1])
+        shifted = jnp.concatenate([here, after], axis=0)
+        total = wide_ref[0:1, cols] * here
         for lag in range(1, TAPS):
-            total = total + wide_ref[lag : lag + 1, cols] * gso_ref[lag : lag + body, cols]
-            end = end + wide_ref[lag : lag + 1, cols] * tail[lag : lag + HALO, cols]
-        out_ref[:, cols] = jnp.concatenate([total, end], axis=0).astype(BF16)
+            total = total + wide_ref[lag : lag + 1, cols] * shifted[lag * 8 : lag * 8 + rows]
+        out_ref[:, cols] = unphased(stage, total).astype(BF16)
         return 0
 
-    lax.fori_loop(0, width_all // LANES, chunk, 0)
-
-
-def call(kernel, outs, scratch, args, cost, scalars=0):
+    per_copy = BLOCK // LANES
+    copies = []
+    for at in range(chunks // per_copy):
+        lax.fori_loop(at * per_copy, (at + 1) * per_copy, chunk, 0, unroll=2)
+        copies.append(copy_out(out_ref, out_hbm, at, sems))
+    for copy in copies:
+        copy.wait()
+
+
+def call(kernel, outs, scratch, args, cost, scalars=0, hbm_outs=()):
     vmem = pl.BlockSpec(memory_space=pltpu.VMEM)
+    hbm = pl.BlockSpec(memory_space=pltpu.HBM)
+    single = not isinstance(outs, tuple)
+    outs = (outs,) if single else outs
+    out_specs = tuple(hbm if at in hbm_outs else vmem for at in range(len(outs)))
     smem = pl.BlockSpec(memory_space=pltpu.SMEM)
-    return pl.pallas_call(
+    results = pl.pallas_call(
         kernel,
         out_shape=outs,
         in_specs=[smem] * scalars + [vmem] * (len(args) - scalars),
-        out_specs=jax.tree.map(lambda _: vmem, outs),
+        out_specs=out_specs,
         scratch_shapes=scratch,
         compiler_params=pltpu.CompilerParams(vmem_limit_bytes=GRANT),
         cost_estimate=estimate(*cost),
     )(*args)
+    return results[0] if single else results
 
 
 def estimate(flops, moved):
@@ -480,13 +542,15 @@
     seqs, ctx_count = lax.axis_size("dp"), lax.axis_size("ctx")
     length = ctx_count * rows
     scale = 1.0 / math.sqrt(seqs * length)
-    first, last, twist, ahead, back = make_tables(ctx_count, rows)
+    tables = make_tables(ctx_count, rows)
     place = lax.axis_index("dp").astype(jnp.int32).reshape(1)
     left_rim = neighbours(feats_in[rows - HALO :], 1)
     pair = (seqs, ctx_count, 2 * OWN, rows)
     vmem = pl.BlockSpec(memory_space=pltpu.VMEM)
     whole = lambda *dims: pl.BlockSpec(dims, lambda i: (0,) * len(dims))
-    feats_shape = shape((3, rows, width), F32)
+    chunks = width_all // LANES
+    feats_shape = shape((chunks, rows, LANES), F32)
+    stages = lambda count: pltpu.VMEM((count, rows + HALO, LANES), F32)
     hbm = pl.BlockSpec(memory_space=pltpu.HBM)
     feats, sent, wide_taps = grid_call(
         functools.partial(short_kernel, group_size),
@@ -497,7 +561,7 @@
             pltpu.VMEM((tap_count, groups), F32),
             pltpu.VMEM((rows, width_all), BF16),
             pltpu.VMEM((rows, width), BF16),
-            pltpu.VMEM((rows + HALO, width_all), F32),
+            stages(8),
             pltpu.SemaphoreType.DMA((4 * width // BLOCK + 1,)),
         ],
         [pltpu.with_memory_space_constraint(arg, pltpu.HBM) for arg in (short_filter, feats_in, cot)],
@@ -506,13 +570,13 @@
         FIRST_GRANT,
     )
     top = pl.BlockSpec((2 * HALO, width_all), lambda i: (0, 0))
-    rows_top = pl.BlockSpec((3, HALO, width), lambda i: (0, 0, 0))
+    rows_top = pl.BlockSpec((chunks, 8 * HALO, LANES), lambda i: (0, 0, 0))
     feats, sent = grid_call(
         functools.partial(rim_kernel, width),
         1,
         (feats_shape, shape(pair, BF16)),
         (rows_top, whole(*pair)),
-        [pltpu.VMEM((2 * HALO, width_all), F32)],
+        [pltpu.VMEM((2 * HALO, width_all), F32), pltpu.VMEM((5, rows, LANES), F32)],
         (feats_in, left_rim, cot, wide_taps, feats, sent),
         [
             top,
@@ -536,7 +600,7 @@
         functools.partial(mix_kernel, seqs, ctx_count, scale),
         (shape(pair, BF16), shape((OWN, length), BF16)),
         [long_rows, long_rows, pltpu.VMEM(spectra, F32), pltpu.VMEM(spectra, F32)],
-        (place, got, long_filter, first, last, twist, ahead, back),
+        (place, got, long_filter, *tables),
         (8e9, 6e6),
         1,
     )
@@ -547,13 +611,19 @@
         functools.partial(gate_kernel, group_size, scale),
         (
             shape((rows, width), BF16),
-            shape((rows, width_all), F32),
+            feats_shape,
             shape((HALO, width_all), BF16),
             shape((8, groups), F32),
         ),
-        [pltpu.VMEM((rows + HALO, width_all), F32), pltpu.VMEM((tap_count * 8, width_all), F32)],
+        [
+            pltpu.VMEM((rows, width), BF16),
+            stages(5),
+            pltpu.VMEM((tap_count * 8, width_all), F32),
+            pltpu.SemaphoreType.DMA((width // BLOCK,)),
+        ],
         (returned, feats, cot, feats_in, left_rim),
         (1e9, 9e6),
+        hbm_outs=(0,),
     )
     right_rim = neighbours(edge, -1)
     far = ctx_count // 2
@@ -568,9 +638,15 @@
             grad_rows = call(
                 back_kernel,
                 shape((rows, width_all), BF16),
-                [pltpu.VMEM((2 * HALO, width_all), F32)],
+                [
+                    pltpu.VMEM((rows, width_all), BF16),
+                    pltpu.VMEM((8 * HALO, LANES), F32),
+                    pltpu.VMEM((rows, LANES), F32),
+                    pltpu.SemaphoreType.DMA((width_all // BLOCK,)),
+                ],
                 (gso, right_rim, wide_taps),
                 (1e9, 6e6),
+                hbm_outs=(0,),
             )
         if at == 7:
             others, short_part = lax.optimization_barrier((others, short_part))

time: 144 us -> 144 us (level)
  transfers between devices with their start and end apart: 13 -> 13, of which waited for: 7 -> 7; matrix products, arithmetic and copies ran while one was open for 0% -> 0% of each run, Pallas kernels for 7% -> 6%
where the time goes in v5:
time: 144 us; the launch traced here: 142 us
  blocking collectives  85.7 us (60%)
  Pallas kernels  21 us (15%)
  starting transfers between devices  19.7 us (14%)
  waiting for transfers between devices  13.4 us (9%)
    all_to_all x1, blocking collectives, shards(): lax.all_to_all(sent.reshape(seqs * ctx_count, 2 * OWN, rows), ('dp', 'ctx...  47.6 us
    all_to_all x1, blocking collectives, shards(): lax.all_to_all(mixed.reshape(seqs * ctx_count, 2 * OWN, rows), ('dp', 'ct...  38.1 us
    pallas_call x4, Pallas kernels, call(): pl.pallas_call(kernel, out_shape=outs, in_specs=[smem] * scalars + [vmem]...  15 us
    ppermute x11, starting transfers between devices, partner(): return lax.ppermute(array, axis, [(i, i ^ mask) for i in range(devices)])  14.5 us
    ppermute x11, waiting for transfers between devices, partner(): return lax.ppermute(array, axis, [(i, i ^ mask) for i in range(devices)])  11.9 us
    pallas_call x2, Pallas kernels, grid_call(): pl.pallas_call(kernel, grid=(steps,), out_shape=outs, in_specs=in_specs,...  5.94 us
    ppermute x2, starting transfers between devices, neighbours(): return lax.ppermute(array, 'ctx', pairs)  5.15 us
  transfers between devices with their start and end apart: 13, of which 7 were waited for; matrix products, arithmetic and copies ran while one was open for 0% of the time, Pallas kernels for 6%

profile of v5, /device:TPU:8, one launch (start us, length us, event | category | flops | bytes accessed | tf_op | source)
XLA Modules:
  0.0 142.3 jit_solution(17919771925680607194)
XLA Ops:
  0.7 1.0 slice_bitcast_fusion
  1.7 1.9 %collective-permute-start = (bf16[8,6144]{1,0:T(8,128)(2,1)S(1)}, bf16[8,6144]{1,0:T(8,128)(2,1)S(1)}, u32[]{:S(2)}, u32[]{:S(2)}) collective-permute-start(bf16[8,6144]{1,0:T(8,128)(2,1)S(1)} %slice_bitcast_fusion), channel_id=1, source_target_pairs={{0,1},{1,2},{2,3},{3,4},{4,5},{5,6},{6,7},{7,8},{8,9},{9,10},{10,1... | collective-permute-start | bytes 294920 | tf_op jit(solution)/shard_map/ppermute | solution.py:528
  3.6 4.6 %shard_map.156 = (f32[48,128,128]{2,1,0:T(8,128)S(1)}, bf16[4,64,16,128]{3,2,1,0:T(8,128)(2,1)S(1)}, f32[8,6144]{1,0:T(8,128)S(1)}) custom-call(f32[7,768]{1,0:T(8,128)} %taps_hbm.1, bf16[128,6144]{1,0:T(8,128)(2,1)} %bitcast.11, bf16[128,2048]{1,0:T(8,128)(2,1)} %bitcast.16), custom_call_target="tpu_custom_call" | custom-call | flops 1000000000 | bytes 6000000 | tf_op jit(solution)/shard_map/pallas_call | solution.py:508
  8.3 1.5 %collective-permute-done.rim_ref = bf16[8,6144]{1,0:T(8,128)(2,1)S(1)} collective-permute-done((bf16[8,6144]{1,0:T(8,128)(2,1)S(1)}, bf16[8,6144]{1,0:T(8,128)(2,1)S(1)}, u32[]{:S(2)}, u32[]{:S(2)}) %collective-permute-start) | collective-permute-done | bytes 98336 | tf_op jit(solution)/shard_map/ppermute | solution.py:528
  9.8 0.0 copy-start.4
  9.8 0.0 copy-start.5
  9.8 1.3 shard_map.157
  11.1 47.6 %all_to_all.10 = bf16[256,16,128]{2,1,0:T(8,128)(2,1)S(1)} all-to-all(bf16[256,16,128]{2,1,0:T(8,128)(2,1)S(1)} %bitcast.14), channel_id=1, replica_groups=mesh['dp'=4,'ctx'=64] {'dp','ctx'}, dimensions={0} | all-to-all | bytes 2097152 | tf_op jit(solution)/shard_map/all_to_all | solution.py:594
  58.8 5.9 %shard_map.158 = (bf16[4,64,16,128]{3,2,1,0:T(8,128)(2,1)S(1)}, bf16[8,8192]{1,0:T(8,128)(2,1)S(1)}) custom-call(s32[1]{0:T(128)} %bitcast.3.place_ref, bf16[4,64,16,128]{3,2,1,0:T(8,128)(2,1)S(1)} %bitcast.19, f32[32,8192]{1,0:T(8,128)S(1)} %copy-done.2, bf16[192,128]{1,0:T(8,128)(2,1)S(1)} %copy-done.5, bf16[1280,256]{1,0:T(8,128)(2,1)S(1)} %copy-done.3, ...), custom_call_target="tpu_custom_call" | custom-call | flops 8000000000 | bytes 6000000 | tf_op jit(solution)/shard_map/pallas_call | solution.py:491
  64.7 38.1 %all_to_all.11 = bf16[256,16,128]{2,1,0:T(8,128)(2,1)S(1)} all-to-all(bf16[256,16,128]{2,1,0:T(8,128)(2,1)S(1)} %bitcast.20), channel_id=1, replica_groups=mesh['dp'=4,'ctx'=64] {'dp','ctx'}, dimensions={0} | all-to-all | bytes 2097152 | tf_op jit(solution)/shard_map/all_to_all | solution.py:607
  102.8 4.6 %shard_map.159 = (bf16[128,2048]{1,0:T(8,128)(2,1)}, f32[48,128,128]{2,1,0:T(8,128)S(1)}, bf16[8,6144]{1,0:T(8,128)(2,1)S(1)}, f32[8,768]{1,0:T(8,128)S(1)}) custom-call(bf16[4,64,16,128]{3,2,1,0:T(8,128)(2,1)S(1)} %bitcast.15, f32[48,128,128]{2,1,0:T(8,128)S(1)} %get-tuple-element.35.feats_ref, bf16[128,2048]{1,0:T(8,128)(2,1)S(1)} %bitcast.18, ...), custom_call_target="tpu_custom_call" | custom-call | flops 1000000000 | bytes 9000000 | tf_op jit(solution)/shard_map/pallas_call | solution.py:491
  107.4 0.1 collective-permute-start.2
  107.5 1.2 collective-permute-done.2
  108.6 0.2 collective-permute-start.3
  108.8 3.2 %collective-permute-start.1 = (bf16[8,6144]{1,0:T(8,128)(2,1)S(1)}, bf16[8,6144]{1,0:T(8,128)(2,1)S(1)}, u32[]{:S(2)}, u32[]{:S(2)}) collective-permute-start(bf16[8,6144]{1,0:T(8,128)(2,1)S(1)} %get-tuple-element.38), channel_id=1, source_target_pairs={{1,0},{2,1},{3,2},{4,3},{5,4},{6,5},{7,6},{8,7},{9,8},{10,9},{11,1... | collective-permute-start | bytes 294920 | tf_op jit(solution)/shard_map/ppermute | solution.py:528
  112.1 0.4 collective-permute-done.3
  112.5 0.2 collective-permute-start.4
  112.7 4.8 %collective-permute-done.4 = f32[8,768]{1,0:T(8,128)S(1)} collective-permute-done((f32[8,768]{1,0:T(8,128)S(1)}, f32[8,768]{1,0:T(8,128)S(1)}, u32[]{:S(2)}, u32[]{:S(2)}) %collective-permute-start.4) | collective-permute-done | bytes 24608 | tf_op jit(solution)/shard_map/ppermute | solution.py:533
  117.5 1.4 collective-permute-start.5
  118.9 2.5 %collective-permute-done.5 = f32[8,768]{1,0:T(8,128)S(1)} collective-permute-done((f32[8,768]{1,0:T(8,128)S(1)}, f32[8,768]{1,0:T(8,128)S(1)}, u32[]{:S(2)}, u32[]{:S(2)}) %collective-permute-start.5) | collective-permute-done | bytes 24608 | tf_op jit(solution)/shard_map/ppermute | solution.py:533
  121.4 0.3 collective-permute-start.6
  121.6 1.1 collective-permute-start.10
  122.7 0.2 collective-permute-start.8
  122.9 3.1 %collective-permute-start.9 = (bf16[8,8192]{1,0:T(8,128)(2,1)S(1)}, bf16[8,8192]{1,0:T(8,128)(2,1)S(1)}, u32[]{:S(2)}, u32[]{:S(2)}) collective-permute-start(bf16[8,8192]{1,0:T(8,128)(2,1)S(1)} %get-tuple-element.46.own_ref), channel_id=1, source_target_pairs={{0,128},{64,192},{128,0},{192,64},{1,129},{65,193},{129,1},{193,65... | collective-permute-start | bytes 393224 | tf_op jit(solution)/shard_map/ppermute | solution.py:533
  126.0 2.3 %collective-permute-start.7 = (f32[8,768]{1,0:T(8,128)S(1)}, f32[8,768]{1,0:T(8,128)S(1)}, u32[]{:S(2)}, u32[]{:S(2)}) collective-permute-start(f32[8,768]{1,0:T(8,128)S(1)} %add.28), channel_id=1, source_target_pairs={{0,224},{1,225},{2,226},{3,227},{4,228},{5,229},{6,230},{7,231},{8... | collective-permute-start | bytes 73736 | tf_op jit(solution)/shard_map/ppermute | solution.py:533
  128.4 3.5 %shard_map.160 = bf16[128,6144]{1,0:T(8,128)(2,1)} custom-call(f32[48,128,128]{2,1,0:T(8,128)S(1)} %get-tuple-element.42.gso_ref, bf16[8,6144]{1,0:T(8,128)(2,1)S(1)} %collective-permute-done.1.rim_ref, f32[8,6144]{1,0:T(8,128)S(1)} %get-tuple-element.28.wide_ref), custom_call_target="tpu_custom_call" | custom-call | flops 1000000000 | bytes 6000000 | tf_op jit(solution)/shard_map/pallas_call | solution.py:491
  131.9 3.1 %collective-permute-start.11 = (f32[8,768]{1,0:T(8,128)S(1)}, f32[8,768]{1,0:T(8,128)S(1)}, u32[]{:S(2)}, u32[]{:S(2)}) collective-permute-start(f32[8,768]{1,0:T(8,128)S(1)} %add.29), channel_id=1, source_target_pairs={{0,64},{64,0},{128,192},{192,128},{1,65},{65,1},{129,193},{193,129... | collective-permute-start | bytes 73736 | tf_op jit(solution)/shard_map/ppermute | solution.py:533
  135.0 1.8 %collective-permute-done.11 = f32[8,768]{1,0:T(8,128)S(1)} collective-permute-done((f32[8,768]{1,0:T(8,128)S(1)}, f32[8,768]{1,0:T(8,128)S(1)}, u32[]{:S(2)}, u32[]{:S(2)}) %collective-permute-start.11) | collective-permute-done | bytes 24608 | tf_op jit(solution)/shard_map/ppermute | solution.py:533
  136.8 2.5 %collective-permute-start.12 = (f32[8,768]{1,0:T(8,128)S(1)}, f32[8,768]{1,0:T(8,128)S(1)}, u32[]{:S(2)}, u32[]{:S(2)}) collective-permute-start(f32[8,768]{1,0:T(8,128)S(1)} %add.30), channel_id=1, source_target_pairs={{0,128},{64,192},{128,0},{192,64},{1,129},{65,193},{129,1},{193,65... | collective-permute-start | bytes 73736 | tf_op jit(solution)/shard_map/ppermute | solution.py:533
  139.4 1.0 shard_map.161
  140.4 1.2 collective-permute-done.12
  141.7 0.6 slice_add_fusion
  (23 shorter events, 0.1 us)
Async XLA Ops:
  0.6 9.1 %copy-start = (bf16[1,128,6144]{2,1,0:T(8,128)(2,1)S(1)}, bf16[1,128,6144]{2,1,0:T(8,128)(2,1)}, u32[]{:S(2)}) copy-start(bf16[1,128,6144]{2,1,0:T(8,128)(2,1)} %param.13) | copy-start | bytes 4718596
  0.6 9.1 %copy-start.1 = (bf16[1,128,2048]{2,1,0:T(8,128)(2,1)S(1)}, bf16[1,128,2048]{2,1,0:T(8,128)(2,1)}, u32[]{:S(2)}) copy-start(bf16[1,128,2048]{2,1,0:T(8,128)(2,1)} %param.16) | copy-start | bytes 1572868
  1.7 8.0 %collective-permute-start = (bf16[8,6144]{1,0:T(8,128)(2,1)S(1)}, bf16[8,6144]{1,0:T(8,128)(2,1)S(1)}, u32[]{:S(2)}, u32[]{:S(2)}) collective-permute-start(bf16[8,6144]{1,0:T(8,128)(2,1)S(1)} %slice_bitcast_fusion), channel_id=1, source_target_pairs={{0,1},{1,2},{2,3},{3,4},{4,5},{5,6},{6,7},{7,8},{8,9},{9,10},{10,1... | collective-permute-start | bytes 294920 | tf_op jit(solution)/shard_map/ppermute | solution.py:528
  9.7 49.0 %copy-start.2 = (f32[32,8192]{1,0:T(8,128)S(1)}, f32[32,8192]{1,0:T(8,128)}, u32[]{:S(2)}) copy-start(f32[32,8192]{1,0:T(8,128)} %taps_ref.1) | copy-start | bytes 3145732
  9.7 49.0 %copy-start.3 = (bf16[1280,256]{1,0:T(8,128)(2,1)S(1)}, bf16[1280,256]{1,0:T(8,128)(2,1)}, u32[]{:S(2)}) copy-start(bf16[1280,256]{1,0:T(8,128)(2,1)} %constant.44.inner_ref) | copy-start | bytes 1966084
  9.8 49.0 %copy-start.4 = (f32[64,512]{1,0:T(8,128)S(1)}, f32[64,512]{1,0:T(8,128)}, u32[]{:S(2)}) copy-start(f32[64,512]{1,0:T(8,128)} %constant.26.clone.twist_ref) | copy-start | bytes 393220
  9.8 49.0 %copy-start.5 = (bf16[192,128]{1,0:T(8,128)(2,1)S(1)}, bf16[192,128]{1,0:T(8,128)(2,1)}, u32[]{:S(2)}) copy-start(bf16[192,128]{1,0:T(8,128)(2,1)} %constant.36.outer_ref) | copy-start | bytes 147460
  107.4 1.3 collective-permute-start.2
  108.6 3.8 %collective-permute-start.3 = (f32[8,768]{1,0:T(8,128)S(1)}, f32[8,768]{1,0:T(8,128)S(1)}, u32[]{:S(2)}, u32[]{:S(2)}) collective-permute-start(f32[8,768]{1,0:T(8,128)S(1)} %add.24), channel_id=1, source_target_pairs={{0,2},{1,3},{2,0},{3,1},{4,6},{5,7},{6,4},{7,5},{8,10},{9,11},{10,... | collective-permute-start | bytes 73736 | tf_op jit(solution)/shard_map/ppermute | solution.py:533
  108.8 17.2 %collective-permute-start.1 = (bf16[8,6144]{1,0:T(8,128)(2,1)S(1)}, bf16[8,6144]{1,0:T(8,128)(2,1)S(1)}, u32[]{:S(2)}, u32[]{:S(2)}) collective-permute-start(bf16[8,6144]{1,0:T(8,128)(2,1)S(1)} %get-tuple-element.38), channel_id=1, source_target_pairs={{1,0},{2,1},{3,2},{4,3},{5,4},{6,5},{7,6},{8,7},{9,8},{10,9},{11,1... | collective-permute-start | bytes 294920 | tf_op jit(solution)/shard_map/ppermute | solution.py:528
  112.5 5.0 %collective-permute-start.4 = (f32[8,768]{1,0:T(8,128)S(1)}, f32[8,768]{1,0:T(8,128)S(1)}, u32[]{:S(2)}, u32[]{:S(2)}) collective-permute-start(f32[8,768]{1,0:T(8,128)S(1)} %add.25), channel_id=1, source_target_pairs={{0,6},{1,7},{2,4},{3,5},{4,2},{5,3},{6,0},{7,1},{8,14},{9,15},{10,... | collective-permute-start | bytes 73736 | tf_op jit(solution)/shard_map/ppermute | solution.py:533
  117.5 3.8 %collective-permute-start.5 = (f32[8,768]{1,0:T(8,128)S(1)}, f32[8,768]{1,0:T(8,128)S(1)}, u32[]{:S(2)}, u32[]{:S(2)}) collective-permute-start(f32[8,768]{1,0:T(8,128)S(1)} %add.26), channel_id=1, source_target_pairs={{0,8},{1,9},{2,10},{3,11},{4,12},{5,13},{6,14},{7,15},{8,0},{9,1},... | collective-permute-start | bytes 73736 | tf_op jit(solution)/shard_map/ppermute | solution.py:533
  121.4 4.7 %collective-permute-start.6 = (f32[8,768]{1,0:T(8,128)S(1)}, f32[8,768]{1,0:T(8,128)S(1)}, u32[]{:S(2)}, u32[]{:S(2)}) collective-permute-start(f32[8,768]{1,0:T(8,128)S(1)} %add.27), channel_id=1, source_target_pairs={{0,24},{1,25},{2,26},{3,27},{4,28},{5,29},{6,30},{7,31},{8,16},{9,... | collective-permute-start | bytes 73736 | tf_op jit(solution)/shard_map/ppermute | solution.py:533
  121.6 15.2 %collective-permute-start.10 = (bf16[8,8192]{1,0:T(8,128)(2,1)S(1)}, bf16[8,8192]{1,0:T(8,128)(2,1)S(1)}, u32[]{:S(2)}, u32[]{:S(2)}) collective-permute-start(bf16[8,8192]{1,0:T(8,128)(2,1)S(1)} %get-tuple-element.46.own_ref), channel_id=1, source_target_pairs={{0,192},{64,128},{128,64},{192,0},{1,193},{65,129},{129,65},{193,1... | collective-permute-start | bytes 393224 | tf_op jit(solution)/shard_map/ppermute | solution.py:533
  122.7 14.1 %collective-permute-start.8 = (bf16[8,8192]{1,0:T(8,128)(2,1)S(1)}, bf16[8,8192]{1,0:T(8,128)(2,1)S(1)}, u32[]{:S(2)}, u32[]{:S(2)}) collective-permute-start(bf16[8,8192]{1,0:T(8,128)(2,1)S(1)} %get-tuple-element.46.own_ref), channel_id=1, source_target_pairs={{0,64},{64,0},{128,192},{192,128},{1,65},{65,1},{129,193},{193,129... | collective-permute-start | bytes 393224 | tf_op jit(solution)/shard_map/ppermute | solution.py:533
  122.9 13.9 %collective-permute-start.9 = (bf16[8,8192]{1,0:T(8,128)(2,1)S(1)}, bf16[8,8192]{1,0:T(8,128)(2,1)S(1)}, u32[]{:S(2)}, u32[]{:S(2)}) collective-permute-start(bf16[8,8192]{1,0:T(8,128)(2,1)S(1)} %get-tuple-element.46.own_ref), channel_id=1, source_target_pairs={{0,128},{64,192},{128,0},{192,64},{1,129},{65,193},{129,1},{193,65... | collective-permute-start | bytes 393224 | tf_op jit(solution)/shard_map/ppermute | solution.py:533
  126.0 5.8 %collective-permute-start.7 = (f32[8,768]{1,0:T(8,128)S(1)}, f32[8,768]{1,0:T(8,128)S(1)}, u32[]{:S(2)}, u32[]{:S(2)}) collective-permute-start(f32[8,768]{1,0:T(8,128)S(1)} %add.28), channel_id=1, source_target_pairs={{0,224},{1,225},{2,226},{3,227},{4,228},{5,229},{6,230},{7,231},{8... | collective-permute-start | bytes 73736 | tf_op jit(solution)/shard_map/ppermute | solution.py:533
  131.9 4.9 %collective-permute-start.11 = (f32[8,768]{1,0:T(8,128)S(1)}, f32[8,768]{1,0:T(8,128)S(1)}, u32[]{:S(2)}, u32[]{:S(2)}) collective-permute-start(f32[8,768]{1,0:T(8,128)S(1)} %add.29), channel_id=1, source_target_pairs={{0,64},{64,0},{128,192},{192,128},{1,65},{65,1},{129,193},{193,129... | collective-permute-start | bytes 73736 | tf_op jit(solution)/shard_map/ppermute | solution.py:533
  136.8 4.8 %collective-permute-start.12 = (f32[8,768]{1,0:T(8,128)S(1)}, f32[8,768]{1,0:T(8,128)S(1)}, u32[]{:S(2)}, u32[]{:S(2)}) collective-permute-start(f32[8,768]{1,0:T(8,128)S(1)} %add.30), channel_id=1, source_target_pairs={{0,128},{64,192},{128,0},{192,64},{1,129},{65,193},{129,1},{193,65... | collective-permute-start | bytes 73736 | tf_op jit(solution)/shard_map/ppermute | solution.py:533
